TPU v7x, 128 devices: a whole 4x4x4 slice. The times are simulated.
128 devices in a mesh: row: 8 (over x_lo, z), col: 16 (over x_hi, y, core).
Axes of the slice: x: 4 (x_hi: 2, x_lo: 2; x = x_hi * 2 + x_lo), y: 4, z: 4, core: 2. Of those that a mesh axis runs over, the one named last changes fastest.
Arguments:
- front: float32 [16384, 16384], P('row', 'col'), may hold values from -6 to 6
- inverses: float32 [2, 512, 512], replicated, may hold values from -2 to 2, as said below
- block_owner: int32 [128, 128], P('row', 'col'), may hold values from -1 to 127, as said below
- block_slot: int32 [128, 128], P('row', 'col'), may hold values from 0 to 47
- parent_in: float32 [6144, 128, 128], P(('row', 'col')), may hold values from -6 to 6
Outputs:
- updated: float32 [16384, 16384], P('row', 'col')
- panels: float32 [16384, 1024], P(('row', 'col'))
- parent_out: float32 [6144, 128, 128], P(('row', 'col'))
Inputs may be any that keep to these rules, and one draw needn't show every extreme that they name: Entries of the pivot block inverses. `block_owner`: -1 exactly for blocks above the diagonal (I < J); on one device's 16 x 8 blocks no device is named more than 1 times, and on some device some device is named exactly 1 times.
All inputs are finite; a program needn't handle non-finite values.
Results may differ from a plain program's by a relative error of at most 0.00014.
Values sent between devices are 32-bit elements; how exact they have to be, the bound alone decides.
No kernel may reach another device: no remote copies, remote signals or barrier semaphores. Data moves between devices by JAX's collectives and lax.ppermute only.
A program may use at most 128 MiB of HBM per device.

v0:
```python
import jax
import jax.numpy as jnp
from jax import lax
from jax.sharding import PartitionSpec as P


def spread_2(block, axis, source):
    block = jnp.where(lax.axis_index(axis) == source, block, jnp.zeros_like(block))
    return lax.psum(block, axis)


def matmul(left_side, right_side):
    return jnp.dot(
        left_side, right_side, preferred_element_type=jnp.float32, precision=lax.Precision.HIGHEST
    )


def spread(columns, rows):
    columns = spread_2(columns, "col", 0)
    rows = spread_2(rows, "row", 0)
    return (columns, rows)


def local(front, inverses, block_owner, block_slot, parent_in):
    panel_width = inverses.shape[1]
    columns_one, rows_one = spread(front[:, 0:panel_width], front[0:panel_width, :])
    factor_one = matmul(columns_one, inverses[0])
    partial_value = front - matmul(factor_one, rows_one)
    columns_two, rows_two = spread(
        partial_value[:, panel_width : 2 * panel_width],
        partial_value[panel_width : 2 * panel_width, :],
    )
    factor_two = matmul(columns_two, inverses[1])
    factors = jnp.concatenate([factor_one, factor_two], axis=1)
    updated = partial_value - matmul(factor_two, rows_two)
    piece_rows = factors.shape[0] // lax.axis_size("col")
    panels = lax.dynamic_slice_in_dim(factors, lax.axis_index("col") * piece_rows, piece_rows, 0)
    block_rows, block_cols = block_owner.shape
    block_edge = parent_in.shape[1]
    held = parent_in.shape[0]
    block_count = block_rows * block_cols
    row_devices = lax.axis_size("row")
    col_devices = lax.axis_size("col")
    devices = row_devices * col_devices
    capacity = max(1, (block_count + devices - 1) // devices)
    blocks = updated.reshape(block_rows, block_edge, block_cols, block_edge).transpose(0, 2, 1, 3)
    blocks = blocks.reshape(block_count, block_edge, block_edge)
    owners = block_owner.reshape(block_count)
    parent_slots = block_slot.reshape(block_count)
    position = jnp.arange(block_count, dtype=jnp.int32)
    earlier = (owners[:, None] == owners[None, :]) & (position[None, :] < position[:, None])
    within = jnp.sum(earlier.astype(jnp.int32), axis=1)
    target = jnp.where(owners >= 0, owners * capacity + within, devices * capacity)
    outgoing = (
        jnp.zeros((devices * capacity, block_edge, block_edge), jnp.float32)
        .at[target]
        .set(blocks, mode="drop")
    )
    labels = (
        jnp.full((devices * capacity,), held, jnp.float32)
        .at[target]
        .set(parent_slots.astype(jnp.float32), mode="drop")
    )
    arrived, markers = (
        lax.all_to_all(
            outgoing.reshape(devices, capacity, block_edge, block_edge),
            ("row", "col"),
            split_axis=0,
            concat_axis=0,
            tiled=True,
        ),
        lax.all_to_all(
            labels.reshape(devices, capacity),
            ("row", "col"),
            split_axis=0,
            concat_axis=0,
            tiled=True,
        ),
    )
    arrived = arrived.reshape(devices * capacity, block_edge, block_edge)
    markers = markers.reshape(devices * capacity).astype(jnp.int32)
    added = jnp.zeros(parent_in.shape, jnp.float32).at[markers].add(arrived, mode="drop")
    parent_out = parent_in + added
    return (updated, panels, parent_out)


def solution(mesh):
    in_specs = (
        P("row", "col"),
        P(),
        P("row", "col"),
        P("row", "col"),
        P(("row", "col"), None, None),
    )
    out_specs = (P("row", "col"), P(("row", "col"), None), P(("row", "col"), None, None))
    return jax.shard_map(local, mesh=mesh, in_specs=in_specs, out_specs=out_specs, check_vma=False)
```

profile of v0, /device:TPU:1, one launch (start us, length us, event | category | flops | bytes accessed | tf_op | source)
XLA Modules:
  0.0 712.4 jit_solution(14219420852811880214)
XLA Ops:
  7.2 0.0 all-reduce.5.cloned.1.call-start
  7.2 4.7 slice_select_fusion.1
  11.9 0.0 all-reduce.5.cloned.1.call-update
  11.9 0.0 copy-start.4
  12.0 0.0 all-reduce.7.cloned.1.call-start
  12.0 3.3 slice_select_fusion.3
  15.3 0.0 all-reduce.7.cloned.1.call-update
  15.4 0.0 all-reduce.9.cloned.1.call-start
  15.4 149.8 %all-reduce.5.cloned.1.call-done = f32[2048,512]{1,0:T(8,128)} async-done(((f32[2048,512]{1,0:T(8,128)}), f32[2048,512]{1,0:T(8,128)}) %all-reduce.5.cloned.1.call-update) | async-done | bytes 4194320 | tf_op jit(solution)/shard_map/psum | solution.py:9
  165.2 0.0 copy-done.4
  165.2 10.0 %fusion.2 = f32[2048,512]{0,1:T(8,128)} fusion(f32[2048,512]{1,0:T(8,128)} %all-reduce.5.cloned.1.call-done, f32[2,512,512]{2,1,0:T(8,128)S(1)} %copy-done.4), kind=kOutput, calls=%fused_computation.14 | convolution fusion | flops 6442450944 | bytes 9437184 | tf_op jit(solution)/shard_map/dot_general | solution.py:13
  175.2 73.1 %all-reduce.7.cloned.1.call-done = f32[512,1024]{1,0:T(8,128)} async-done(((f32[512,1024]{1,0:T(8,128)}), f32[512,1024]{1,0:T(8,128)}) %all-reduce.7.cloned.1.call-update) | async-done | bytes 2097168 | tf_op jit(solution)/shard_map/psum | solution.py:9
  248.3 16.6 %convolution_subtract_fusion.1 = f32[2048,1024]{1,0:T(8,128)S(1)} fusion(f32[2048,1024]{1,0:T(8,128)} %param.5, f32[2048,512]{0,1:T(8,128)} %fusion.2, f32[512,1024]{1,0:T(8,128)} %all-reduce.7.cloned.1.call-done), kind=kOutput, calls=%fused_computation.9 | convolution fusion | flops 12886999040 | bytes 23068672 | tf_op jit(solution)/shard_map/dot_general | solution.py:13
  264.9 0.0 copy-start
  264.9 3.4 copy-done
  268.3 2.7 slice_select_fusion
  271.0 0.0 all-reduce.9.cloned.1.call-update
  271.0 0.0 copy-start.5
  271.0 0.0 copy-start.6
  271.0 0.0 all-reduce.11.cloned.1.call-start
  271.1 3.2 slice_select_fusion.2
  274.3 0.0 all-reduce.11.cloned.1.call-update
  274.3 0.0 copy-done.5
  274.3 0.1 copy.30
  274.4 0.1 eq.25
  274.5 0.1 reshape.84
  274.6 0.0 copy-done.6
  274.6 0.1 copy.32
  274.7 0.1 reshape.93
  274.7 0.2 convert_reduce_fusion.1
  274.9 1.0 scatter_custom_fusion
  275.9 0.7 copy.33
  276.7 12.2 %all-to-all-start = ((f32[128,1,1]{2,1,0:T(1,128)}), f32[128,1,1]{2,1,0:T(1,128)S(1)}, u32[]{:S(2)}, u32[]{:S(2)}) async-start(f32[128,1,1]{2,1,0:T(1,128)} %copy.33), calls=%async_computation | async-start | bytes 131072 | tf_op jit(solution)/shard_map/all_to_all | solution.py:72
  288.9 136.6 %all-reduce.9.cloned.1.call-done = f32[2048,512]{1,0:T(8,128)} async-done(((f32[2048,512]{1,0:T(8,128)}), f32[2048,512]{1,0:T(8,128)}) %all-reduce.9.cloned.1.call-update) | async-done | bytes 4194320 | tf_op jit(solution)/shard_map/psum | solution.py:9
  425.4 10.0 %fusion = f32[2048,512]{0,1:T(8,128)} fusion(f32[2048,512]{1,0:T(8,128)} %all-reduce.9.cloned.1.call-done, f32[2,512,512]{2,1,0:T(8,128)S(1)} %copy-done.4), kind=kOutput, calls=%fused_computation.12 | convolution fusion | flops 6442450944 | bytes 9437184 | tf_op jit(solution)/shard_map/dot_general | solution.py:13
  435.4 73.0 %all-reduce.11.cloned.1.call-done = f32[512,1024]{1,0:T(8,128)} async-done(((f32[512,1024]{1,0:T(8,128)}), f32[512,1024]{1,0:T(8,128)}) %all-reduce.11.cloned.1.call-update) | async-done | bytes 2097168 | tf_op jit(solution)/shard_map/psum | solution.py:9
  508.4 16.8 %convolution_subtract_fusion = f32[2048,1024]{1,0:T(8,128)S(1)} fusion(f32[2048,1024]{1,0:T(8,128)} %copy-done, f32[2048,512]{0,1:T(8,128)} %fusion, f32[512,1024]{1,0:T(8,128)} %all-reduce.11.cloned.1.call-done), kind=kOutput, calls=%fused_computation.8 | convolution fusion | flops 12886999040 | bytes 23068672 | tf_op jit(solution)/shard_map/dot_general | solution.py:13
  525.1 0.0 copy-start.3
  525.1 2.2 copy.36
  527.3 1.5 copy-done.3
  528.9 0.8 bitcast_bitcast_fusion
  529.6 4.7 copy.34
  534.3 4.3 broadcast_in_dim.18
  538.6 22.2 %scatter_fusion = f32[128,128,128]{2,1,0:T(8,128)} fusion(f32[128,128,128]{2,1,0:T(8,128)} %broadcast_in_dim.18, s32[128]{0:T(128)S(1)} %fusion.9, f32[128,128,128]{2,1,0:T(8,128)} %bitcast.39), kind=kCustom, calls=%fused_computation.1 | custom fusion | bytes 25166336 | tf_op jit(solution)/shard_map/scatter | solution.py:57
  560.8 0.0 all-to-all-done
  560.8 14.0 %all-to-all-start.1 = ((f32[128,1,128,128]{3,2,1,0:T(8,128)}), f32[128,1,128,128]{3,2,1,0:T(8,128)}, u32[]{:S(2)}, u32[]{:S(2)}) async-start(f32[128,1,128,128]{3,2,1,0:T(8,128)} %bitcast.37), calls=%async_computation.1 | async-start | bytes 16777216 | tf_op jit(solution)/shard_map/all_to_all | solution.py:65
  574.8 2.4 convert_reduce_fusion
  577.1 0.0 copy-start.2
  577.2 2.0 fusion.6
  579.2 2.0 copy.35
  581.2 106.0 %all-to-all-done.1 = f32[128,1,128,128]{3,2,1,0:T(8,128)} async-done(((f32[128,1,128,128]{3,2,1,0:T(8,128)}), f32[128,1,128,128]{3,2,1,0:T(8,128)}, u32[]{:S(2)}, u32[]{:S(2)}) %all-to-all-start.1) | async-done | bytes 8388640 | tf_op jit(solution)/shard_map/all_to_all | solution.py:65
  687.2 0.0 copy-done.2
  687.2 17.0 %scatter_fusion.1 = f32[48,128,128]{2,1,0:T(8,128)S(1)} fusion(f32[48,128,128]{2,1,0:T(8,128)S(1)} %copy-done.2, s32[128]{0:T(128)S(1)} %fusion.8, f32[128,128,128]{2,1,0:T(8,128)} %bitcast.9), kind=kCustom, calls=%fused_computation.2 | custom fusion | flops 2097152 | bytes 25166336 | tf_op jit(solution)/shard_map/scatter-add | solution.py:82
  704.2 0.0 copy-start.1
  704.3 1.7 copy-done.1
  (3 shorter events, 0.0 us)
Async XLA Ops:
  7.2 158.0 %all-reduce.5.cloned.1.call-start = ((), (), s32[]{:S(2)}) async-start(), calls=%async_computation.2 | async-start | bytes 8388608 | tf_op jit(solution)/shard_map/psum | solution.py:9
  11.9 153.3 %copy-start.4 = (f32[2,512,512]{2,1,0:T(8,128)S(1)}, f32[2,512,512]{2,1,0:T(8,128)}, u32[]{:S(2)}) copy-start(f32[2,512,512]{2,1,0:T(8,128)} %param.6) | copy-start | bytes 6291460
  12.0 236.4 %all-reduce.7.cloned.1.call-start = ((), (), s32[]{:S(2)}) async-start(), calls=%async_computation.3 | async-start | bytes 4194304 | tf_op jit(solution)/shard_map/psum | solution.py:9
  15.4 410.1 %all-reduce.9.cloned.1.call-start = ((), (), s32[]{:S(2)}) async-start(), calls=%async_computation.4 | async-start | bytes 8388608 | tf_op jit(solution)/shard_map/psum | solution.py:9
  264.9 3.4 copy-start
  271.0 3.3 copy-start.5
  271.0 3.5 copy-start.6
  271.0 237.3 %all-reduce.11.cloned.1.call-start = ((), (), s32[]{:S(2)}) async-start(), calls=%async_computation.5 | async-start | bytes 4194304 | tf_op jit(solution)/shard_map/psum | solution.py:9
  276.7 284.1 %all-to-all-start = ((f32[128,1,1]{2,1,0:T(1,128)}), f32[128,1,1]{2,1,0:T(1,128)S(1)}, u32[]{:S(2)}, u32[]{:S(2)}) async-start(f32[128,1,1]{2,1,0:T(1,128)} %copy.33), calls=%async_computation | async-start | bytes 131072 | tf_op jit(solution)/shard_map/all_to_all | solution.py:72
  525.1 3.7 copy-start.3
  560.8 126.4 %all-to-all-start.1 = ((f32[128,1,128,128]{3,2,1,0:T(8,128)}), f32[128,1,128,128]{3,2,1,0:T(8,128)}, u32[]{:S(2)}, u32[]{:S(2)}) async-start(f32[128,1,128,128]{3,2,1,0:T(8,128)} %bitcast.37), calls=%async_computation.1 | async-start | bytes 16777216 | tf_op jit(solution)/shard_map/all_to_all | solution.py:65
  577.1 110.1 %copy-start.2 = (f32[48,128,128]{2,1,0:T(8,128)S(1)}, f32[48,128,128]{2,1,0:T(8,128)}, u32[]{:S(2)}) copy-start(f32[48,128,128]{2,1,0:T(8,128)} %param.9) | copy-start | bytes 9437188
  704.2 1.7 copy-start.1
Sparse Core Ops, SparseCore 0:
  12.1 153.1 all-reduce.4
  168.3 79.9 all-reduce.6
  271.1 154.2 all-reduce.8
  428.4 79.9 all-reduce.10
where the time goes:
time: 713 us; the launch traced here: 712 us
  waiting for transfers between devices  538 us (75%)
  matrix products  53.3 us (7%)
  local copies, waits for them, and re-layouts  44.8 us (6%)
  other arithmetic  35.5 us (5%)
  starting transfers between devices  26.4 us (4%)
  between operations  14 us (2%)
    psum x4, waiting for transfers between devices, spread_2(): return lax.psum(block, axis)  432 us
    all_to_all x1, waiting for transfers between devices, local(): lax.all_to_all(outgoing.reshape(devices, capacity, block_edge, block_edge...  106 us
    dot_general x4, matrix products, matmul(): jnp.dot(left_side, right_side, preferred_element_type=jnp.float32, precis...  53.3 us
    scatter x1, local copies, waits for them, and re-layouts, local(): outgoing = jnp.zeros((devices * capacity, block_edge, block_edge), jnp.fl...  22.2 us
    scatter-add x1, other arithmetic, local(): jnp.zeros(parent_in.shape, jnp.float32).at[markers]  17 us
  transfers between devices with their start and end apart: 6, of which 5 were waited for; matrix products, arithmetic and copies ran while one was open for 12% of the time, Pallas kernels for 0%

commit v1 on v0

v1 whole, which is shorter than its diff:
```python
import functools

import jax
import jax.numpy as jnp
from jax import lax
from jax.experimental import pallas as pl
from jax.experimental.pallas import tpu as pltpu
from jax.sharding import PartitionSpec as P

AXES = ("row", "col")
MIB = 1024 * 1024


def device(xl, z, xh, y, core):
    return (xl * 4 + z) * 16 + xh * 8 + y * 2 + core


def pairs(move, keep=lambda *place: True):
    listed = []
    for xl in range(2):
        for z in range(4):
            for xh in range(2):
                for y in range(4):
                    for core in range(2):
                        place = (xl, z, xh, y, core)
                        if keep(*place):
                            listed.append((device(*place), device(*move(*place))))
    return listed


def send(value, move, keep=lambda *place: True):
    return lax.ppermute(value, AXES, pairs(move, keep))


def place():
    row = lax.axis_index("row")
    col = lax.axis_index("col")
    return row // 4, row % 4, col // 8, (col // 2) % 4, col % 2


def choose(index, options):
    value = options[-1]
    for number in range(len(options) - 2, -1, -1):
        value = jnp.where(index == number, options[number], value)
    return value


def assemble(index, own, before, after, across):
    size = own.shape[0]
    whole = jnp.zeros((4 * size,) + own.shape[1:], own.dtype)
    for shift, piece in ((0, own), (3, before), (1, after), (2, across)):
        whole = lax.dynamic_update_slice(whole, piece, (((index + shift) % 4) * size, 0))
    return whole


def spread_columns(columns):
    _, _, xh, y, core = place()
    size = columns.shape[0] // 4
    parts = [columns[k * size : (k + 1) * size] for k in range(4)]
    arrived = [
        send(
            parts[k],
            lambda xl, z, xh, y, core, k=k: (xl, z, xh, k, core),
            lambda xl, z, xh, y, core: xh == 0 and y == 0 and core == 0,
        )
        for k in (1, 2, 3)
    ]
    piece = choose(y, [parts[0]] + arrived)
    across = send(
        piece,
        lambda xl, z, xh, y, core: (xl, z, 1, y, core),
        lambda xl, z, xh, y, core: xh == 0 and core == 0,
    )
    piece = jnp.where(xh == 0, piece, across)
    around = [
        send(
            piece,
            lambda xl, z, xh, y, core, step=step: (xl, z, xh, (y + step) % 4, core),
            lambda xl, z, xh, y, core: core == 0,
        )
        for step in (1, 3, 2)
    ]
    whole = assemble(y, piece, around[0], around[1], around[2])
    other = send(
        whole, lambda xl, z, xh, y, core: (xl, z, xh, y, 1), lambda xl, z, xh, y, core: core == 0
    )
    return jnp.where(core == 0, whole, other)


def spread_rows(rows):
    xl, z, _, _, _ = place()
    size = rows.shape[0] // 4
    parts = [rows[k * size : (k + 1) * size] for k in range(4)]
    arrived = [
        send(
            parts[k],
            lambda xl, z, xh, y, core, k=k: (xl, k, xh, y, core),
            lambda xl, z, xh, y, core: xl == 0 and z == 0,
        )
        for k in (1, 2, 3)
    ]
    piece = choose(z, [parts[0]] + arrived)
    across = send(
        piece,
        lambda xl, z, xh, y, core: (1, z, xh, y, core),
        lambda xl, z, xh, y, core: xl == 0,
    )
    piece = jnp.where(xl == 0, piece, across)
    around = [
        send(piece, lambda xl, z, xh, y, core, step=step: (xl, (z + step) % 4, xh, y, core))
        for step in (1, 3, 2)
    ]
    return assemble(z, piece, around[0], around[1], around[2])


def product(left, right):
    return jnp.dot(left, right, preferred_element_type=jnp.float32, precision=lax.Precision.HIGH)


def halves(value):
    high = value.astype(jnp.bfloat16)
    low = (value - high.astype(jnp.float32)).astype(jnp.bfloat16)
    return high, low


def update_kernel(
    owner_ref, front_ref, left_one, left_two, right_one, right_two,
    updated_ref, outgoing_ref, high_one, low_one, high_two, low_two, result, whole_sem, block_sem,
):
    step = pl.program_id(0)
    steps = pl.num_programs(0)
    slot = lax.rem(step, 2)
    tile = result.shape[1]
    edge = outgoing_ref.shape[1]
    down, across = tile // edge, result.shape[2] // edge

    def whole_copy(at, number):
        return pltpu.make_async_copy(
            result.at[at], updated_ref.at[pl.ds(number * tile, tile)], whole_sem.at[at]
        )

    def block_copies(at, number, act):
        for i in range(down):
            for j in range(across):
                owner = owner_ref[number * down + i, j]

                @pl.when(owner >= 0)
                def _():
                    act(
                        pltpu.make_async_copy(
                            result.at[at, pl.ds(i * edge, edge), pl.ds(j * edge, edge)],
                            outgoing_ref.at[jnp.maximum(owner, 0)],
                            block_sem.at[at],
                        )
                    )

    def finish(at, number):
        whole_copy(at, number).wait()
        block_copies(at, number, lambda copy: copy.wait())

    @pl.when(step == 0)
    def _():
        high_one[...], low_one[...] = halves(right_one[...])
        high_two[...], low_two[...] = halves(right_two[...])

    @pl.when(step >= 2)
    def _():
        finish(slot, step - 2)

    total = front_ref[...]
    for left, high, low in ((left_one, high_one, low_one), (left_two, high_two, low_two)):
        left_high, left_low = halves(left[...])
        total -= (
            jnp.dot(left_high, low[...], preferred_element_type=jnp.float32)
            + jnp.dot(left_low, high[...], preferred_element_type=jnp.float32)
        ) + jnp.dot(left_high, high[...], preferred_element_type=jnp.float32)
    result[slot] = total
    whole_copy(slot, step).start()
    block_copies(slot, step, lambda copy: copy.start())

    @pl.when(step == steps - 1)
    def _():
        finish(1 - slot, step - 1)
        finish(slot, step)


def update(front, block_owner, left_one, left_two, right_one, right_two, devices, edge):
    rows, columns = front.shape
    depth = left_one.shape[1]
    tile = 2 * edge
    return pl.pallas_call(
        update_kernel,
        grid=(rows // tile,),
        in_specs=[
            pl.BlockSpec(memory_space=pltpu.SMEM),
            pl.BlockSpec((tile, columns), lambda i: (i, 0)),
            pl.BlockSpec((tile, depth), lambda i: (i, 0)),
            pl.BlockSpec((tile, depth), lambda i: (i, 0)),
            pl.BlockSpec((depth, columns), lambda i: (0, 0)),
            pl.BlockSpec((depth, columns), lambda i: (0, 0)),
        ],
        out_specs=[pl.BlockSpec(memory_space=pl.ANY), pl.BlockSpec(memory_space=pl.ANY)],
        out_shape=[
            jax.ShapeDtypeStruct((rows, columns), jnp.float32),
            jax.ShapeDtypeStruct((devices, edge, edge), jnp.float32),
        ],
        scratch_shapes=[pltpu.VMEM((depth, columns), jnp.bfloat16)] * 4
        + [
            pltpu.VMEM((2, tile, columns), jnp.float32),
            pltpu.SemaphoreType.DMA((2,)),
            pltpu.SemaphoreType.DMA((2,)),
        ],
        compiler_params=pltpu.CompilerParams(vmem_limit_bytes=40 * MIB),
        cost_estimate=pl.CostEstimate(
            flops=12 * rows * columns * depth, bytes_accessed=32 * MIB, transcendentals=0
        ),
        name="update",
    )(block_owner, front, left_one, left_two, right_one, right_two)


def add_kernel(slot_ref, parent_ref, arrived_ref, out_ref):
    step = pl.program_id(0)
    count = arrived_ref.shape[0]

    @pl.when(step == 0)
    def _():
        out_ref[...] = parent_ref[...]

    for k in range(count):
        slot = slot_ref[step * count + k]

        @pl.when(slot >= 0)
        def _():
            at = jnp.maximum(slot, 0)
            out_ref[at] = out_ref[at] + arrived_ref[k]


def extend_add(slots, parent, arrived):
    count = 8
    held, edge, _ = parent.shape
    return pl.pallas_call(
        add_kernel,
        grid=(arrived.shape[0] // count,),
        in_specs=[
            pl.BlockSpec(memory_space=pltpu.SMEM),
            pl.BlockSpec((held, edge, edge), lambda i: (0, 0, 0)),
            pl.BlockSpec((count, edge, edge), lambda i: (i, 0, 0)),
        ],
        out_specs=pl.BlockSpec((held, edge, edge), lambda i: (0, 0, 0)),
        out_shape=jax.ShapeDtypeStruct(parent.shape, jnp.float32),
        compiler_params=pltpu.CompilerParams(vmem_limit_bytes=32 * MIB),
        cost_estimate=pl.CostEstimate(flops=2 * MIB, bytes_accessed=14 * MIB, transcendentals=0),
        name="extend_add",
    )(slots, parent, arrived)


def local(front, inverses, block_owner, block_slot, parent_in):
    width = inverses.shape[1]
    edge = parent_in.shape[1]
    devices = lax.axis_size("row") * lax.axis_size("col")

    owners = block_owner.reshape(-1)
    slots = block_slot.reshape(-1)
    named = owners[None, :] == jnp.arange(devices, dtype=jnp.int32)[:, None]
    labels = jnp.sum(jnp.where(named, slots[None, :] + 1, 0), axis=1) - 1
    markers = lax.all_to_all(labels.reshape(devices, 1, 1), AXES, 0, 0, tiled=True).reshape(devices)

    columns_one = front[:, :width]
    rows_one = product(inverses[0], front[:width])
    left_one = spread_columns(columns_one)
    right_one = spread_rows(rows_one)

    columns_two = front[:, width : 2 * width] - product(columns_one, right_one[:, width : 2 * width])
    rows_two = front[width : 2 * width] - product(left_one[width : 2 * width], right_one)
    rows_two = product(inverses[1], rows_two)
    left_two = spread_columns(columns_two)
    right_two = spread_rows(rows_two)

    updated, outgoing = update(
        front, block_owner, left_one, left_two, right_one, right_two, devices, edge
    )
    arrived = lax.all_to_all(outgoing, AXES, 0, 0, tiled=True)

    piece = front.shape[0] // lax.axis_size("col")
    start = lax.axis_index("col") * piece
    panels = jnp.concatenate(
        [
            product(lax.dynamic_slice_in_dim(left_one, start, piece, 0), inverses[0]),
            product(lax.dynamic_slice_in_dim(left_two, start, piece, 0), inverses[1]),
        ],
        axis=1,
    )
    parent_out = extend_add(markers, parent_in, arrived)
    return (updated, panels, parent_out)


def solution(mesh):
    in_specs = (
        P("row", "col"),
        P(),
        P("row", "col"),
        P("row", "col"),
        P(("row", "col"), None, None),
    )
    out_specs = (P("row", "col"), P(("row", "col"), None), P(("row", "col"), None, None))
    return jax.shard_map(local, mesh=mesh, in_specs=in_specs, out_specs=out_specs, check_vma=False)
```

time: 713 us -> 418 us (0.59)
  waiting for transfers between devices: 538 us -> 178 us
  starting transfers between devices: 26.4 us -> 133 us
  matrix products: 53.3 us -> 20.8 us
  Pallas kernels: 0 us -> 30.3 us
  other arithmetic: 35.5 us -> 21 us
  between operations: 14 us -> 1.16 us
  local copies, waits for them, and re-layouts: 44.8 us -> 32.2 us
    psum x4 -> x0, waiting for transfers between devices: 432 us -> none  [spread_2(): return lax.psum(block, axis)]
    ppermute x0 -> x30, waiting for transfers between devices: none -> 72.2 us  [send(): return lax.ppermute(value, AXES, pairs(move, keep))]
    all_to_all x2, starting transfers between devices: 26.2 us -> 81 us  [the longest x1 72.5 us: local(): lax.all_to_all(labels.reshape(devices, 1, 1), AXES, 0, 0, tiled=True)]
    ppermute x0 -> x30, starting transfers between devices: none -> 51.7 us  [send(): return lax.ppermute(value, AXES, pairs(move, keep))]
    dot_general x4 -> x6, matrix products: 53.3 us -> 20.8 us  [product(): jnp.dot(left, right, preferred_element_type=jnp.float32, precision=lax.Pr...]
    pallas_call x0 -> x2, Pallas kernels: none -> 30.3 us  [the longest x1 18.7 us: update(): pl.pallas_call(update_kernel, grid=(rows // tile,), in_specs=[pl.BlockSpe...]
    scatter x2 -> x0, local copies, waits for them, and re-layouts: 23.1 us -> none  [the longest x1 22.2 us: local(): outgoing = jnp.zeros((devices * capacity, block_edge, block_edge), jnp.fl...]
    scatter-add x1 -> x0, other arithmetic: 17 us -> none  [local(): jnp.zeros(parent_in.shape, jnp.float32).at[markers]]
  transfers between devices with their start and end apart: 6 -> 32, of which waited for: 5 -> 10; matrix products, arithmetic and copies ran while one was open for 12% -> 15% of each run, Pallas kernels for 0% -> 5%
where the time goes in v1:
time: 418 us; the launch traced here: 416 us
  waiting for transfers between devices  178 us (43%)
  starting transfers between devices  133 us (32%)
  local copies, waits for them, and re-layouts  32.2 us (8%)
  Pallas kernels  30.3 us (7%)
  other arithmetic  21 us (5%)
  matrix products  20.8 us (5%)
    all_to_all x1, waiting for transfers between devices, local(): arrived = lax.all_to_all(outgoing, AXES, 0, 0, tiled=True)  106 us
    all_to_all x1, starting transfers between devices, local(): lax.all_to_all(labels.reshape(devices, 1, 1), AXES, 0, 0, tiled=True)  72.5 us
    ppermute x30, waiting for transfers between devices, send(): return lax.ppermute(value, AXES, pairs(move, keep))  72.2 us
    ppermute x30, starting transfers between devices, send(): return lax.ppermute(value, AXES, pairs(move, keep))  51.7 us
    dot_general x6, matrix products, product(): jnp.dot(left, right, preferred_element_type=jnp.float32, precision=lax.Pr...  20.8 us
    pallas_call x1, Pallas kernels, update(): pl.pallas_call(update_kernel, grid=(rows // tile,), in_specs=[pl.BlockSpe...  18.7 us
    pallas_call x1, Pallas kernels, extend_add(): pl.pallas_call(add_kernel, grid=(arrived.shape[0] // count,), in_specs=[p...  11.5 us
    dynamic_update_slice x12, local copies, waits for them, and re-layouts, assemble(): lax.dynamic_update_slice(whole, piece, ((index + shift) % 4 * size, 0))  11.1 us
  transfers between devices with their start and end apart: 32, of which 10 were waited for; matrix products, arithmetic and copies ran while one was open for 15% of the time, Pallas kernels for 5%

profile of v1, /device:TPU:1, one launch (start us, length us, event | category | flops | bytes accessed | tf_op | source)
XLA Modules:
  0.0 416.1 jit_solution(3102431788792641085)
XLA Ops:
  0.6 3.3 fusion.29
  3.9 1.6 collective-permute-start
  5.6 1.6 collective-permute-start.1
  7.2 1.6 collective-permute-start.2
  8.8 3.5 fusion.7
  12.3 1.3 copy-done.9
  14.5 4.4 %collective-permute-start.8 = (f32[128,1024]{1,0:T(8,128)}, f32[128,1024]{1,0:T(8,128)S(1)}, u32[]{:S(2)}, u32[]{:S(2)}) collective-permute-start(f32[128,1024]{1,0:T(8,128)} %get-tuple-element.26), channel_id=1, source_target_pairs={{0,16},{1,17},{2,18},{3,19},{4,20},{5,21},{6,22},{7,23},{8,24},{9,... | collective-permute-start | bytes 1572872 | tf_op jit(solution)/shard_map/ppermute | solution.py:32
  18.9 2.7 collective-permute-start.9
  21.6 2.1 collective-permute-start.10
  23.7 2.0 select_select_fusion
  25.7 1.7 collective-permute-start.3
  27.4 8.4 %collective-permute-done.9 = f32[128,1024]{1,0:T(8,128)S(1)} collective-permute-done((f32[128,1024]{1,0:T(8,128)S(1)}, f32[128,1024]{1,0:T(8,128)S(1)}, u32[]{:S(2)}, u32[]{:S(2)}) %collective-permute-start.9) | collective-permute-done | bytes 524320 | tf_op jit(solution)/shard_map/ppermute | solution.py:32
  35.8 1.4 slice_select_fusion.2
  37.2 2.1 collective-permute-start.11
  39.3 11.0 %collective-permute-done.11 = f32[128,1024]{1,0:T(8,128)} collective-permute-done((f32[128,1024]{1,0:T(8,128)S(1)}, f32[128,1024]{1,0:T(8,128)}, u32[]{:S(2)}, u32[]{:S(2)}) %collective-permute-start.11) | collective-permute-done | bytes 524320 | tf_op jit(solution)/shard_map/ppermute | solution.py:32
  50.5 2.0 constant_dynamic-update-slice_fusion.11
  52.5 2.7 collective-permute-start.13
  55.1 2.0 collective-permute-start.14
  57.7 1.2 constant_dynamic-update-slice_fusion.15
  59.6 2.4 collective-permute-done.12
  64.2 5.4 %collective-permute-done.14 = f32[128,1024]{1,0:T(8,128)S(1)} collective-permute-done((f32[128,1024]{1,0:T(8,128)}, f32[128,1024]{1,0:T(8,128)S(1)}, u32[]{:S(2)}, u32[]{:S(2)}) %collective-permute-start.14) | collective-permute-done | bytes 524320 | tf_op jit(solution)/shard_map/ppermute | solution.py:32
  69.7 1.7 collective-permute-start.5
  71.3 1.6 collective-permute-start.6
  73.0 8.5 %bitcast_subtract_fusion = f32[2048,512]{1,0:T(8,128)S(1)} fusion(f32[2048,1024]{1,0:T(8,128)} %front_ref.1, f32[512,1024]{1,0:T(8,128)S(1)} %constant_dynamic-update-slice_fusion.8.right_one), kind=kOutput, calls=%fused_computation | convolution fusion | flops 3222274048 | bytes 13631488 | tf_op jit(solution)/shard_map/dot_general | solution.py:117
  81.4 2.0 copy-done.4
  83.4 1.7 fusion.30
  85.2 1.6 collective-permute-start.15
  86.8 1.6 collective-permute-start.16
  88.4 1.6 collective-permute-start.17
  91.1 2.3 constant_dynamic-update-slice_fusion.13
  93.3 2.3 constant_dynamic-update-slice_fusion.12
  95.6 1.3 collective-permute-start.7
  96.9 2.0 slice_select_fusion
  99.7 2.6 broadcast.39.clone.1
  108.9 1.5 collective-permute-start.22
  110.3 17.5 %collective-permute-done.7 = f32[2048,512]{1,0:T(8,128)} collective-permute-done((f32[2048,512]{1,0:T(8,128)}, f32[2048,512]{1,0:T(8,128)}, u32[]{:S(2)}, u32[]{:S(2)}) %collective-permute-start.7) | collective-permute-done | bytes 4194336 | tf_op jit(solution)/shard_map/ppermute | solution.py:32
  127.8 3.2 broadcast_select_fusion.1.left_one
  131.0 1.9 fusion.12
  132.9 1.2 copy-done.7
  134.1 3.6 fusion.9
  137.7 1.2 fusion.31
  139.0 4.3 %collective-permute-start.23 = (f32[128,1024]{1,0:T(8,128)}, f32[128,1024]{1,0:T(8,128)S(1)}, u32[]{:S(2)}, u32[]{:S(2)}) collective-permute-start(f32[128,1024]{1,0:T(8,128)} %get-tuple-element.23), channel_id=1, source_target_pairs={{0,16},{1,17},{2,18},{3,19},{4,20},{5,21},{6,22},{7,23},{8,24},{9,... | collective-permute-start | bytes 1572872 | tf_op jit(solution)/shard_map/ppermute | solution.py:32
  143.3 2.1 collective-permute-start.24
  145.4 2.1 collective-permute-start.25
  147.6 2.1 collective-permute-done.23
  149.7 5.6 %collective-permute-done.24 = f32[128,1024]{1,0:T(8,128)S(1)} collective-permute-done((f32[128,1024]{1,0:T(8,128)}, f32[128,1024]{1,0:T(8,128)S(1)}, u32[]{:S(2)}, u32[]{:S(2)}) %collective-permute-start.24) | collective-permute-done | bytes 524320 | tf_op jit(solution)/shard_map/ppermute | solution.py:32
  156.1 1.4 slice_select_fusion.1
  157.4 1.3 collective-permute-start.26
  159.9 72.5 %all-to-all-start = ((s32[128,1,1]{2,1,0:T(1,128)}), s32[128,1,1]{2,1,0:T(1,128)S(1)}, u32[]{:S(2)}, u32[]{:S(2)}) async-start(s32[128,1,1]{2,1,0:T(1,128)} %copy.35), calls=%async_computation | async-start | bytes 131072 | tf_op jit(solution)/shard_map/all_to_all | solution.py:266
  232.8 1.6 collective-permute-start.27
  234.4 1.8 collective-permute-start.28
  236.2 1.4 collective-permute-start.29
  237.6 3.2 broadcast_select_fusion.left_two
  240.8 7.5 %collective-permute-done.27 = f32[128,1024]{1,0:T(8,128)S(1)} collective-permute-done((f32[128,1024]{1,0:T(8,128)S(1)}, f32[128,1024]{1,0:T(8,128)S(1)}, u32[]{:S(2)}, u32[]{:S(2)}) %collective-permute-start.27) | collective-permute-done | bytes 524320 | tf_op jit(solution)/shard_map/ppermute | solution.py:32
  248.5 12.4 %collective-permute-done.29 = f32[128,1024]{1,0:T(8,128)S(1)} collective-permute-done((f32[128,1024]{1,0:T(8,128)S(1)}, f32[128,1024]{1,0:T(8,128)S(1)}, u32[]{:S(2)}, u32[]{:S(2)}) %collective-permute-start.29) | collective-permute-done | bytes 524320 | tf_op jit(solution)/shard_map/ppermute | solution.py:32
  261.0 18.7 %update.1 = (f32[2048,1024]{1,0:T(8,128)}, f32[128,128,128]{2,1,0:T(8,128)}) custom-call(s32[16,8]{1,0:T(8,128)S(1)} %copy.32.owner_ref, f32[2048,1024]{1,0:T(8,128)} %front_ref.1, f32[2048,512]{1,0:T(8,128)S(1)} %copy-done.1, f32[2048,512]{1,0:T(8,128)S(1)} %broadcast_select_fusion.left_two, f32[512,1024]{1,0:T(8,128)S(1)} %constant_dynamic-update-slice_fusion.8.right_one, ...), custom_call_target="tpu_custom_call" | custom-call | flops 12884901888 | bytes 33554432 | tf_op jit(solution)/shard_map/update/pallas_call | solution.py:191
  279.7 2.0 copy-done.2
  281.7 8.5 %all-to-all-start.1 = ((f32[128,128,128]{2,1,0:T(8,128)}), f32[128,128,128]{2,1,0:T(8,128)}, u32[]{:S(2)}, u32[]{:S(2)}) async-start(f32[128,128,128]{2,1,0:T(8,128)} %get-tuple-element.6), calls=%async_computation.1 | async-start | bytes 16777216 | tf_op jit(solution)/shard_map/all_to_all | solution.py:282
  290.3 2.4 reduce.slot_ref
  292.6 1.7 fusion.18
  294.4 1.7 fusion.15
  296.9 105.7 %all-to-all-done.1.arrived_ref = f32[128,128,128]{2,1,0:T(8,128)} async-done(((f32[128,128,128]{2,1,0:T(8,128)}), f32[128,128,128]{2,1,0:T(8,128)}, u32[]{:S(2)}, u32[]{:S(2)}) %all-to-all-start.1) | async-done | bytes 8388640 | tf_op jit(solution)/shard_map/all_to_all | solution.py:282
  402.7 1.9 copy-done.3
  404.5 11.5 %extend_add.1 = f32[48,128,128]{2,1,0:T(8,128)} custom-call(s32[128]{0:T(128)S(1)} %reduce.slot_ref, f32[48,128,128]{2,1,0:T(8,128)S(1)} %copy-done.3, f32[128,128,128]{2,1,0:T(8,128)} %all-to-all-done.1.arrived_ref), custom_call_target="tpu_custom_call" | custom-call | flops 2097152 | bytes 14680064 | tf_op jit(solution)/shard_map/extend_add/pallas_call | solution.py:241
  (76 shorter events, 16.3 us)
Async XLA Ops:
  0.6 8.2 %copy-start.6 = (f32[2,512,512]{2,1,0:T(8,128)S(1)}, f32[2,512,512]{2,1,0:T(8,128)}, u32[]{:S(2)}) copy-start(f32[2,512,512]{2,1,0:T(8,128)} %param.6) | copy-start | bytes 6291460
  3.9 17.7 %collective-permute-start = (f32[512,512]{1,0:T(8,128)S(1)}, f32[512,512]{1,0:T(8,128)}, u32[]{:S(2)}, u32[]{:S(2)}) collective-permute-start(f32[512,512]{1,0:T(8,128)S(1)} %get-tuple-element.17), channel_id=1, source_target_pairs={{0,2},{16,18},{32,34},{48,50},{64,66},{80,82},{96,98},{112,114}} | collective-permute-start | bytes 3145736 | tf_op jit(solution)/shard_map/ppermute | solution.py:32
  5.6 18.1 %collective-permute-start.1 = (f32[512,512]{1,0:T(8,128)}, f32[512,512]{1,0:T(8,128)}, u32[]{:S(2)}, u32[]{:S(2)}) collective-permute-start(f32[512,512]{1,0:T(8,128)} %get-tuple-element.16), channel_id=1, source_target_pairs={{0,4},{16,20},{32,36},{48,52},{64,68},{80,84},{96,100},{112,116}} | collective-permute-start | bytes 3145736 | tf_op jit(solution)/shard_map/ppermute | solution.py:32
  7.2 16.5 %collective-permute-start.2 = (f32[512,512]{1,0:T(8,128)S(1)}, f32[512,512]{1,0:T(8,128)}, u32[]{:S(2)}, u32[]{:S(2)}) collective-permute-start(f32[512,512]{1,0:T(8,128)S(1)} %get-tuple-element.15), channel_id=1, source_target_pairs={{0,6},{16,22},{32,38},{48,54},{64,70},{80,86},{96,102},{112,118}} | collective-permute-start | bytes 3145736 | tf_op jit(solution)/shard_map/ppermute | solution.py:32
  12.3 1.3 copy-start.9
  14.5 12.9 %collective-permute-start.8 = (f32[128,1024]{1,0:T(8,128)}, f32[128,1024]{1,0:T(8,128)S(1)}, u32[]{:S(2)}, u32[]{:S(2)}) collective-permute-start(f32[128,1024]{1,0:T(8,128)} %get-tuple-element.26), channel_id=1, source_target_pairs={{0,16},{1,17},{2,18},{3,19},{4,20},{5,21},{6,22},{7,23},{8,24},{9,... | collective-permute-start | bytes 1572872 | tf_op jit(solution)/shard_map/ppermute | solution.py:32
  18.9 16.9 %collective-permute-start.9 = (f32[128,1024]{1,0:T(8,128)S(1)}, f32[128,1024]{1,0:T(8,128)S(1)}, u32[]{:S(2)}, u32[]{:S(2)}) collective-permute-start(f32[128,1024]{1,0:T(8,128)S(1)} %get-tuple-element.25), channel_id=1, source_target_pairs={{0,32},{1,33},{2,34},{3,35},{4,36},{5,37},{6,38},{7,39},{8,40},{9,... | collective-permute-start | bytes 1572872 | tf_op jit(solution)/shard_map/ppermute | solution.py:32
  21.6 14.2 %collective-permute-start.10 = (f32[128,1024]{1,0:T(8,128)S(1)}, f32[128,1024]{1,0:T(8,128)}, u32[]{:S(2)}, u32[]{:S(2)}) collective-permute-start(f32[128,1024]{1,0:T(8,128)S(1)} %get-tuple-element.24), channel_id=1, source_target_pairs={{0,48},{1,49},{2,50},{3,51},{4,52},{5,53},{6,54},{7,55},{8,56},{9,... | collective-permute-start | bytes 1572872 | tf_op jit(solution)/shard_map/ppermute | solution.py:32
  25.7 31.5 %collective-permute-start.3 = (f32[512,512]{1,0:T(8,128)S(1)}, f32[512,512]{1,0:T(8,128)}, u32[]{:S(2)}, u32[]{:S(2)}) collective-permute-start(f32[512,512]{1,0:T(8,128)S(1)} %select_select_fusion), channel_id=1, source_target_pairs={{0,8},{2,10},{4,12},{6,14},{16,24},{18,26},{20,28},{22,30},{32,40}... | collective-permute-start | bytes 3145736 | tf_op jit(solution)/shard_map/ppermute | solution.py:32
  37.2 2.1 copy-start.10
  37.2 13.1 %collective-permute-start.11 = (f32[128,1024]{1,0:T(8,128)S(1)}, f32[128,1024]{1,0:T(8,128)}, u32[]{:S(2)}, u32[]{:S(2)}) collective-permute-start(f32[128,1024]{1,0:T(8,128)S(1)} %slice_select_fusion.2), channel_id=1, source_target_pairs={{0,64},{1,65},{2,66},{3,67},{4,68},{5,69},{6,70},{7,71},{8,72},{9,... | collective-permute-start | bytes 1572872 | tf_op jit(solution)/shard_map/ppermute | solution.py:32
  52.5 9.6 %collective-permute-start.12 = (f32[128,1024]{1,0:T(8,128)}, f32[128,1024]{1,0:T(8,128)}, u32[]{:S(2)}, u32[]{:S(2)}) collective-permute-start(f32[128,1024]{1,0:T(8,128)} %get-tuple-element.12), channel_id=1, source_target_pairs={{0,16},{1,17},{2,18},{3,19},{4,20},{5,21},{6,22},{7,23},{8,24},{9,... | collective-permute-start | bytes 1572872 | tf_op jit(solution)/shard_map/ppermute | solution.py:32
  52.5 10.6 %collective-permute-start.13 = (f32[128,1024]{1,0:T(8,128)}, f32[128,1024]{1,0:T(8,128)}, u32[]{:S(2)}, u32[]{:S(2)}) collective-permute-start(f32[128,1024]{1,0:T(8,128)} %get-tuple-element.12), channel_id=1, source_target_pairs={{0,48},{1,49},{2,50},{3,51},{4,52},{5,53},{6,54},{7,55},{8,56},{9,... | collective-permute-start | bytes 1572872 | tf_op jit(solution)/shard_map/ppermute | solution.py:32
  55.1 14.5 %collective-permute-start.14 = (f32[128,1024]{1,0:T(8,128)}, f32[128,1024]{1,0:T(8,128)S(1)}, u32[]{:S(2)}, u32[]{:S(2)}) collective-permute-start(f32[128,1024]{1,0:T(8,128)} %get-tuple-element.12), channel_id=1, source_target_pairs={{0,32},{1,33},{2,34},{3,35},{4,36},{5,37},{6,38},{7,39},{8,40},{9,... | collective-permute-start | bytes 1572872 | tf_op jit(solution)/shard_map/ppermute | solution.py:32
  58.9 12.4 %copy-start.5 = (f32[2048,512]{1,0:T(8,128)}, f32[2048,512]{1,0:T(8,128)S(1)}, u32[]{:S(2)}) copy-start(f32[2048,512]{1,0:T(8,128)S(1)} %get-tuple-element.13) | copy-start | bytes 12582916
  58.9 29.5 %collective-permute-start.4 = (f32[512,512]{1,0:T(8,128)}, f32[512,512]{1,0:T(8,128)S(1)}, u32[]{:S(2)}, u32[]{:S(2)}) collective-permute-start(f32[512,512]{1,0:T(8,128)} %get-tuple-element.14), channel_id=1, source_target_pairs={{0,2},{2,4},{4,6},{6,0},{8,10},{10,12},{12,14},{14,8},{16,18},{18,... | collective-permute-start | bytes 3145736 | tf_op jit(solution)/shard_map/ppermute | solution.py:32
  69.7 21.4 %collective-permute-start.5 = (f32[512,512]{1,0:T(8,128)}, f32[512,512]{1,0:T(8,128)}, u32[]{:S(2)}, u32[]{:S(2)}) collective-permute-start(f32[512,512]{1,0:T(8,128)} %get-tuple-element.14), channel_id=1, source_target_pairs={{0,6},{2,0},{4,2},{6,4},{8,14},{10,8},{12,10},{14,12},{16,22},{18,... | collective-permute-start | bytes 3145736 | tf_op jit(solution)/shard_map/ppermute | solution.py:32
  71.3 22.0 %collective-permute-start.6 = (f32[512,512]{1,0:T(8,128)}, f32[512,512]{1,0:T(8,128)}, u32[]{:S(2)}, u32[]{:S(2)}) collective-permute-start(f32[512,512]{1,0:T(8,128)} %get-tuple-element.14), channel_id=1, source_target_pairs={{0,4},{2,6},{4,0},{6,2},{8,12},{10,14},{12,8},{14,10},{16,20},{18,... | collective-permute-start | bytes 3145736 | tf_op jit(solution)/shard_map/ppermute | solution.py:32
  81.4 2.0 copy-start.4
  85.2 11.7 %collective-permute-start.15 = (f32[512,512]{1,0:T(8,128)}, f32[512,512]{1,0:T(8,128)}, u32[]{:S(2)}, u32[]{:S(2)}) collective-permute-start(f32[512,512]{1,0:T(8,128)} %get-tuple-element.20), channel_id=1, source_target_pairs={{0,2},{16,18},{32,34},{48,50},{64,66},{80,82},{96,98},{112,114}} | collective-permute-start | bytes 3145736 | tf_op jit(solution)/shard_map/ppermute | solution.py:32
  86.8 10.1 %collective-permute-start.16 = (f32[512,512]{1,0:T(8,128)}, f32[512,512]{1,0:T(8,128)}, u32[]{:S(2)}, u32[]{:S(2)}) collective-permute-start(f32[512,512]{1,0:T(8,128)} %get-tuple-element.19), channel_id=1, source_target_pairs={{0,4},{16,20},{32,36},{48,52},{64,68},{80,84},{96,100},{112,116}} | collective-permute-start | bytes 3145736 | tf_op jit(solution)/shard_map/ppermute | solution.py:32
  88.4 8.5 %collective-permute-start.17 = (f32[512,512]{1,0:T(8,128)}, f32[512,512]{1,0:T(8,128)}, u32[]{:S(2)}, u32[]{:S(2)}) collective-permute-start(f32[512,512]{1,0:T(8,128)} %get-tuple-element.18), channel_id=1, source_target_pairs={{0,6},{16,22},{32,38},{48,54},{64,70},{80,86},{96,102},{112,118}} | collective-permute-start | bytes 3145736 | tf_op jit(solution)/shard_map/ppermute | solution.py:32
  95.6 32.2 %collective-permute-start.7 = (f32[2048,512]{1,0:T(8,128)}, f32[2048,512]{1,0:T(8,128)}, u32[]{:S(2)}, u32[]{:S(2)}) collective-permute-start(f32[2048,512]{1,0:T(8,128)} %constant_dynamic-update-slice_fusion.12), channel_id=1, source_target_pairs={{0,1},{2,3},{4,5},{6,7},{8,9},{10,11},{12,13},{14,15},{16,17},{18,... | collective-permute-start | bytes 12582920 | tf_op jit(solution)/shard_map/ppermute | solution.py:32
  99.0 0.7 collective-permute-start.18
  103.5 2.2 collective-permute-start.19
  104.2 2.6 collective-permute-start.20
  104.9 2.9 collective-permute-start.21
  108.9 128.7 %collective-permute-start.22 = (f32[2048,512]{1,0:T(8,128)}, f32[2048,512]{1,0:T(8,128)}, u32[]{:S(2)}, u32[]{:S(2)}) collective-permute-start(f32[2048,512]{1,0:T(8,128)} %constant_dynamic-update-slice_fusion.4), channel_id=1, source_target_pairs={{0,1},{2,3},{4,5},{6,7},{8,9},{10,11},{12,13},{14,15},{16,17},{18,... | collective-permute-start | bytes 12582920 | tf_op jit(solution)/shard_map/ppermute | solution.py:32
  131.0 6.7 %copy-start = (f32[2048,512]{1,0:T(8,128)}, f32[2048,512]{1,0:T(8,128)S(1)}, u32[]{:S(2)}) copy-start(f32[2048,512]{1,0:T(8,128)S(1)} %broadcast_select_fusion.1.left_one) | copy-start | bytes 12582916
  131.0 3.1 copy-start.7
  134.1 13.4 %copy-start.12 = (s32[16,8]{0,1:T(8,128)S(1)}, s32[16,8]{0,1:T(8,128)}, u32[]{:S(2)}) copy-start(s32[16,8]{0,1:T(8,128)} %param.7) | copy-start | bytes 1540
  137.7 7.7 %copy-start.8 = (f32[512,1024]{1,0:T(8,128)}, f32[512,1024]{1,0:T(8,128)S(1)}, u32[]{:S(2)}) copy-start(f32[512,1024]{1,0:T(8,128)S(1)} %fusion.9) | copy-start | bytes 6291460
  137.7 21.0 %copy-start.13 = (s32[16,8]{0,1:T(8,128)S(1)}, s32[16,8]{0,1:T(8,128)}, u32[]{:S(2)}) copy-start(s32[16,8]{0,1:T(8,128)} %param.8) | copy-start | bytes 1540
  139.0 10.7 %collective-permute-start.23 = (f32[128,1024]{1,0:T(8,128)}, f32[128,1024]{1,0:T(8,128)S(1)}, u32[]{:S(2)}, u32[]{:S(2)}) collective-permute-start(f32[128,1024]{1,0:T(8,128)} %get-tuple-element.23), channel_id=1, source_target_pairs={{0,16},{1,17},{2,18},{3,19},{4,20},{5,21},{6,22},{7,23},{8,24},{9,... | collective-permute-start | bytes 1572872 | tf_op jit(solution)/shard_map/ppermute | solution.py:32
  143.3 12.0 %collective-permute-start.24 = (f32[128,1024]{1,0:T(8,128)}, f32[128,1024]{1,0:T(8,128)S(1)}, u32[]{:S(2)}, u32[]{:S(2)}) collective-permute-start(f32[128,1024]{1,0:T(8,128)} %get-tuple-element.22), channel_id=1, source_target_pairs={{0,32},{1,33},{2,34},{3,35},{4,36},{5,37},{6,38},{7,39},{8,40},{9,... | collective-permute-start | bytes 1572872 | tf_op jit(solution)/shard_map/ppermute | solution.py:32
  145.4 10.7 %collective-permute-start.25 = (f32[128,1024]{1,0:T(8,128)}, f32[128,1024]{1,0:T(8,128)}, u32[]{:S(2)}, u32[]{:S(2)}) collective-permute-start(f32[128,1024]{1,0:T(8,128)} %get-tuple-element.21), channel_id=1, source_target_pairs={{0,48},{1,49},{2,50},{3,51},{4,52},{5,53},{6,54},{7,55},{8,56},{9,... | collective-permute-start | bytes 1572872 | tf_op jit(solution)/shard_map/ppermute | solution.py:32
  155.3 0.8 copy-start.11
  157.4 75.0 %collective-permute-start.26 = (f32[128,1024]{1,0:T(8,128)S(1)}, f32[128,1024]{1,0:T(8,128)S(1)}, u32[]{:S(2)}, u32[]{:S(2)}) collective-permute-start(f32[128,1024]{1,0:T(8,128)S(1)} %slice_select_fusion.1), channel_id=1, source_target_pairs={{0,64},{1,65},{2,66},{3,67},{4,68},{5,69},{6,70},{7,71},{8,72},{9,... | collective-permute-start | bytes 1572872 | tf_op jit(solution)/shard_map/ppermute | solution.py:32
  159.9 121.8 %all-to-all-start = ((s32[128,1,1]{2,1,0:T(1,128)}), s32[128,1,1]{2,1,0:T(1,128)S(1)}, u32[]{:S(2)}, u32[]{:S(2)}) async-start(s32[128,1,1]{2,1,0:T(1,128)} %copy.35), calls=%async_computation | async-start | bytes 131072 | tf_op jit(solution)/shard_map/all_to_all | solution.py:266
  232.8 28.2 %copy-start.1 = (f32[2048,512]{1,0:T(8,128)S(1)}, f32[2048,512]{1,0:T(8,128)}, u32[]{:S(2)}) copy-start(f32[2048,512]{1,0:T(8,128)} %copy-done) | copy-start | bytes 12582916
  232.8 15.6 %collective-permute-start.27 = (f32[128,1024]{1,0:T(8,128)S(1)}, f32[128,1024]{1,0:T(8,128)S(1)}, u32[]{:S(2)}, u32[]{:S(2)}) collective-permute-start(f32[128,1024]{1,0:T(8,128)S(1)} %get-tuple-element.8), channel_id=1, source_target_pairs={{0,16},{1,17},{2,18},{3,19},{4,20},{5,21},{6,22},{7,23},{8,24},{9,... | collective-permute-start | bytes 1572872 | tf_op jit(solution)/shard_map/ppermute | solution.py:32
  234.4 14.1 %collective-permute-start.28 = (f32[128,1024]{1,0:T(8,128)S(1)}, f32[128,1024]{1,0:T(8,128)S(1)}, u32[]{:S(2)}, u32[]{:S(2)}) collective-permute-start(f32[128,1024]{1,0:T(8,128)S(1)} %get-tuple-element.8), channel_id=1, source_target_pairs={{0,48},{1,49},{2,50},{3,51},{4,52},{5,53},{6,54},{7,55},{8,56},{9,... | collective-permute-start | bytes 1572872 | tf_op jit(solution)/shard_map/ppermute | solution.py:32
  236.2 24.7 %collective-permute-start.29 = (f32[128,1024]{1,0:T(8,128)S(1)}, f32[128,1024]{1,0:T(8,128)S(1)}, u32[]{:S(2)}, u32[]{:S(2)}) collective-permute-start(f32[128,1024]{1,0:T(8,128)S(1)} %get-tuple-element.8), channel_id=1, source_target_pairs={{0,32},{1,33},{2,34},{3,35},{4,36},{5,37},{6,38},{7,39},{8,40},{9,... | collective-permute-start | bytes 1572872 | tf_op jit(solution)/shard_map/ppermute | solution.py:32
  279.7 2.0 copy-start.2
  281.7 120.9 %all-to-all-start.1 = ((f32[128,128,128]{2,1,0:T(8,128)}), f32[128,128,128]{2,1,0:T(8,128)}, u32[]{:S(2)}, u32[]{:S(2)}) async-start(f32[128,128,128]{2,1,0:T(8,128)} %get-tuple-element.6), calls=%async_computation.1 | async-start | bytes 16777216 | tf_op jit(solution)/shard_map/all_to_all | solution.py:282
  402.7 1.9 copy-start.3

commit v2 on v1

v2 whole, which is shorter than its diff:
```python
import jax
import jax.numpy as jnp
from jax import lax
from jax.experimental import pallas as pl
from jax.experimental.pallas import tpu as pltpu
from jax.sharding import PartitionSpec as P

AXES = ("row", "col")
MIB = 1024 * 1024


def device(xl, z, xh, y, core):
    return (xl * 4 + z) * 16 + xh * 8 + y * 2 + core


def pairs(move, keep=lambda *place: True):
    listed = []
    for xl in range(2):
        for z in range(4):
            for xh in range(2):
                for y in range(4):
                    for core in range(2):
                        place = (xl, z, xh, y, core)
                        if keep(*place):
                            listed.append((device(*place), device(*move(*place))))
    return listed


def send(value, move, keep=lambda *place: True):
    return lax.ppermute(value, AXES, pairs(move, keep))


def place():
    row = lax.axis_index("row")
    col = lax.axis_index("col")
    return row // 4, row % 4, col // 8, (col // 2) % 4, col % 2


def choose(index, options):
    value = options[-1]
    for number in range(len(options) - 2, -1, -1):
        value = jnp.where(index == number, options[number], value)
    return value


def partner(k, first):
    return k ^ 1 if first else 3 - k


def exchange(columns, rows):
    xl, z, xh, y, core = place()
    edge = columns.shape[0] // 8
    parts = [columns[k * edge : (k + 1) * edge] for k in range(8)]
    lift = rows.shape[0] // 4
    layers = [rows[k * lift : (k + 1) * lift] for k in range(4)]

    came_columns = {}
    came_rows = {}
    for k in (2, 1, 3):
        for to in range(2):
            came_columns[2 * k + to] = send(
                parts[2 * k + to],
                lambda xl, z, xh, y, core, k=k, to=to: (xl, z, xh, k, to),
                lambda xl, z, xh, y, core: xh == 0 and y == 0 and core == 0,
            )
    for k in (2, 1, 3):
        came_rows[k] = send(
            layers[k],
            lambda xl, z, xh, y, core, k=k: (xl, k, xh, y, core),
            lambda xl, z, xh, y, core: xl == 0 and z == 0,
        )
    came_columns[1] = send(
        parts[1],
        lambda xl, z, xh, y, core: (xl, z, xh, y, 1),
        lambda xl, z, xh, y, core: xh == 0 and y == 0 and core == 0,
    )
    column = choose(2 * y + core, [parts[0]] + [came_columns[k] for k in range(1, 8)])
    row = choose(z, [layers[0]] + [came_rows[k] for k in range(1, 4)])
    column, row = lax.optimization_barrier((column, row))

    column_across = send(
        column,
        lambda xl, z, xh, y, core: (xl, z, 1, y, core),
        lambda xl, z, xh, y, core: xh == 0,
    )
    row_across = send(
        row,
        lambda xl, z, xh, y, core: (1, z, xh, y, core),
        lambda xl, z, xh, y, core: xl == 0,
    )
    column = jnp.where(xh == 0, column, column_across)
    row = jnp.where(xl == 0, row, row_across)
    column, row = lax.optimization_barrier((column, row))

    def around(value, step):
        return send(
            value,
            lambda xl, z, xh, y, core: (xl, z, xh, partner(y, (core == 0) == (step == 0)), core),
        )

    def along(value, step):
        return send(
            value,
            lambda xl, z, xh, y, core: (xl, partner(z, (core == 0) == (step == 0)), xh, y, core),
        )

    def swap(value):
        return send(value, lambda xl, z, xh, y, core: (xl, z, xh, y, 1 - core))

    column_a, row_a = around(column, 0), along(row, 0)
    column_b, row_b = around(column, 1), along(row, 1)
    other = swap(column)
    column_a, row_a = lax.optimization_barrier((column_a, row_a))
    column_c, row_c = around(column_a, 1), along(row_a, 1)
    other_a, other_b = swap(column_a), swap(column_b)
    other_c = swap(column_c)

    def order(k, core):
        one = jnp.where(core == 0, k ^ 1, 3 - k)
        two = jnp.where(core == 0, 3 - k, k ^ 1)
        return [k, one, two, 3 - (k ^ 1)]

    pieces = [column, other, column_a, column_b, other_a, other_b, column_c, other_c]
    mine, theirs = order(y, core), order(y, 1 - core)
    numbers = [
        2 * mine[0] + core,
        2 * theirs[0] + 1 - core,
        2 * mine[1] + core,
        2 * mine[2] + core,
        2 * theirs[1] + 1 - core,
        2 * theirs[2] + 1 - core,
        2 * mine[3] + core,
        2 * theirs[3] + 1 - core,
    ]
    return pieces, numbers, [row, row_a, row_b, row_c], order(z, core)


def halves(value):
    high = value.astype(jnp.bfloat16)
    low = (value - high.astype(jnp.float32)).astype(jnp.bfloat16)
    return high, low


def dot(left, right):
    return jnp.dot(left, right, preferred_element_type=jnp.float32)


def product(left, right):
    left_high, left_low = halves(left)
    right_high, right_low = halves(right)
    return dot(left_high, right_low) + dot(left_low, right_high) + dot(left_high, right_high)


def update_kernel(
    table_ref, owner_ref, front_ref, pivot_ref, inverse_ref, *refs
):
    column_refs = refs[:8]
    row_refs = refs[8:12]
    updated_ref, outgoing_ref, mine_ref = refs[12:15]
    right, high, low, held, result, held_sem, whole_sem, block_sem = refs[15:]
    step = pl.program_id(0)
    steps = pl.num_programs(0)
    slot = lax.rem(step, 2)
    tile = result.shape[1]
    edge = outgoing_ref.shape[1]
    depth = inverse_ref.shape[0]
    down, across = tile // edge, result.shape[2] // edge

    def fetch(number, at):
        return pltpu.make_async_copy(column_refs[number], held.at[at], held_sem.at[at])

    def whole_copy(at, number):
        top = pl.multiple_of(table_ref[number] * tile, tile)
        return pltpu.make_async_copy(
            result.at[at], updated_ref.at[pl.ds(top, tile)], whole_sem.at[at]
        )

    def block_copies(at, number, act):
        for i in range(down):
            for j in range(across):
                owner = owner_ref[table_ref[number] * down + i, j]

                @pl.when(owner >= 0)
                def _():
                    act(
                        pltpu.make_async_copy(
                            result.at[at, pl.ds(i * edge, edge), pl.ds(j * edge, edge)],
                            outgoing_ref.at[jnp.maximum(owner, 0)],
                            block_sem.at[at],
                        )
                    )

    def finish(at, number):
        whole_copy(at, number).wait()
        block_copies(at, number, lambda copy: copy.wait())

    @pl.when(step == 0)
    def _():
        fetch(0, 0).start()
        lift = row_refs[0].shape[0]
        for k in range(4):
            top = pl.multiple_of(table_ref[8 + k] * lift, lift)
            right[pl.ds(top, lift)] = row_refs[k][...]
        one = right[:depth]
        two = right[depth:] - product(pivot_ref[depth:], one)
        two = product(inverse_ref[...], two)
        high[depth:], low[depth:] = halves(two)
        one = one - product(pivot_ref[:depth], two)
        high[:depth], low[:depth] = halves(one)

    for number in range(8):

        @pl.when(step == number)
        def _():
            if number < 7:
                fetch(number + 1, (number + 1) % 2).start()
            fetch(number, number % 2).wait()

    @pl.when(step >= 2)
    def _():
        finish(slot, step - 2)

    left = held[slot]
    left_high, left_low = halves(left)
    total = front_ref[...] - dot(left_high, low[...])
    total -= dot(left_low, high[...])
    total -= dot(left_high, high[...])
    result[slot] = total
    whole_copy(slot, step).start()
    block_copies(slot, step, lambda copy: copy.start())

    @pl.when(table_ref[step] == table_ref[12])
    def _():
        top = pl.multiple_of(table_ref[13] * edge, edge)
        mine_ref[...] = held[slot, pl.ds(top, edge)]

    @pl.when(step == steps - 1)
    def _():
        finish(1 - slot, step - 1)
        finish(slot, step)


def update(front, block_owner, pivot, inverse, pieces, layers, table, devices, edge):
    rows, columns = front.shape
    tile = pieces[0].shape[0]
    whole = lambda *shape: pl.BlockSpec(shape, lambda i, table: (0,) * len(shape))
    return pl.pallas_call(
        update_kernel,
        grid_spec=pltpu.PrefetchScalarGridSpec(
            num_scalar_prefetch=1,
            grid=(rows // tile,),
            in_specs=[
                pl.BlockSpec(memory_space=pltpu.SMEM),
                pl.BlockSpec((tile, columns), lambda i, table: (table[i], 0)),
                whole(*pivot.shape),
                whole(*inverse.shape),
            ]
            + [pl.BlockSpec(memory_space=pl.ANY)] * 8
            + [whole(*layers[0].shape)] * 4,
            out_specs=[
                pl.BlockSpec(memory_space=pl.ANY),
                pl.BlockSpec(memory_space=pl.ANY),
                whole(edge, pieces[0].shape[1]),
            ],
            scratch_shapes=[
                pltpu.VMEM((2 * inverse.shape[0], columns), jnp.float32),
                pltpu.VMEM((2 * inverse.shape[0], columns), jnp.bfloat16),
                pltpu.VMEM((2 * inverse.shape[0], columns), jnp.bfloat16),
                pltpu.VMEM((2, tile, pieces[0].shape[1]), jnp.float32),
                pltpu.VMEM((2, tile, columns), jnp.float32),
                pltpu.SemaphoreType.DMA((2,)),
                pltpu.SemaphoreType.DMA((2,)),
                pltpu.SemaphoreType.DMA((2,)),
            ],
        ),
        out_shape=[
            jax.ShapeDtypeStruct((rows, columns), jnp.float32),
            jax.ShapeDtypeStruct((devices, edge, edge), jnp.float32),
            jax.ShapeDtypeStruct((edge, pieces[0].shape[1]), jnp.float32),
        ],
        compiler_params=pltpu.CompilerParams(vmem_limit_bytes=44 * MIB),
        cost_estimate=pl.CostEstimate(
            flops=16 * rows * columns * inverse.shape[0],
            bytes_accessed=40 * MIB,
            transcendentals=0,
        ),
        name="update",
    )(table, block_owner, front, pivot, inverse, *pieces, *layers)


def add_kernel(slot_ref, parent_ref, arrived_ref, out_ref, sem):
    step = pl.program_id(0)
    count = arrived_ref.shape[0]

    @pl.when(step == 0)
    def _():
        copy = pltpu.make_async_copy(parent_ref, out_ref, sem)
        copy.start()
        copy.wait()

    for k in range(count):
        slot = slot_ref[step * count + k]

        @pl.when(slot >= 0)
        def _():
            at = jnp.maximum(slot, 0)
            out_ref[at] = out_ref[at] + arrived_ref[k]


def extend_add(slots, parent, arrived):
    count = 16
    held, edge, _ = parent.shape
    return pl.pallas_call(
        add_kernel,
        grid=(arrived.shape[0] // count,),
        in_specs=[
            pl.BlockSpec(memory_space=pltpu.SMEM),
            pl.BlockSpec(memory_space=pl.ANY),
            pl.BlockSpec((count, edge, edge), lambda i: (i, 0, 0)),
        ],
        out_specs=pl.BlockSpec((held, edge, edge), lambda i: (0, 0, 0)),
        out_shape=jax.ShapeDtypeStruct(parent.shape, jnp.float32),
        scratch_shapes=[pltpu.SemaphoreType.DMA],
        compiler_params=pltpu.CompilerParams(vmem_limit_bytes=32 * MIB),
        cost_estimate=pl.CostEstimate(flops=2 * MIB, bytes_accessed=14 * MIB, transcendentals=0),
        name="extend_add",
    )(slots, parent, arrived)


def exact(left, right):
    return jnp.dot(left, right, preferred_element_type=jnp.float32, precision=lax.Precision.HIGHEST)


def local(front, inverses, block_owner, block_slot, parent_in):
    width = inverses.shape[1]
    edge = parent_in.shape[1]
    devices = lax.axis_size("row") * lax.axis_size("col")
    row, col = lax.axis_index("row"), lax.axis_index("col")
    me = row * lax.axis_size("col") + col

    columns = front[:, : 2 * width]
    rows_one = product_rows(inverses[0], front[:width])
    rows = jnp.concatenate([rows_one, front[width : 2 * width]], axis=0)

    owners = block_owner.reshape(-1)
    slots = block_slot.reshape(-1)
    names = jnp.arange(devices, dtype=jnp.int32)
    named = owners[None, :] == names[:, None]
    labels = jnp.sum(jnp.where(named, slots[None, :] + 1, 0), axis=1).astype(jnp.float32)
    labels = jnp.where(names[None, :] == me, labels[:, None], 0.0)
    pivot = jnp.concatenate(
        [rows_one[:, width : 2 * width], front[width : 2 * width, :width]], axis=0
    )
    pivot = jnp.where(me == 0, pivot, 0.0)
    fill = devices * devices // width
    shared = lax.psum(jnp.concatenate([pivot, labels.reshape(fill, width)], axis=0), AXES)
    pivot = shared[: 2 * width]
    markers = shared[2 * width :].reshape(devices, devices)
    markers = lax.dynamic_slice_in_dim(markers, me, 1, 0).reshape(devices).astype(jnp.int32) - 1

    pieces, numbers, layers, heights = exchange(columns, rows)
    table = jnp.stack(numbers + heights + [col // 2, col % 2]).astype(jnp.int32)
    updated, outgoing, mine = update(
        front, block_owner, pivot, inverses[1], pieces, layers, table, devices, edge
    )
    arrived = lax.all_to_all(outgoing, AXES, 0, 0, tiled=True)

    mine_one, mine_two = mine[:, :width], mine[:, width:]
    mine_two = mine_two - exact(mine_one, pivot[:width])
    panels = jnp.concatenate([exact(mine_one, inverses[0]), exact(mine_two, inverses[1])], axis=1)
    parent_out = extend_add(markers, parent_in, arrived)
    return (updated, panels, parent_out)


def product_rows(left, right):
    return jnp.dot(left, right, preferred_element_type=jnp.float32, precision=lax.Precision.HIGH)


def solution(mesh):
    in_specs = (
        P("row", "col"),
        P(),
        P("row", "col"),
        P("row", "col"),
        P(("row", "col"), None, None),
    )
    out_specs = (P("row", "col"), P(("row", "col"), None), P(("row", "col"), None, None))
    return jax.shard_map(local, mesh=mesh, in_specs=in_specs, out_specs=out_specs, check_vma=False)
```

time: 418 us -> 467 us (1.12)
  waiting for transfers between devices: 178 us -> 306 us
  starting transfers between devices: 133 us -> 74.9 us
  local copies, waits for them, and re-layouts: 32.2 us -> 14.4 us
  between operations: 1.16 us -> 14.5 us
  matrix products: 20.8 us -> 8.31 us
  other arithmetic: 21 us -> 13.4 us
    psum x0 -> x1, waiting for transfers between devices: none -> 141 us  [local(): lax.psum(jnp.concatenate([pivot, labels.reshape(fill, width)], axis=0), A...]
    all_to_all x1 -> x0, starting transfers between devices: 72.5 us -> none  [local(): lax.all_to_all(labels.reshape(devices, 1, 1), AXES, 0, 0, tiled=True)]
    ppermute x30 -> x22, starting transfers between devices: 51.7 us -> 67.1 us  [send(): return lax.ppermute(value, AXES, pairs(move, keep))]
    ppermute x30 -> x22, waiting for transfers between devices: 72.2 us -> 58.3 us  [send(): return lax.ppermute(value, AXES, pairs(move, keep))]
    dot_general x6 -> x4, matrix products: 20.8 us -> 8.31 us  [the longest x3 4.55 us: exact(): jnp.dot(left, right, preferred_element_type=jnp.float32, precision=lax.Pr...]
    dynamic_update_slice x12 -> x0, local copies, waits for them, and re-layouts: 11.1 us -> none  [assemble(): lax.dynamic_update_slice(whole, piece, ((index + shift) % 4 * size, 0))]
    unnamed x29 -> x31, local copies, waits for them, and re-layouts: 9.33 us -> 0.14 us
    pallas_call x1, Pallas kernels: 18.7 us -> 26.6 us  [update(): pl.pallas_call(update_kernel, grid_spec=pltpu.PrefetchScalarGridSpec(num_...]
  transfers between devices with their start and end apart: 32 -> 24, of which waited for: 10 -> 9; matrix products, arithmetic and copies ran while one was open for 15% -> 6% of each run, Pallas kernels for 5% -> 0%
where the time goes in v2:
time: 467 us; the launch traced here: 466 us
  waiting for transfers between devices  306 us (66%)
  starting transfers between devices  74.9 us (16%)
  Pallas kernels  34.8 us (7%)
  between operations  14.5 us (3%)
  local copies, waits for them, and re-layouts  14.4 us (3%)
  other arithmetic  13.4 us (3%)
  matrix products  8.31 us (2%)
    psum x1, waiting for transfers between devices, local(): lax.psum(jnp.concatenate([pivot, labels.reshape(fill, width)], axis=0), A...  141 us
    all_to_all x1, waiting for transfers between devices, local(): arrived = lax.all_to_all(outgoing, AXES, 0, 0, tiled=True)  107 us
    ppermute x22, starting transfers between devices, send(): return lax.ppermute(value, AXES, pairs(move, keep))  67.1 us
    ppermute x22, waiting for transfers between devices, send(): return lax.ppermute(value, AXES, pairs(move, keep))  58.3 us
    pallas_call x1, Pallas kernels, update(): pl.pallas_call(update_kernel, grid_spec=pltpu.PrefetchScalarGridSpec(num_...  26.6 us
  transfers between devices with their start and end apart: 24, of which 9 were waited for; matrix products, arithmetic and copies ran while one was open for 6% of the time, Pallas kernels for 0%

profile of v2, /device:TPU:1, one launch (start us, length us, event | category | flops | bytes accessed | tf_op | source)
XLA Modules:
  0.0 466.1 jit_solution(17373514583674138861)
XLA Ops:
  7.2 0.0 all-reduce.2.cloned.1.call-start
  7.2 3.8 fusion
  11.0 0.1 slice.91
  11.1 4.4 collective-permute-start.7
  15.5 5.9 %fusion.14 = (f32[256,1024]{1,0:T(8,128)S(1)}, f32[256,1024]{1,0:T(8,128)S(1)}, f32[256,1024]{1,0:T(8,128)}, f32[256,1024]{1,0:T(8,128)}, f32[256,1024]{1,0:T(8,...) fusion(f32[2048,1024]{1,0:T(8,128)} %front_ref.1), kind=kLoop, calls=%fused_computation.29 | loop fusion | bytes 14680064 | tf_op jit(solution)/shard_map/slice | solution.py:53
  21.4 0.7 collective-permute-start.6
  22.1 0.7 collective-permute-start.5
  22.9 2.8 collective-permute-start.9
  25.7 1.4 collective-permute-start.8
  27.1 10.1 %collective-permute-done.7 = f32[256,1024]{1,0:T(8,128)S(1)} collective-permute-done((f32[256,1024]{1,0:T(8,128)S(1)}, f32[256,1024]{1,0:T(8,128)S(1)}, u32[]{:S(2)}, u32[]{:S(2)}) %collective-permute-start.7) | collective-permute-done | bytes 1048608 | tf_op jit(solution)/shard_map/ppermute | solution.py:30
  37.2 1.6 collective-permute-start.2
  38.9 1.7 collective-permute-start.4
  40.5 1.7 collective-permute-start.3
  42.2 1.2 collective-permute-done.9
  43.4 1.3 collective-permute-start
  44.7 15.0 %collective-permute-done.8 = f32[256,1024]{1,0:T(8,128)S(1)} collective-permute-done((f32[256,1024]{1,0:T(8,128)S(1)}, f32[256,1024]{1,0:T(8,128)S(1)}, u32[]{:S(2)}, u32[]{:S(2)}) %collective-permute-start.8) | collective-permute-done | bytes 1048608 | tf_op jit(solution)/shard_map/ppermute | solution.py:30
  59.7 1.7 collective-permute-start.1
  61.6 2.8 slice_select_fusion
  64.4 2.5 select_select_fusion
  66.9 0.0 copy-start.4
  66.9 5.6 %collective-permute-start.10 = (f32[256,1024]{1,0:T(8,128)S(1)}, f32[256,1024]{1,0:T(8,128)}, u32[]{:S(2)}, u32[]{:S(2)}) collective-permute-start(f32[256,1024]{1,0:T(8,128)S(1)} %select_select_fusion), channel_id=1, source_target_pairs={{0,8},{1,9},{2,10},{3,11},{4,12},{5,13},{6,14},{7,15},{16,24},{17,... | collective-permute-start | bytes 3145736 | tf_op jit(solution)/shard_map/ppermute | solution.py:30
  72.6 2.3 collective-permute-start.11
  74.8 8.5 %collective-permute-done.10 = f32[256,1024]{1,0:T(8,128)} collective-permute-done((f32[256,1024]{1,0:T(8,128)S(1)}, f32[256,1024]{1,0:T(8,128)}, u32[]{:S(2)}, u32[]{:S(2)}) %collective-permute-start.10) | collective-permute-done | bytes 1048608 | tf_op jit(solution)/shard_map/ppermute | solution.py:30
  83.3 1.4 broadcast_select_fusion.1.refs_0_
  84.7 12.8 %collective-permute-done.11 = f32[256,1024]{1,0:T(8,128)} collective-permute-done((f32[256,1024]{1,0:T(8,128)}, f32[256,1024]{1,0:T(8,128)}, u32[]{:S(2)}, u32[]{:S(2)}) %collective-permute-start.11) | collective-permute-done | bytes 1048608 | tf_op jit(solution)/shard_map/ppermute | solution.py:30
  97.5 2.4 broadcast_select_fusion.refs_8_
  100.0 20.1 %collective-permute-start.13 = (f32[256,1024]{1,0:T(8,128)S(1)}, f32[256,1024]{1,0:T(8,128)}, u32[]{:S(2)}, u32[]{:S(2)}) collective-permute-start(f32[256,1024]{1,0:T(8,128)S(1)} %broadcast_select_fusion.1.refs_0_), channel_id=1, source_target_pairs={{0,2},{1,7},{2,0},{3,5},{4,6},{5,3},{6,4},{7,1},{8,10},{9,15},{10,... | collective-permute-start | bytes 3145736 | tf_op jit(solution)/shard_map/ppermute | solution.py:30
  120.0 2.3 slice.71
  122.3 1.1 slice.88
  123.3 0.1 copy.15
  123.4 0.1 add.77
  123.5 0.1 copy.16.owner_ref
  123.6 0.1 eq.85
  123.7 0.1 select_reduce_fusion
  123.8 0.1 convert_element_type.15
  123.9 3.4 collective-permute-start.20
  127.3 0.2 collective-permute-start.15
  127.5 5.0 %collective-permute-done.13.refs_2_ = f32[256,1024]{1,0:T(8,128)} collective-permute-done((f32[256,1024]{1,0:T(8,128)S(1)}, f32[256,1024]{1,0:T(8,128)}, u32[]{:S(2)}, u32[]{:S(2)}) %collective-permute-start.13) | collective-permute-done | bytes 1048608 | tf_op jit(solution)/shard_map/ppermute | solution.py:30
  132.5 1.8 maximum_select_fusion
  134.3 0.1 broadcast_in_dim.51
  134.4 1.5 pad_maximum_fusion
  135.9 0.0 all-reduce.2.cloned.1.call-update
  136.0 13.5 %collective-permute-start.12 = (f32[256,1024]{1,0:T(8,128)S(1)}, f32[256,1024]{1,0:T(8,128)}, u32[]{:S(2)}, u32[]{:S(2)}) collective-permute-start(f32[256,1024]{1,0:T(8,128)S(1)} %broadcast_select_fusion.1.refs_0_), channel_id=1, source_target_pairs={{0,1},{1,0},{2,3},{3,2},{4,5},{5,4},{6,7},{7,6},{8,9},{9,8},{10,11... | collective-permute-start | bytes 3145736 | tf_op jit(solution)/shard_map/ppermute | solution.py:30
  149.5 0.1 collective-permute-start.16
  149.6 0.4 collective-permute-start.17
  150.0 1.7 collective-permute-start.21
  151.8 5.6 %collective-permute-done.18.refs_6_ = f32[256,1024]{1,0:T(8,128)} collective-permute-done((f32[256,1024]{1,0:T(8,128)}, f32[256,1024]{1,0:T(8,128)}, u32[]{:S(2)}, u32[]{:S(2)}) %collective-permute-start.18) | collective-permute-done | bytes 1048608 | tf_op jit(solution)/shard_map/ppermute | solution.py:30
  157.4 1.7 collective-permute-start.19
  159.1 0.1 stack.59.table_ref
  159.2 1.3 slice_bitcast_fusion.inverse_ref
  160.5 140.6 %all-reduce.2.cloned.1.call-done = f32[1056,512]{1,0:T(8,128)} async-done(((f32[1056,512]{1,0:T(8,128)}), f32[1056,512]{1,0:T(8,128)}) %all-reduce.2.cloned.1.call-update) | async-done | bytes 2162704 | tf_op jit(solution)/shard_map/psum | solution.py:356
  301.1 3.1 slice.89.pivot_ref
  304.2 26.6 %update.1 = (f32[2048,1024]{1,0:T(8,128)}, f32[128,128,128]{2,1,0:T(8,128)}, f32[128,1024]{1,0:T(8,128)S(1)}) custom-call(s32[14]{0:T(128)S(1)} %stack.59.table_ref, s32[16,8]{1,0:T(8,128)S(1)} %copy.16.owner_ref, f32[2048,1024]{1,0:T(8,128)} %front_ref.1, f32[1024,512]{1,0:T(8,128)} %slice.89.pivot_ref, f32[512,512]{1,0:T(8,128)S(1)} %slice_bitcast_fusion.inverse_ref, ...), custom_call_target="tpu_custom_call" | custom-call | flops 17179869184 | bytes 41943040 | tf_op jit(solution)/shard_map/update/pallas_call | solution.py:247
  330.8 0.0 copy-start.1
  330.8 0.0 copy-start.2
  330.8 7.8 %all-to-all-start = ((f32[128,128,128]{2,1,0:T(8,128)}), f32[128,128,128]{2,1,0:T(8,128)}, u32[]{:S(2)}, u32[]{:S(2)}) async-start(f32[128,128,128]{2,1,0:T(8,128)} %get-tuple-element.20), calls=%async_computation | async-start | bytes 16777216 | tf_op jit(solution)/shard_map/all_to_all | solution.py:366
  338.6 0.0 copy-start.3
  338.7 0.7 fusion.4
  339.4 0.0 copy-start
  339.4 2.2 fusion.2
  341.6 1.7 fusion.9
  343.3 0.8 pad_maximum_fusion.1
  344.1 106.9 %all-to-all-done.arrived_ref = f32[128,128,128]{2,1,0:T(8,128)} async-done(((f32[128,128,128]{2,1,0:T(8,128)}), f32[128,128,128]{2,1,0:T(8,128)}, u32[]{:S(2)}, u32[]{:S(2)}) %all-to-all-start) | async-done | bytes 8388640 | tf_op jit(solution)/shard_map/all_to_all | solution.py:366
  451.0 8.2 %extend_add.1 = f32[48,128,128]{2,1,0:T(8,128)} custom-call(s32[128]{0:T(128)S(1)} %add_bitcast_fusion.slot_ref, f32[48,128,128]{2,1,0:T(8,128)S(1)} %copy-done, f32[128,128,128]{2,1,0:T(8,128)} %all-to-all-done.arrived_ref), custom_call_target="tpu_custom_call" | custom-call | flops 2097152 | bytes 14680064 | tf_op jit(solution)/shard_map/extend_add/pallas_call | solution.py:313
  (51 shorter events, 0.1 us)
Async XLA Ops:
  7.2 293.9 %all-reduce.2.cloned.1.call-start = ((), (), s32[]{:S(2)}) async-start(), calls=%async_computation.1 | async-start | bytes 4325376 | tf_op jit(solution)/shard_map/psum | solution.py:356
  11.1 26.2 %collective-permute-start.7 = (f32[256,1024]{1,0:T(8,128)S(1)}, f32[256,1024]{1,0:T(8,128)S(1)}, u32[]{:S(2)}, u32[]{:S(2)}) collective-permute-start(f32[256,1024]{1,0:T(8,128)S(1)} %slice.91), channel_id=1, source_target_pairs={{0,16},{1,17},{2,18},{3,19},{4,20},{5,21},{6,22},{7,23},{8,24},{9,... | collective-permute-start | bytes 3145736 | tf_op jit(solution)/shard_map/ppermute | solution.py:30
  21.4 17.4 %collective-permute-start.6 = (f32[256,1024]{1,0:T(8,128)S(1)}, f32[256,1024]{1,0:T(8,128)S(1)}, u32[]{:S(2)}, u32[]{:S(2)}) collective-permute-start(f32[256,1024]{1,0:T(8,128)S(1)} %get-tuple-element.21), channel_id=1, source_target_pairs={{0,7},{16,23},{32,39},{48,55},{64,71},{80,87},{96,103},{112,119}} | collective-permute-start | bytes 3145736 | tf_op jit(solution)/shard_map/ppermute | solution.py:30
  22.1 18.4 %collective-permute-start.5 = (f32[256,1024]{1,0:T(8,128)S(1)}, f32[256,1024]{1,0:T(8,128)S(1)}, u32[]{:S(2)}, u32[]{:S(2)}) collective-permute-start(f32[256,1024]{1,0:T(8,128)S(1)} %get-tuple-element.22), channel_id=1, source_target_pairs={{0,6},{16,22},{32,38},{48,54},{64,70},{80,86},{96,102},{112,118}} | collective-permute-start | bytes 3145736 | tf_op jit(solution)/shard_map/ppermute | solution.py:30
  22.9 20.5 %collective-permute-start.9 = (f32[256,1024]{1,0:T(8,128)}, f32[256,1024]{1,0:T(8,128)S(1)}, u32[]{:S(2)}, u32[]{:S(2)}) collective-permute-start(f32[256,1024]{1,0:T(8,128)} %get-tuple-element.25), channel_id=1, source_target_pairs={{0,48},{1,49},{2,50},{3,51},{4,52},{5,53},{6,54},{7,55},{8,56},{9,... | collective-permute-start | bytes 3145736 | tf_op jit(solution)/shard_map/ppermute | solution.py:30
  25.7 34.0 %collective-permute-start.8 = (f32[256,1024]{1,0:T(8,128)S(1)}, f32[256,1024]{1,0:T(8,128)S(1)}, u32[]{:S(2)}, u32[]{:S(2)}) collective-permute-start(f32[256,1024]{1,0:T(8,128)S(1)} %get-tuple-element.26), channel_id=1, source_target_pairs={{0,32},{1,33},{2,34},{3,35},{4,36},{5,37},{6,38},{7,39},{8,40},{9,... | collective-permute-start | bytes 3145736 | tf_op jit(solution)/shard_map/ppermute | solution.py:30
  37.2 24.2 %copy-start.5 = (f32[256,1024]{1,0:T(8,128)}, f32[256,1024]{1,0:T(8,128)S(1)}, u32[]{:S(2)}) copy-start(f32[256,1024]{1,0:T(8,128)S(1)} %collective-permute-done.7) | copy-start | bytes 3145732
  37.2 27.1 %collective-permute-start.2 = (f32[256,1024]{1,0:T(8,128)}, f32[256,1024]{1,0:T(8,128)}, u32[]{:S(2)}, u32[]{:S(2)}) collective-permute-start(f32[256,1024]{1,0:T(8,128)} %get-tuple-element.25), channel_id=1, source_target_pairs={{0,3},{16,19},{32,35},{48,51},{64,67},{80,83},{96,99},{112,115}} | collective-permute-start | bytes 3145736 | tf_op jit(solution)/shard_map/ppermute | solution.py:30
  38.9 22.6 %copy-start.8 = (f32[256,1024]{1,0:T(8,128)}, f32[256,1024]{1,0:T(8,128)S(1)}, u32[]{:S(2)}) copy-start(f32[256,1024]{1,0:T(8,128)S(1)} %collective-permute-done.6) | copy-start | bytes 3145732
  38.9 25.5 %collective-permute-start.4 = (f32[256,1024]{1,0:T(8,128)}, f32[256,1024]{1,0:T(8,128)}, u32[]{:S(2)}, u32[]{:S(2)}) collective-permute-start(f32[256,1024]{1,0:T(8,128)} %get-tuple-element.23), channel_id=1, source_target_pairs={{0,5},{16,21},{32,37},{48,53},{64,69},{80,85},{96,101},{112,117}} | collective-permute-start | bytes 3145736 | tf_op jit(solution)/shard_map/ppermute | solution.py:30
  40.5 20.9 %copy-start.10 = (f32[256,1024]{1,0:T(8,128)}, f32[256,1024]{1,0:T(8,128)S(1)}, u32[]{:S(2)}) copy-start(f32[256,1024]{1,0:T(8,128)S(1)} %collective-permute-done.5) | copy-start | bytes 3145732
  40.5 23.8 %collective-permute-start.3 = (f32[256,1024]{1,0:T(8,128)}, f32[256,1024]{1,0:T(8,128)}, u32[]{:S(2)}, u32[]{:S(2)}) collective-permute-start(f32[256,1024]{1,0:T(8,128)} %get-tuple-element.24), channel_id=1, source_target_pairs={{0,4},{16,20},{32,36},{48,52},{64,68},{80,84},{96,100},{112,116}} | collective-permute-start | bytes 3145736 | tf_op jit(solution)/shard_map/ppermute | solution.py:30
  43.4 18.0 %copy-start.6 = (f32[256,1024]{1,0:T(8,128)}, f32[256,1024]{1,0:T(8,128)S(1)}, u32[]{:S(2)}) copy-start(f32[256,1024]{1,0:T(8,128)S(1)} %collective-permute-done.9) | copy-start | bytes 3145732
  43.4 20.9 %collective-permute-start = (f32[256,1024]{1,0:T(8,128)}, f32[256,1024]{1,0:T(8,128)}, u32[]{:S(2)}, u32[]{:S(2)}) collective-permute-start(f32[256,1024]{1,0:T(8,128)} %get-tuple-element.27), channel_id=1, source_target_pairs={{0,1},{16,17},{32,33},{48,49},{64,65},{80,81},{96,97},{112,113}} | collective-permute-start | bytes 3145736 | tf_op jit(solution)/shard_map/ppermute | solution.py:30
  59.7 1.8 copy-start.7
  59.7 4.7 %collective-permute-start.1 = (f32[256,1024]{1,0:T(8,128)S(1)}, f32[256,1024]{1,0:T(8,128)}, u32[]{:S(2)}, u32[]{:S(2)}) collective-permute-start(f32[256,1024]{1,0:T(8,128)S(1)} %get-tuple-element.26), channel_id=1, source_target_pairs={{0,2},{16,18},{32,34},{48,50},{64,66},{80,82},{96,98},{112,114}} | collective-permute-start | bytes 3145736 | tf_op jit(solution)/shard_map/ppermute | solution.py:30
  61.5 2.9 copy-start.9
  61.5 2.9 copy-start.11
  66.9 7.9 %copy-start.4 = (f32[256,1024]{1,0:T(8,128)}, f32[256,1024]{1,0:T(8,128)S(1)}, u32[]{:S(2)}) copy-start(f32[256,1024]{1,0:T(8,128)S(1)} %select_select_fusion) | copy-start | bytes 3145732
  66.9 16.4 %collective-permute-start.10 = (f32[256,1024]{1,0:T(8,128)S(1)}, f32[256,1024]{1,0:T(8,128)}, u32[]{:S(2)}, u32[]{:S(2)}) collective-permute-start(f32[256,1024]{1,0:T(8,128)S(1)} %select_select_fusion), channel_id=1, source_target_pairs={{0,8},{1,9},{2,10},{3,11},{4,12},{5,13},{6,14},{7,15},{16,24},{17,... | collective-permute-start | bytes 3145736 | tf_op jit(solution)/shard_map/ppermute | solution.py:30
  72.6 25.0 %collective-permute-start.11 = (f32[256,1024]{1,0:T(8,128)}, f32[256,1024]{1,0:T(8,128)}, u32[]{:S(2)}, u32[]{:S(2)}) collective-permute-start(f32[256,1024]{1,0:T(8,128)} %slice_select_fusion), channel_id=1, source_target_pairs={{0,64},{1,65},{2,66},{3,67},{4,68},{5,69},{6,70},{7,71},{8,72},{9,... | collective-permute-start | bytes 3145736 | tf_op jit(solution)/shard_map/ppermute | solution.py:30
  100.0 23.4 %copy-start.13 = (s32[16,8]{0,1:T(8,128)S(1)}, s32[16,8]{0,1:T(8,128)}, u32[]{:S(2)}) copy-start(s32[16,8]{0,1:T(8,128)} %param.8) | copy-start | bytes 1540
  100.0 23.6 %copy-start.12 = (s32[16,8]{0,1:T(8,128)S(1)}, s32[16,8]{0,1:T(8,128)}, u32[]{:S(2)}) copy-start(s32[16,8]{0,1:T(8,128)} %param.7) | copy-start | bytes 1540
  100.0 27.5 %collective-permute-start.14 = (f32[256,1024]{1,0:T(8,128)}, f32[256,1024]{1,0:T(8,128)}, u32[]{:S(2)}, u32[]{:S(2)}) collective-permute-start(f32[256,1024]{1,0:T(8,128)} %broadcast_select_fusion.refs_8_), channel_id=1, source_target_pairs={{0,16},{1,49},{2,18},{3,51},{4,20},{5,53},{6,22},{7,55},{8,24},{9,... | collective-permute-start | bytes 3145736 | tf_op jit(solution)/shard_map/ppermute | solution.py:30
  100.0 32.5 %collective-permute-start.13 = (f32[256,1024]{1,0:T(8,128)S(1)}, f32[256,1024]{1,0:T(8,128)}, u32[]{:S(2)}, u32[]{:S(2)}) collective-permute-start(f32[256,1024]{1,0:T(8,128)S(1)} %broadcast_select_fusion.1.refs_0_), channel_id=1, source_target_pairs={{0,2},{1,7},{2,0},{3,5},{4,6},{5,3},{6,4},{7,1},{8,10},{9,15},{10,... | collective-permute-start | bytes 3145736 | tf_op jit(solution)/shard_map/ppermute | solution.py:30
  123.9 26.1 %collective-permute-start.20 = (f32[256,1024]{1,0:T(8,128)}, f32[256,1024]{1,0:T(8,128)S(1)}, u32[]{:S(2)}, u32[]{:S(2)}) collective-permute-start(f32[256,1024]{1,0:T(8,128)} %broadcast_select_fusion.refs_8_), channel_id=1, source_target_pairs={{0,48},{1,17},{2,50},{3,19},{4,52},{5,21},{6,54},{7,23},{8,56},{9,... | collective-permute-start | bytes 3145736 | tf_op jit(solution)/shard_map/ppermute | solution.py:30
  127.3 22.3 %collective-permute-start.15 = (f32[256,1024]{1,0:T(8,128)S(1)}, f32[256,1024]{1,0:T(8,128)}, u32[]{:S(2)}, u32[]{:S(2)}) collective-permute-start(f32[256,1024]{1,0:T(8,128)S(1)} %broadcast_select_fusion.1.refs_0_), channel_id=1, source_target_pairs={{0,6},{1,3},{2,4},{3,1},{4,2},{5,7},{6,0},{7,5},{8,14},{9,11},{10,... | collective-permute-start | bytes 3145736 | tf_op jit(solution)/shard_map/ppermute | solution.py:30
  132.5 24.9 %collective-permute-start.18 = (f32[256,1024]{1,0:T(8,128)}, f32[256,1024]{1,0:T(8,128)}, u32[]{:S(2)}, u32[]{:S(2)}) collective-permute-start(f32[256,1024]{1,0:T(8,128)} %collective-permute-done.13.refs_2_), channel_id=1, source_target_pairs={{0,6},{1,3},{2,4},{3,1},{4,2},{5,7},{6,0},{7,5},{8,14},{9,11},{10,... | collective-permute-start | bytes 3145736 | tf_op jit(solution)/shard_map/ppermute | solution.py:30
  136.0 168.2 %collective-permute-start.12 = (f32[256,1024]{1,0:T(8,128)S(1)}, f32[256,1024]{1,0:T(8,128)}, u32[]{:S(2)}, u32[]{:S(2)}) collective-permute-start(f32[256,1024]{1,0:T(8,128)S(1)} %broadcast_select_fusion.1.refs_0_), channel_id=1, source_target_pairs={{0,1},{1,0},{2,3},{3,2},{4,5},{5,4},{6,7},{7,6},{8,9},{9,8},{10,11... | collective-permute-start | bytes 3145736 | tf_op jit(solution)/shard_map/ppermute | solution.py:30
  149.5 154.7 %collective-permute-start.16 = (f32[256,1024]{1,0:T(8,128)}, f32[256,1024]{1,0:T(8,128)}, u32[]{:S(2)}, u32[]{:S(2)}) collective-permute-start(f32[256,1024]{1,0:T(8,128)} %collective-permute-done.13.refs_2_), channel_id=1, source_target_pairs={{0,1},{1,0},{2,3},{3,2},{4,5},{5,4},{6,7},{7,6},{8,9},{9,8},{10,11... | collective-permute-start | bytes 3145736 | tf_op jit(solution)/shard_map/ppermute | solution.py:30
  149.6 154.6 %collective-permute-start.17 = (f32[256,1024]{1,0:T(8,128)}, f32[256,1024]{1,0:T(8,128)}, u32[]{:S(2)}, u32[]{:S(2)}) collective-permute-start(f32[256,1024]{1,0:T(8,128)} %collective-permute-done.15.refs_3_), channel_id=1, source_target_pairs={{0,1},{1,0},{2,3},{3,2},{4,5},{5,4},{6,7},{7,6},{8,9},{9,8},{10,11... | collective-permute-start | bytes 3145736 | tf_op jit(solution)/shard_map/ppermute | solution.py:30
  150.0 9.0 %copy-start.14 = (f32[256,1024]{1,0:T(8,128)}, f32[256,1024]{1,0:T(8,128)S(1)}, u32[]{:S(2)}) copy-start(f32[256,1024]{1,0:T(8,128)S(1)} %collective-permute-done.20.refs_10_) | copy-start | bytes 3145732
  150.0 154.2 %collective-permute-start.21 = (f32[256,1024]{1,0:T(8,128)}, f32[256,1024]{1,0:T(8,128)}, u32[]{:S(2)}, u32[]{:S(2)}) collective-permute-start(f32[256,1024]{1,0:T(8,128)} %collective-permute-done.14.refs_9_), channel_id=1, source_target_pairs={{0,48},{1,17},{2,50},{3,19},{4,52},{5,21},{6,54},{7,23},{8,56},{9,... | collective-permute-start | bytes 3145736 | tf_op jit(solution)/shard_map/ppermute | solution.py:30
  157.4 146.8 %collective-permute-start.19 = (f32[256,1024]{1,0:T(8,128)}, f32[256,1024]{1,0:T(8,128)}, u32[]{:S(2)}, u32[]{:S(2)}) collective-permute-start(f32[256,1024]{1,0:T(8,128)} %collective-permute-done.18.refs_6_), channel_id=1, source_target_pairs={{0,1},{1,0},{2,3},{3,2},{4,5},{5,4},{6,7},{7,6},{8,9},{9,8},{10,11... | collective-permute-start | bytes 3145736 | tf_op jit(solution)/shard_map/ppermute | solution.py:30
  330.8 7.9 %copy-start.1 = (f32[128,1024]{1,0:T(8,128)}, f32[128,1024]{1,0:T(8,128)S(1)}, u32[]{:S(2)}) copy-start(f32[128,1024]{1,0:T(8,128)S(1)} %get-tuple-element.19) | copy-start | bytes 1572868
  330.8 7.8 %slice-start = ((f32[1056,512]{1,0:T(8,128)}), f32[32,512]{1,0:T(8,128)S(1)}, s32[]{:S(2)}) async-start(f32[1056,512]{1,0:T(8,128)} %all-reduce.2.cloned.1.call-done), calls=%async_computation.2 | async-start | bytes 131072 | tf_op jit(solution)/shard_map/slice | solution.py:358
  330.8 7.8 %copy-start.2 = (f32[2,512,512]{2,1,0:T(8,128)S(1)}, f32[2,512,512]{2,1,0:T(8,128)}, u32[]{:S(2)}) copy-start(f32[2,512,512]{2,1,0:T(8,128)} %param.6) | copy-start | bytes 6291460
  330.8 120.2 %all-to-all-start = ((f32[128,128,128]{2,1,0:T(8,128)}), f32[128,128,128]{2,1,0:T(8,128)}, u32[]{:S(2)}, u32[]{:S(2)}) async-start(f32[128,128,128]{2,1,0:T(8,128)} %get-tuple-element.20), calls=%async_computation | async-start | bytes 16777216 | tf_op jit(solution)/shard_map/all_to_all | solution.py:366
  338.6 3.0 copy-start.3
  339.4 111.6 %copy-start = (f32[48,128,128]{2,1,0:T(8,128)S(1)}, f32[48,128,128]{2,1,0:T(8,128)}, u32[]{:S(2)}) copy-start(f32[48,128,128]{2,1,0:T(8,128)} %parent_ref.1) | copy-start | bytes 9437188
Sparse Core Ops, SparseCore 0:
  136.1 164.9 all-reduce.1

commit v3 on v2

--- a/solution.py
+++ b/solution.py
@@ -47,50 +47,53 @@
     return k ^ 1 if first else 3 - k
 
 
-def exchange(columns, rows):
+def exchange(columns, rows, deal, spread_pivot):
     xl, z, xh, y, core = place()
     edge = columns.shape[0] // 8
-    parts = [columns[k * edge : (k + 1) * edge] for k in range(8)]
     lift = rows.shape[0] // 4
+    parts = [columns[2 * k * edge : 2 * (k + 1) * edge] for k in range(4)]
     layers = [rows[k * lift : (k + 1) * lift] for k in range(4)]
 
-    came_columns = {}
-    came_rows = {}
-    for k in (2, 1, 3):
-        for to in range(2):
-            came_columns[2 * k + to] = send(
-                parts[2 * k + to],
-                lambda xl, z, xh, y, core, k=k, to=to: (xl, z, xh, k, to),
-                lambda xl, z, xh, y, core: xh == 0 and y == 0 and core == 0,
-            )
-    for k in (2, 1, 3):
-        came_rows[k] = send(
+    came_columns = [
+        send(
+            parts[k],
+            lambda xl, z, xh, y, core, k=k: (xl, z, xh, k, core),
+            lambda xl, z, xh, y, core: xh == 0 and y == 0 and core == 0,
+        )
+        for k in (1, 2, 3)
+    ]
+    came_rows = [
+        send(
             layers[k],
             lambda xl, z, xh, y, core, k=k: (xl, k, xh, y, core),
             lambda xl, z, xh, y, core: xl == 0 and z == 0,
         )
-    came_columns[1] = send(
-        parts[1],
-        lambda xl, z, xh, y, core: (xl, z, xh, y, 1),
-        lambda xl, z, xh, y, core: xh == 0 and y == 0 and core == 0,
-    )
-    column = choose(2 * y + core, [parts[0]] + [came_columns[k] for k in range(1, 8)])
-    row = choose(z, [layers[0]] + [came_rows[k] for k in range(1, 4)])
-    column, row = lax.optimization_barrier((column, row))
-
-    column_across = send(
-        column,
-        lambda xl, z, xh, y, core: (xl, z, 1, y, core),
-        lambda xl, z, xh, y, core: xh == 0,
-    )
+        for k in (1, 2, 3)
+    ]
+    dealt = lax.all_to_all(deal, AXES, 0, 0, tiled=True)
+    part = [
+        choose(y, [one[k * edge : (k + 1) * edge] for one in [parts[0]] + came_columns])
+        for k in range(2)
+    ]
+    row = choose(z, [layers[0]] + came_rows)
+    part, row, dealt = lax.optimization_barrier((part, row, dealt))
+
     row_across = send(
         row,
         lambda xl, z, xh, y, core: (1, z, xh, y, core),
         lambda xl, z, xh, y, core: xl == 0,
     )
-    column = jnp.where(xh == 0, column, column_across)
+    from_core = lambda xl, z, xh, y, core: xh == 0 and core == 0
+    across = [
+        send(part[k], lambda xl, z, xh, y, core, k=k: (xl, z, 1, y, k), from_core) for k in range(2)
+    ]
+    beside = send(part[1], lambda xl, z, xh, y, core: (xl, z, xh, y, 1), from_core)
+    column = jnp.where(
+        xh == 0, jnp.where(core == 0, part[0], beside), jnp.where(core == 0, across[0], across[1])
+    )
     row = jnp.where(xl == 0, row, row_across)
     column, row = lax.optimization_barrier((column, row))
+    pivot = spread_pivot(dealt)
 
     def around(value, step):
         return send(
@@ -107,11 +110,11 @@
     def swap(value):
         return send(value, lambda xl, z, xh, y, core: (xl, z, xh, y, 1 - core))
 
-    column_a, row_a = around(column, 0), along(row, 0)
-    column_b, row_b = around(column, 1), along(row, 1)
+    row_a, column_a = along(row, 0), around(column, 0)
+    row_b, column_b = along(row, 1), around(column, 1)
     other = swap(column)
-    column_a, row_a = lax.optimization_barrier((column_a, row_a))
-    column_c, row_c = around(column_a, 1), along(row_a, 1)
+    column_a, row_a, pivot = lax.optimization_barrier((column_a, row_a, pivot))
+    row_c, column_c = along(row_a, 1), around(column_a, 1)
     other_a, other_b = swap(column_a), swap(column_b)
     other_c = swap(column_c)
 
@@ -132,7 +135,7 @@
         2 * mine[3] + core,
         2 * theirs[3] + 1 - core,
     ]
-    return pieces, numbers, [row, row_a, row_b, row_c], order(z, core)
+    return pieces, numbers, [row, row_a, row_b, row_c], order(z, core), dealt, pivot
 
 
 def halves(value):
@@ -163,7 +166,7 @@
     slot = lax.rem(step, 2)
     tile = result.shape[1]
     edge = outgoing_ref.shape[1]
-    depth = inverse_ref.shape[0]
+    depth = inverse_ref.shape[1]
     down, across = tile // edge, result.shape[2] // edge
 
     def fetch(number, at):
@@ -201,11 +204,22 @@
         for k in range(4):
             top = pl.multiple_of(table_ref[8 + k] * lift, lift)
             right[pl.ds(top, lift)] = row_refs[k][...]
+        side = pivot_ref.shape[1]
+        pivot = [
+            jnp.concatenate(
+                [
+                    pivot_ref[k * 2 * depth + half * depth : k * 2 * depth + (half + 1) * depth]
+                    for k in range(depth // side)
+                ],
+                axis=1,
+            )
+            for half in range(2)
+        ]
         one = right[:depth]
-        two = right[depth:] - product(pivot_ref[depth:], one)
-        two = product(inverse_ref[...], two)
+        two = right[depth:] - product(pivot[1], one)
+        two = product(inverse_ref[0], two)
         high[depth:], low[depth:] = halves(two)
-        one = one - product(pivot_ref[:depth], two)
+        one = one - product(pivot[0], two)
         high[:depth], low[:depth] = halves(one)
 
     for number in range(8):
@@ -240,8 +254,9 @@
         finish(slot, step)
 
 
-def update(front, block_owner, pivot, inverse, pieces, layers, table, devices, edge):
+def update(front, block_owner, pivot, inverses, pieces, layers, table, devices, edge):
     rows, columns = front.shape
+    depth = inverses.shape[1]
     tile = pieces[0].shape[0]
     whole = lambda *shape: pl.BlockSpec(shape, lambda i, table: (0,) * len(shape))
     return pl.pallas_call(
@@ -253,7 +268,7 @@
                 pl.BlockSpec(memory_space=pltpu.SMEM),
                 pl.BlockSpec((tile, columns), lambda i, table: (table[i], 0)),
                 whole(*pivot.shape),
-                whole(*inverse.shape),
+                pl.BlockSpec((1,) + inverses.shape[1:], lambda i, table: (1, 0, 0)),
             ]
             + [pl.BlockSpec(memory_space=pl.ANY)] * 8
             + [whole(*layers[0].shape)] * 4,
@@ -263,9 +278,9 @@
                 whole(edge, pieces[0].shape[1]),
             ],
             scratch_shapes=[
-                pltpu.VMEM((2 * inverse.shape[0], columns), jnp.float32),
-                pltpu.VMEM((2 * inverse.shape[0], columns), jnp.bfloat16),
-                pltpu.VMEM((2 * inverse.shape[0], columns), jnp.bfloat16),
+                pltpu.VMEM((2 * depth, columns), jnp.float32),
+                pltpu.VMEM((2 * depth, columns), jnp.bfloat16),
+                pltpu.VMEM((2 * depth, columns), jnp.bfloat16),
                 pltpu.VMEM((2, tile, pieces[0].shape[1]), jnp.float32),
                 pltpu.VMEM((2, tile, columns), jnp.float32),
                 pltpu.SemaphoreType.DMA((2,)),
@@ -280,12 +295,12 @@
         ],
         compiler_params=pltpu.CompilerParams(vmem_limit_bytes=44 * MIB),
         cost_estimate=pl.CostEstimate(
-            flops=16 * rows * columns * inverse.shape[0],
+            flops=16 * rows * columns * depth,
             bytes_accessed=40 * MIB,
             transcendentals=0,
         ),
         name="update",
-    )(table, block_owner, front, pivot, inverse, *pieces, *layers)
+    )(table, block_owner, front, pivot, inverses, *pieces, *layers)
 
 
 def add_kernel(slot_ref, parent_ref, arrived_ref, out_ref, sem):
@@ -335,8 +350,7 @@
     width = inverses.shape[1]
     edge = parent_in.shape[1]
     devices = lax.axis_size("row") * lax.axis_size("col")
-    row, col = lax.axis_index("row"), lax.axis_index("col")
-    me = row * lax.axis_size("col") + col
+    col = lax.axis_index("col")
 
     columns = front[:, : 2 * width]
     rows_one = product_rows(inverses[0], front[:width])
@@ -344,29 +358,33 @@
 
     owners = block_owner.reshape(-1)
     slots = block_slot.reshape(-1)
-    names = jnp.arange(devices, dtype=jnp.int32)
-    named = owners[None, :] == names[:, None]
+    named = owners[None, :] == jnp.arange(devices, dtype=jnp.int32)[:, None]
     labels = jnp.sum(jnp.where(named, slots[None, :] + 1, 0), axis=1).astype(jnp.float32)
-    labels = jnp.where(names[None, :] == me, labels[:, None], 0.0)
+    labels = jnp.broadcast_to(labels[:, None, None], (devices, 8, edge))
     pivot = jnp.concatenate(
         [rows_one[:, width : 2 * width], front[width : 2 * width, :width]], axis=0
     )
-    pivot = jnp.where(me == 0, pivot, 0.0)
-    fill = devices * devices // width
-    shared = lax.psum(jnp.concatenate([pivot, labels.reshape(fill, width)], axis=0), AXES)
-    pivot = shared[: 2 * width]
-    markers = shared[2 * width :].reshape(devices, devices)
-    markers = lax.dynamic_slice_in_dim(markers, me, 1, 0).reshape(devices).astype(jnp.int32) - 1
-
-    pieces, numbers, layers, heights = exchange(columns, rows)
+    pivot = pivot.reshape(2 * width, width // edge, edge).transpose(1, 0, 2)
+    pivot = pivot.reshape(devices, -1, edge)
+    deal = jnp.concatenate([pivot, labels], axis=1)
+    share = pivot.shape[1]
+
+    def spread_pivot(dealt):
+        copies = jnp.broadcast_to(dealt[:1, :share], pivot.shape)
+        return lax.all_to_all(copies, AXES, 0, 0, tiled=True).reshape(-1, edge)
+
+    pieces, numbers, layers, heights, dealt, pivot = exchange(columns, rows, deal, spread_pivot)
+    markers = dealt[:, share, 0].astype(jnp.int32) - 1
     table = jnp.stack(numbers + heights + [col // 2, col % 2]).astype(jnp.int32)
     updated, outgoing, mine = update(
-        front, block_owner, pivot, inverses[1], pieces, layers, table, devices, edge
+        front, block_owner, pivot, inverses, pieces, layers, table, devices, edge
     )
     arrived = lax.all_to_all(outgoing, AXES, 0, 0, tiled=True)
 
     mine_one, mine_two = mine[:, :width], mine[:, width:]
-    mine_two = mine_two - exact(mine_one, pivot[:width])
+    corner = pivot.reshape(width // edge, 2 * width, edge)[:, :width]
+    corner = corner.transpose(1, 0, 2).reshape(width, width)
+    mine_two = mine_two - exact(mine_one, corner)
     panels = jnp.concatenate([exact(mine_one, inverses[0]), exact(mine_two, inverses[1])], axis=1)
     parent_out = extend_add(markers, parent_in, arrived)
     return (updated, panels, parent_out)

time: 467 us -> 372 us (0.80)
  waiting for transfers between devices: 306 us -> 175 us
  starting transfers between devices: 74.9 us -> 116 us
  between operations: 14.5 us -> 1.1 us
    psum x1 -> x0, waiting for transfers between devices: 141 us -> none  [local(): lax.psum(jnp.concatenate([pivot, labels.reshape(fill, width)], axis=0), A...]
    all_to_all x0 -> x2, starting transfers between devices: none -> 38.6 us  [the longest x1 25.9 us: spread_pivot(): return lax.all_to_all(copies, AXES, 0, 0, tiled=True).reshape(-1, edge)]
    all_to_all x0 -> x2, waiting for transfers between devices: none -> 21.9 us  [the longest x1 21.9 us: spread_pivot(): return lax.all_to_all(copies, AXES, 0, 0, tiled=True).reshape(-1, edge)]
    all_to_all x1, waiting for transfers between devices: 107 us -> 98.2 us  [local(): arrived = lax.all_to_all(outgoing, AXES, 0, 0, tiled=True)]
    slice x0 -> x1, other arithmetic: none -> 6.72 us  [exchange(): layers = [rows[k * lift:(k + 1) * lift] for k in range(4)]]
    ppermute x22 -> x20, waiting for transfers between devices: 58.3 us -> 55 us  [send(): return lax.ppermute(value, AXES, pairs(move, keep))]
    ppermute x22 -> x20, starting transfers between devices: 67.1 us -> 67.5 us  [send(): return lax.ppermute(value, AXES, pairs(move, keep))]
  transfers between devices with their start and end apart: 24 -> 23, of which waited for: 9 -> 6; matrix products, arithmetic and copies ran while one was open for 6% -> 10% of each run, Pallas kernels for 0% -> 0%
where the time goes in v3:
time: 372 us; the launch traced here: 371 us
  waiting for transfers between devices  175 us (47%)
  starting transfers between devices  116 us (31%)
  Pallas kernels  35.2 us (9%)
  other arithmetic  17.8 us (5%)
  local copies, waits for them, and re-layouts  16.2 us (4%)
  matrix products  8.77 us (2%)
    all_to_all x1, waiting for transfers between devices, local(): arrived = lax.all_to_all(outgoing, AXES, 0, 0, tiled=True)  98.2 us
    ppermute x20, starting transfers between devices, send(): return lax.ppermute(value, AXES, pairs(move, keep))  67.5 us
    ppermute x20, waiting for transfers between devices, send(): return lax.ppermute(value, AXES, pairs(move, keep))  55 us
    pallas_call x1, Pallas kernels, update(): pl.pallas_call(update_kernel, grid_spec=pltpu.PrefetchScalarGridSpec(num_...  27 us
    all_to_all x1, starting transfers between devices, spread_pivot(): return lax.all_to_all(copies, AXES, 0, 0, tiled=True).reshape(-1, edge)  25.9 us
    all_to_all x1, waiting for transfers between devices, spread_pivot(): return lax.all_to_all(copies, AXES, 0, 0, tiled=True).reshape(-1, edge)  21.9 us
    all_to_all x1, starting transfers between devices, exchange(): dealt = lax.all_to_all(deal, AXES, 0, 0, tiled=True)  12.6 us
    all_to_all x1, starting transfers between devices, local(): arrived = lax.all_to_all(outgoing, AXES, 0, 0, tiled=True)  10.5 us
  transfers between devices with their start and end apart: 23, of which 6 were waited for; matrix products, arithmetic and copies ran while one was open for 10% of the time, Pallas kernels for 0%

profile of v3, /device:TPU:1, one launch (start us, length us, event | category | flops | bytes accessed | tf_op | source)
XLA Modules:
  0.0 370.6 jit_solution(12518523937020621434)
XLA Ops:
  0.6 5.9 %fusion.20 = (f32[512,1024]{1,0:T(8,128)}, f32[512,1024]{1,0:T(8,128)}, f32[512,1024]{1,0:T(8,128)}) fusion(f32[2048,1024]{1,0:T(8,128)} %front_ref.1), kind=kLoop, calls=%fused_computation.34 | loop fusion | bytes 12582912 | tf_op jit(solution)/shard_map/slice | solution.py:54
  6.5 2.2 collective-permute-start
  8.7 2.0 collective-permute-start.2
  10.7 2.0 collective-permute-start.1
  12.6 1.3 slice.100
  14.0 0.1 copy.23
  14.0 0.1 add.67
  14.1 0.1 copy.24.owner_ref
  14.2 0.1 eq.68
  14.3 0.1 select_reduce_fusion
  14.4 3.8 %fusion = f32[512,1024]{1,0:T(8,128)S(1)} fusion(f32[2048,1024]{1,0:T(8,128)} %front_ref.1, f32[2,512,512]{2,1,0:T(8,128)} %inverse_ref.1), kind=kOutput, calls=%fused_computation.3 | convolution fusion | flops 1610612736 | bytes 5242880 | tf_op jit(solution)/shard_map/dot_general | solution.py:394
  18.2 0.1 slice.115
  18.3 0.1 copy_bitcast_fusion
  18.4 0.2 broadcast_in_dim.28
  18.6 1.7 pad_maximum_fusion
  20.3 12.6 %all-to-all-start = ((f32[128,40,128]{2,1,0:T(8,128)}), f32[128,40,128]{2,1,0:T(8,128)}, u32[]{:S(2)}, u32[]{:S(2)}) async-start(f32[128,40,128]{2,1,0:T(8,128)} %pad_maximum_fusion), calls=%async_computation | async-start | bytes 5242880 | tf_op jit(solution)/shard_map/all_to_all | solution.py:73
  32.9 1.1 slice.114
  34.0 4.4 %collective-permute-start.3 = (f32[256,1024]{1,0:T(8,128)}, f32[256,1024]{1,0:T(8,128)}, u32[]{:S(2)}, u32[]{:S(2)}) collective-permute-start(f32[256,1024]{1,0:T(8,128)} %slice.114), channel_id=1, source_target_pairs={{0,16},{1,17},{2,18},{3,19},{4,20},{5,21},{6,22},{7,23},{8,24},{9,... | collective-permute-start | bytes 3145736 | tf_op jit(solution)/shard_map/ppermute | solution.py:30
  38.4 0.0 collective-permute-done.1
  38.4 6.7 %fusion.19 = (f32[256,1024]{1,0:T(8,128)}, f32[256,1024]{1,0:T(8,128)}, f32[256,1024]{1,0:T(8,128)S(1)}, f32[256,1024]{1,0:T(8,128)}) fusion(f32[2048,1024]{1,0:T(8,128)} %front_ref.1, f32[512,1024]{1,0:T(8,128)} %collective-permute-done.2, f32[512,1024]{1,0:T(8,128)} %collective-permute-done.1, pred[]{:T(512)S(6)} %eq.64, ...), kind=kLoop, calls=%fused_computation.33 | loop fusion | flops 1572864 | bytes 14680067 | tf_op jit(solution)/shard_map/slice | solution.py:55
  45.1 3.4 collective-permute-start.5
  48.5 2.3 collective-permute-start.4
  50.9 33.1 %collective-permute-done.3 = f32[256,1024]{1,0:T(8,128)} collective-permute-done((f32[256,1024]{1,0:T(8,128)}, f32[256,1024]{1,0:T(8,128)}, u32[]{:S(2)}, u32[]{:S(2)}) %collective-permute-start.3) | collective-permute-done | bytes 1048608 | tf_op jit(solution)/shard_map/ppermute | solution.py:30
  83.9 0.0 collective-permute-done.5
  83.9 11.4 %collective-permute-done.4 = f32[256,1024]{1,0:T(8,128)} collective-permute-done((f32[256,1024]{1,0:T(8,128)}, f32[256,1024]{1,0:T(8,128)}, u32[]{:S(2)}, u32[]{:S(2)}) %collective-permute-start.4) | collective-permute-done | bytes 1048608 | tf_op jit(solution)/shard_map/ppermute | solution.py:30
  95.3 2.6 slice_select_fusion
  98.0 0.0 all-to-all-done
  98.0 2.2 collective-permute-start.9
  100.2 1.6 collective-permute-start.7
  101.9 1.6 collective-permute-start.8
  103.5 1.3 collective-permute-start.6
  104.8 0.7 slice_bitcast_fusion
  105.5 1.6 broadcast_in_dim.30
  107.1 25.9 %all-to-all-start.1 = ((f32[128,32,128]{2,1,0:T(8,128)}), f32[128,32,128]{2,1,0:T(8,128)}, u32[]{:S(2)}, u32[]{:S(2)}) async-start(f32[128,32,128]{2,1,0:T(8,128)} %broadcast_in_dim.30), calls=%async_computation.1 | async-start | bytes 4194304 | tf_op jit(solution)/shard_map/all_to_all | solution.py:374
  133.1 0.0 collective-permute-done.9
  133.1 0.2 broadcast_select_fusion.refs_8_
  133.3 0.0 collective-permute-done.7
  133.3 0.0 collective-permute-done.8
  133.3 0.0 collective-permute-done.6
  133.4 2.0 select_select_fusion.refs_0_
  135.4 3.3 collective-permute-start.11
  138.7 2.6 collective-permute-start.10
  141.3 21.9 %all-to-all-done.1 = f32[128,32,128]{2,1,0:T(8,128)} async-done(((f32[128,32,128]{2,1,0:T(8,128)}), f32[128,32,128]{2,1,0:T(8,128)}, u32[]{:S(2)}, u32[]{:S(2)}) %all-to-all-start.1) | async-done | bytes 2097184 | tf_op jit(solution)/shard_map/all_to_all | solution.py:374
  163.2 7.4 %collective-permute-done.11.refs_9_ = f32[256,1024]{1,0:T(8,128)} collective-permute-done((f32[256,1024]{1,0:T(8,128)S(1)}, f32[256,1024]{1,0:T(8,128)}, u32[]{:S(2)}, u32[]{:S(2)}) %collective-permute-start.11) | collective-permute-done | bytes 1048608 | tf_op jit(solution)/shard_map/ppermute | solution.py:30
  170.6 0.6 collective-permute-start.16
  171.1 24.9 %collective-permute-start.12 = (f32[256,1024]{1,0:T(8,128)S(1)}, f32[256,1024]{1,0:T(8,128)}, u32[]{:S(2)}, u32[]{:S(2)}) collective-permute-start(f32[256,1024]{1,0:T(8,128)S(1)} %select_select_fusion.refs_0_), channel_id=1, source_target_pairs={{0,1},{1,0},{2,3},{3,2},{4,5},{5,4},{6,7},{7,6},{8,9},{9,8},{10,11... | collective-permute-start | bytes 3145736 | tf_op jit(solution)/shard_map/ppermute | solution.py:30
  196.0 0.5 collective-permute-start.15
  196.5 3.0 collective-permute-start.19
  199.5 9.6 %collective-permute-start.17 = (f32[256,1024]{1,0:T(8,128)}, f32[256,1024]{1,0:T(8,128)}, u32[]{:S(2)}, u32[]{:S(2)}) collective-permute-start(f32[256,1024]{1,0:T(8,128)} %collective-permute-done.16.refs_6_), channel_id=1, source_target_pairs={{0,1},{1,0},{2,3},{3,2},{4,5},{5,4},{6,7},{7,6},{8,9},{9,8},{10,11... | collective-permute-start | bytes 3145736 | tf_op jit(solution)/shard_map/ppermute | solution.py:30
  209.1 0.1 stack.59.table_ref
  209.2 3.1 collective-permute-done.19.refs_11_
  212.3 27.0 %update.1 = (f32[2048,1024]{1,0:T(8,128)}, f32[128,128,128]{2,1,0:T(8,128)}, f32[128,1024]{1,0:T(8,128)S(1)}) custom-call(s32[14]{0:T(128)S(1)} %stack.59.table_ref, s32[16,8]{1,0:T(8,128)S(1)} %copy.24.owner_ref, f32[2048,1024]{1,0:T(8,128)} %front_ref.1, f32[4096,128]{1,0:T(8,128)} %bitcast.18.pivot_ref, f32[2,512,512]{2,1,0:T(8,128)} %inverse_ref.1, ...), custom_call_target="tpu_custom_call" | custom-call | flops 17179869184 | bytes 41943040 | tf_op jit(solution)/shard_map/update/pallas_call | solution.py:262
  239.3 0.0 copy-start.1
  239.3 10.5 %all-to-all-start.2 = ((f32[128,128,128]{2,1,0:T(8,128)}), f32[128,128,128]{2,1,0:T(8,128)}, u32[]{:S(2)}, u32[]{:S(2)}) async-start(f32[128,128,128]{2,1,0:T(8,128)} %get-tuple-element.26), calls=%async_computation.2 | async-start | bytes 16777216 | tf_op jit(solution)/shard_map/all_to_all | solution.py:382
  249.8 3.4 add_reduce_fusion.slot_ref
  253.2 2.4 slice.116
  255.6 2.5 copy.26
  258.1 0.7 fusion.8
  258.8 0.0 copy-start
  258.9 2.6 fusion.16
  261.5 1.7 fusion.6
  263.2 0.8 pad_maximum_fusion.1
  264.0 98.2 %all-to-all-done.2.arrived_ref = f32[128,128,128]{2,1,0:T(8,128)} async-done(((f32[128,128,128]{2,1,0:T(8,128)}), f32[128,128,128]{2,1,0:T(8,128)}, u32[]{:S(2)}, u32[]{:S(2)}) %all-to-all-start.2) | async-done | bytes 8388640 | tf_op jit(solution)/shard_map/all_to_all | solution.py:382
  362.2 8.2 %extend_add.1 = f32[48,128,128]{2,1,0:T(8,128)} custom-call(s32[128]{0:T(128)S(1)} %add_reduce_fusion.slot_ref, f32[48,128,128]{2,1,0:T(8,128)S(1)} %copy-done, f32[128,128,128]{2,1,0:T(8,128)} %all-to-all-done.2.arrived_ref), custom_call_target="tpu_custom_call" | custom-call | flops 2097152 | bytes 14680064 | tf_op jit(solution)/shard_map/extend_add/pallas_call | solution.py:328
  (29 shorter events, 0.1 us)
Async XLA Ops:
  6.5 7.4 %copy-start.6 = (s32[16,8]{0,1:T(8,128)S(1)}, s32[16,8]{0,1:T(8,128)}, u32[]{:S(2)}) copy-start(s32[16,8]{0,1:T(8,128)} %param.8) | copy-start | bytes 1540
  6.5 7.6 %copy-start.5 = (s32[16,8]{0,1:T(8,128)S(1)}, s32[16,8]{0,1:T(8,128)}, u32[]{:S(2)}) copy-start(s32[16,8]{0,1:T(8,128)} %param.7) | copy-start | bytes 1540
  6.5 31.9 %collective-permute-start = (f32[512,1024]{1,0:T(8,128)}, f32[512,1024]{1,0:T(8,128)}, u32[]{:S(2)}, u32[]{:S(2)}) collective-permute-start(f32[512,1024]{1,0:T(8,128)} %get-tuple-element.33), channel_id=1, source_target_pairs={{0,2},{16,18},{32,34},{48,50},{64,66},{80,82},{96,98},{112,114}} | collective-permute-start | bytes 6291464 | tf_op jit(solution)/shard_map/ppermute | solution.py:30
  8.7 29.7 %collective-permute-start.2 = (f32[512,1024]{1,0:T(8,128)}, f32[512,1024]{1,0:T(8,128)}, u32[]{:S(2)}, u32[]{:S(2)}) collective-permute-start(f32[512,1024]{1,0:T(8,128)} %get-tuple-element.34), channel_id=1, source_target_pairs={{0,6},{16,22},{32,38},{48,54},{64,70},{80,86},{96,102},{112,118}} | collective-permute-start | bytes 6291464 | tf_op jit(solution)/shard_map/ppermute | solution.py:30
  10.7 27.7 %collective-permute-start.1 = (f32[512,1024]{1,0:T(8,128)}, f32[512,1024]{1,0:T(8,128)}, u32[]{:S(2)}, u32[]{:S(2)}) collective-permute-start(f32[512,1024]{1,0:T(8,128)} %get-tuple-element.35), channel_id=1, source_target_pairs={{0,4},{16,20},{32,36},{48,52},{64,68},{80,84},{96,100},{112,116}} | collective-permute-start | bytes 6291464 | tf_op jit(solution)/shard_map/ppermute | solution.py:30
  20.3 77.7 %all-to-all-start = ((f32[128,40,128]{2,1,0:T(8,128)}), f32[128,40,128]{2,1,0:T(8,128)}, u32[]{:S(2)}, u32[]{:S(2)}) async-start(f32[128,40,128]{2,1,0:T(8,128)} %pad_maximum_fusion), calls=%async_computation | async-start | bytes 5242880 | tf_op jit(solution)/shard_map/all_to_all | solution.py:73
  34.0 49.9 %collective-permute-start.3 = (f32[256,1024]{1,0:T(8,128)}, f32[256,1024]{1,0:T(8,128)}, u32[]{:S(2)}, u32[]{:S(2)}) collective-permute-start(f32[256,1024]{1,0:T(8,128)} %slice.114), channel_id=1, source_target_pairs={{0,16},{1,17},{2,18},{3,19},{4,20},{5,21},{6,22},{7,23},{8,24},{9,... | collective-permute-start | bytes 3145736 | tf_op jit(solution)/shard_map/ppermute | solution.py:30
  45.1 38.8 %collective-permute-start.5 = (f32[256,1024]{1,0:T(8,128)}, f32[256,1024]{1,0:T(8,128)}, u32[]{:S(2)}, u32[]{:S(2)}) collective-permute-start(f32[256,1024]{1,0:T(8,128)} %get-tuple-element.29), channel_id=1, source_target_pairs={{0,48},{1,49},{2,50},{3,51},{4,52},{5,53},{6,54},{7,55},{8,56},{9,... | collective-permute-start | bytes 3145736 | tf_op jit(solution)/shard_map/ppermute | solution.py:30
  48.5 46.8 %collective-permute-start.4 = (f32[256,1024]{1,0:T(8,128)}, f32[256,1024]{1,0:T(8,128)}, u32[]{:S(2)}, u32[]{:S(2)}) collective-permute-start(f32[256,1024]{1,0:T(8,128)} %get-tuple-element.30), channel_id=1, source_target_pairs={{0,32},{1,33},{2,34},{3,35},{4,36},{5,37},{6,38},{7,39},{8,40},{9,... | collective-permute-start | bytes 3145736 | tf_op jit(solution)/shard_map/ppermute | solution.py:30
  98.0 35.1 %collective-permute-start.9 = (f32[256,1024]{1,0:T(8,128)}, f32[256,1024]{1,0:T(8,128)}, u32[]{:S(2)}, u32[]{:S(2)}) collective-permute-start(f32[256,1024]{1,0:T(8,128)} %slice_select_fusion), channel_id=1, source_target_pairs={{0,64},{1,65},{2,66},{3,67},{4,68},{5,69},{6,70},{7,71},{8,72},{9,... | collective-permute-start | bytes 3145736 | tf_op jit(solution)/shard_map/ppermute | solution.py:30
  100.2 33.1 %collective-permute-start.7 = (f32[256,1024]{1,0:T(8,128)S(1)}, f32[256,1024]{1,0:T(8,128)}, u32[]{:S(2)}, u32[]{:S(2)}) collective-permute-start(f32[256,1024]{1,0:T(8,128)S(1)} %get-tuple-element.15), channel_id=1, source_target_pairs={{0,8},{2,10},{4,12},{6,14},{16,24},{18,26},{20,28},{22,30},{32,40}... | collective-permute-start | bytes 3145736 | tf_op jit(solution)/shard_map/ppermute | solution.py:30
  101.9 31.5 %collective-permute-start.8 = (f32[256,1024]{1,0:T(8,128)}, f32[256,1024]{1,0:T(8,128)}, u32[]{:S(2)}, u32[]{:S(2)}) collective-permute-start(f32[256,1024]{1,0:T(8,128)} %get-tuple-element.16), channel_id=1, source_target_pairs={{0,9},{2,11},{4,13},{6,15},{16,25},{18,27},{20,29},{22,31},{32,41}... | collective-permute-start | bytes 3145736 | tf_op jit(solution)/shard_map/ppermute | solution.py:30
  103.5 29.9 %collective-permute-start.6 = (f32[256,1024]{1,0:T(8,128)}, f32[256,1024]{1,0:T(8,128)}, u32[]{:S(2)}, u32[]{:S(2)}) collective-permute-start(f32[256,1024]{1,0:T(8,128)} %get-tuple-element.16), channel_id=1, source_target_pairs={{0,1},{2,3},{4,5},{6,7},{16,17},{18,19},{20,21},{22,23},{32,33},{3... | collective-permute-start | bytes 3145736 | tf_op jit(solution)/shard_map/ppermute | solution.py:30
  107.1 26.0 %copy-start.4 = (f32[256,1024]{1,0:T(8,128)S(1)}, f32[256,1024]{1,0:T(8,128)}, u32[]{:S(2)}) copy-start(f32[256,1024]{1,0:T(8,128)} %slice_select_fusion) | copy-start | bytes 3145732
  107.1 56.1 %all-to-all-start.1 = ((f32[128,32,128]{2,1,0:T(8,128)}), f32[128,32,128]{2,1,0:T(8,128)}, u32[]{:S(2)}, u32[]{:S(2)}) async-start(f32[128,32,128]{2,1,0:T(8,128)} %broadcast_in_dim.30), calls=%async_computation.1 | async-start | bytes 4194304 | tf_op jit(solution)/shard_map/all_to_all | solution.py:374
  135.4 35.2 %collective-permute-start.11 = (f32[256,1024]{1,0:T(8,128)S(1)}, f32[256,1024]{1,0:T(8,128)}, u32[]{:S(2)}, u32[]{:S(2)}) collective-permute-start(f32[256,1024]{1,0:T(8,128)S(1)} %broadcast_select_fusion.refs_8_), channel_id=1, source_target_pairs={{0,16},{1,49},{2,18},{3,51},{4,20},{5,53},{6,22},{7,55},{8,24},{9,... | collective-permute-start | bytes 3145736 | tf_op jit(solution)/shard_map/ppermute | solution.py:30
  138.7 31.9 %collective-permute-start.10 = (f32[256,1024]{1,0:T(8,128)S(1)}, f32[256,1024]{1,0:T(8,128)}, u32[]{:S(2)}, u32[]{:S(2)}) collective-permute-start(f32[256,1024]{1,0:T(8,128)S(1)} %select_select_fusion.refs_0_), channel_id=1, source_target_pairs={{0,2},{1,7},{2,0},{3,5},{4,6},{5,3},{6,4},{7,1},{8,10},{9,15},{10,... | collective-permute-start | bytes 3145736 | tf_op jit(solution)/shard_map/ppermute | solution.py:30
  141.3 55.2 %collective-permute-start.18 = (f32[256,1024]{1,0:T(8,128)S(1)}, f32[256,1024]{1,0:T(8,128)S(1)}, u32[]{:S(2)}, u32[]{:S(2)}) collective-permute-start(f32[256,1024]{1,0:T(8,128)S(1)} %broadcast_select_fusion.refs_8_), channel_id=1, source_target_pairs={{0,48},{1,17},{2,50},{3,19},{4,52},{5,21},{6,54},{7,23},{8,56},{9,... | collective-permute-start | bytes 3145736 | tf_op jit(solution)/shard_map/ppermute | solution.py:30
  141.3 54.7 %collective-permute-start.13 = (f32[256,1024]{1,0:T(8,128)S(1)}, f32[256,1024]{1,0:T(8,128)}, u32[]{:S(2)}, u32[]{:S(2)}) collective-permute-start(f32[256,1024]{1,0:T(8,128)S(1)} %select_select_fusion.refs_0_), channel_id=1, source_target_pairs={{0,6},{1,3},{2,4},{3,1},{4,2},{5,7},{6,0},{7,5},{8,14},{9,11},{10,... | collective-permute-start | bytes 3145736 | tf_op jit(solution)/shard_map/ppermute | solution.py:30
  170.6 28.9 %collective-permute-start.16 = (f32[256,1024]{1,0:T(8,128)}, f32[256,1024]{1,0:T(8,128)}, u32[]{:S(2)}, u32[]{:S(2)}) collective-permute-start(f32[256,1024]{1,0:T(8,128)} %collective-permute-done.10.refs_2_), channel_id=1, source_target_pairs={{0,6},{1,3},{2,4},{3,1},{4,2},{5,7},{6,0},{7,5},{8,14},{9,11},{10,... | collective-permute-start | bytes 3145736 | tf_op jit(solution)/shard_map/ppermute | solution.py:30
  171.1 38.0 %collective-permute-start.12 = (f32[256,1024]{1,0:T(8,128)S(1)}, f32[256,1024]{1,0:T(8,128)}, u32[]{:S(2)}, u32[]{:S(2)}) collective-permute-start(f32[256,1024]{1,0:T(8,128)S(1)} %select_select_fusion.refs_0_), channel_id=1, source_target_pairs={{0,1},{1,0},{2,3},{3,2},{4,5},{5,4},{6,7},{7,6},{8,9},{9,8},{10,11... | collective-permute-start | bytes 3145736 | tf_op jit(solution)/shard_map/ppermute | solution.py:30
  196.0 16.3 %collective-permute-start.14 = (f32[256,1024]{1,0:T(8,128)}, f32[256,1024]{1,0:T(8,128)}, u32[]{:S(2)}, u32[]{:S(2)}) collective-permute-start(f32[256,1024]{1,0:T(8,128)} %collective-permute-done.10.refs_2_), channel_id=1, source_target_pairs={{0,1},{1,0},{2,3},{3,2},{4,5},{5,4},{6,7},{7,6},{8,9},{9,8},{10,11... | collective-permute-start | bytes 3145736 | tf_op jit(solution)/shard_map/ppermute | solution.py:30
  196.0 13.2 %collective-permute-start.15 = (f32[256,1024]{1,0:T(8,128)}, f32[256,1024]{1,0:T(8,128)}, u32[]{:S(2)}, u32[]{:S(2)}) collective-permute-start(f32[256,1024]{1,0:T(8,128)} %collective-permute-done.13.refs_3_), channel_id=1, source_target_pairs={{0,1},{1,0},{2,3},{3,2},{4,5},{5,4},{6,7},{7,6},{8,9},{9,8},{10,11... | collective-permute-start | bytes 3145736 | tf_op jit(solution)/shard_map/ppermute | solution.py:30
  196.5 12.6 %copy-start.7 = (f32[256,1024]{1,0:T(8,128)}, f32[256,1024]{1,0:T(8,128)S(1)}, u32[]{:S(2)}) copy-start(f32[256,1024]{1,0:T(8,128)S(1)} %collective-permute-done.18.refs_10_) | copy-start | bytes 3145732
  196.5 15.8 %collective-permute-start.19 = (f32[256,1024]{1,0:T(8,128)}, f32[256,1024]{1,0:T(8,128)}, u32[]{:S(2)}, u32[]{:S(2)}) collective-permute-start(f32[256,1024]{1,0:T(8,128)} %collective-permute-done.11.refs_9_), channel_id=1, source_target_pairs={{0,48},{1,17},{2,50},{3,19},{4,52},{5,21},{6,54},{7,23},{8,56},{9,... | collective-permute-start | bytes 3145736 | tf_op jit(solution)/shard_map/ppermute | solution.py:30
  199.5 12.8 %collective-permute-start.17 = (f32[256,1024]{1,0:T(8,128)}, f32[256,1024]{1,0:T(8,128)}, u32[]{:S(2)}, u32[]{:S(2)}) collective-permute-start(f32[256,1024]{1,0:T(8,128)} %collective-permute-done.16.refs_6_), channel_id=1, source_target_pairs={{0,1},{1,0},{2,3},{3,2},{4,5},{5,4},{6,7},{7,6},{8,9},{9,8},{10,11... | collective-permute-start | bytes 3145736 | tf_op jit(solution)/shard_map/ppermute | solution.py:30
  239.3 18.8 %copy-start.1 = (f32[128,1024]{1,0:T(8,128)}, f32[128,1024]{1,0:T(8,128)S(1)}, u32[]{:S(2)}) copy-start(f32[128,1024]{1,0:T(8,128)S(1)} %get-tuple-element.25) | copy-start | bytes 1572868
  239.3 122.9 %all-to-all-start.2 = ((f32[128,128,128]{2,1,0:T(8,128)}), f32[128,128,128]{2,1,0:T(8,128)}, u32[]{:S(2)}, u32[]{:S(2)}) async-start(f32[128,128,128]{2,1,0:T(8,128)} %get-tuple-element.26), calls=%async_computation.2 | async-start | bytes 16777216 | tf_op jit(solution)/shard_map/all_to_all | solution.py:382
  253.2 5.0 %copy-start.2 = (f32[2,512,512]{2,1,0:T(8,128)S(1)}, f32[2,512,512]{2,1,0:T(8,128)}, u32[]{:S(2)}) copy-start(f32[2,512,512]{2,1,0:T(8,128)} %inverse_ref.1) | copy-start | bytes 6291460
  258.1 3.4 copy-start.3
  258.8 103.3 %copy-start = (f32[48,128,128]{2,1,0:T(8,128)S(1)}, f32[48,128,128]{2,1,0:T(8,128)}, u32[]{:S(2)}) copy-start(f32[48,128,128]{2,1,0:T(8,128)} %parent_ref.1) | copy-start | bytes 9437188

commit v4 on v2

--- a/solution.py
+++ b/solution.py
@@ -36,47 +36,103 @@
     return row // 4, row % 4, col // 8, (col // 2) % 4, col % 2
 
 
-def choose(index, options):
-    value = options[-1]
-    for number in range(len(options) - 2, -1, -1):
-        value = jnp.where(index == number, options[number], value)
-    return value
-
-
 def partner(k, first):
     return k ^ 1 if first else 3 - k
 
 
-def exchange(columns, rows):
+STEPS = ("z0", "z1", "y0", "y1", "xl", "xh")
+
+
+def moved(spot, step):
+    xl, z, xh, y = spot
+    if step[0] == "z":
+        return (xl, partner(z, step == "z0"), xh, y)
+    if step[0] == "y":
+        return (xl, z, xh, partner(y, step == "y0"))
+    return (1 - xl, z, xh, y) if step == "xl" else (xl, z, 1 - xh, y)
+
+
+def doubling():
+    orders = (STEPS, STEPS[2:4] + STEPS[:2] + ("xh", "xl"))
+    having = [{(0, 0, 0, 0)}, {(0, 0, 0, 0)}]
+    rounds = []
+    for number in range(6):
+        listed = []
+        for core in range(2):
+            new = {moved(spot, orders[core][number]): spot for spot in sorted(having[core])}
+            for to, start in new.items():
+                listed.append((device(*start, core), device(*to, core)))
+            having[core] = having[core] | set(new)
+        rounds.append(listed)
+    return rounds
+
+
+def exchange(columns, rows, pivot_one, pivot_two, labels):
     xl, z, xh, y, core = place()
+    first = core == 0
     edge = columns.shape[0] // 8
-    parts = [columns[k * edge : (k + 1) * edge] for k in range(8)]
     lift = rows.shape[0] // 4
-    layers = [rows[k * lift : (k + 1) * lift] for k in range(4)]
-
-    came_columns = {}
-    came_rows = {}
-    for k in (2, 1, 3):
-        for to in range(2):
-            came_columns[2 * k + to] = send(
-                parts[2 * k + to],
-                lambda xl, z, xh, y, core, k=k, to=to: (xl, z, xh, k, to),
-                lambda xl, z, xh, y, core: xh == 0 and y == 0 and core == 0,
-            )
-    for k in (2, 1, 3):
-        came_rows[k] = send(
-            layers[k],
-            lambda xl, z, xh, y, core, k=k: (xl, k, xh, y, core),
-            lambda xl, z, xh, y, core: xl == 0 and z == 0,
-        )
-    came_columns[1] = send(
-        parts[1],
-        lambda xl, z, xh, y, core: (xl, z, xh, y, 1),
-        lambda xl, z, xh, y, core: xh == 0 and y == 0 and core == 0,
-    )
-    column = choose(2 * y + core, [parts[0]] + [came_columns[k] for k in range(1, 8)])
-    row = choose(z, [layers[0]] + [came_rows[k] for k in range(1, 4)])
-    column, row = lax.optimization_barrier((column, row))
+    part = lambda k, count=1: columns[k * edge : (k + count) * edge]
+    layer = lambda k, count=1: rows[k * lift : (k + count) * lift]
+    rounds = doubling()
+    corner = ((xl == 0) & (z == 0)) & ((xh == 0) & (y == 0))
+
+    def swap(value):
+        return send(value, lambda xl, z, xh, y, core: (xl, z, xh, y, 1 - core))
+
+    def spread(value, number):
+        return value + lax.ppermute(value, AXES, rounds[number])
+
+    source = lambda xl, z, xh, y, core: xh == 0 and y == 0 and core == 0
+
+    one = send(part(1, 2), lambda xl, z, xh, y, core: (xl, z, xh, 1, 0), source)
+    two = send(part(6, 2), lambda xl, z, xh, y, core: (xl, z, xh, 3, 1), source)
+    low = send(
+        jnp.where(first, layer(1, 2), layer(2, 2)),
+        lambda xl, z, xh, y, core: (xl, partner(z, core == 0), xh, y, core),
+        lambda xl, z, xh, y, core: xl == 0 and z == 0,
+    )
+    beside = lax.ppermute(pivot_two, AXES, [(0, 1)])
+    pivot = jnp.where(corner & first, pivot_one, beside)
+    pivot = spread(pivot, 0)
+    one, two, low, pivot = lax.optimization_barrier((one, two, low, pivot))
+
+    three = send(
+        jnp.where(y == 0, part(3), one[edge:]),
+        lambda xl, z, xh, y, core: (xl, z, xh, 3 - y, 0),
+        lambda xl, z, xh, y, core: xh == 0 and core == 0 and y in (0, 1),
+    )
+    four = send(
+        jnp.where(y == 0, part(5), two[:edge]),
+        lambda xl, z, xh, y, core: (xl, z, xh, y ^ 1, 1),
+        lambda xl, z, xh, y, core: xh == 0 and ((core == 0 and y == 0) or (core == 1 and y == 3)),
+    )
+    high = send(
+        jnp.where(
+            z == 0,
+            jnp.where(first, layer(3), layer(1)),
+            jnp.where(first, low[lift:], low[:lift]),
+        ),
+        lambda xl, z, xh, y, core: (xl, partner(z, core == 1), xh, y, core),
+        lambda xl, z, xh, y, core: xl == 0 and z in ((0, 1) if core == 0 else (0, 3)),
+    )
+    five = send(part(4), lambda xl, z, xh, y, core: (xl, z, xh, y, 1), source)
+    pivot = spread(pivot, 1)
+    column = jnp.where(
+        first,
+        jnp.where(y == 0, part(0), jnp.where(y == 1, one[:edge], three)),
+        jnp.where(y == 0, five, jnp.where(y == 3, two[edge:], four)),
+    )
+    row = jnp.where(
+        z == 0,
+        layer(0),
+        jnp.where(
+            first & (z == 1),
+            low[:lift],
+            jnp.where((core == 1) & (z == 3), low[lift:], high),
+        ),
+    )
+    column, row, pivot, labels = lax.optimization_barrier((column, row, pivot, labels))
 
     column_across = send(
         column,
@@ -88,9 +144,12 @@
         lambda xl, z, xh, y, core: (1, z, xh, y, core),
         lambda xl, z, xh, y, core: xl == 0,
     )
+    pivot = spread(pivot, 2)
+    labels = lax.all_to_all(labels, AXES, 0, 0, tiled=True)
+    pivot = spread(pivot, 3)
     column = jnp.where(xh == 0, column, column_across)
     row = jnp.where(xl == 0, row, row_across)
-    column, row = lax.optimization_barrier((column, row))
+    column, row, pivot = lax.optimization_barrier((column, row, pivot))
 
     def around(value, step):
         return send(
@@ -104,14 +163,14 @@
             lambda xl, z, xh, y, core: (xl, partner(z, (core == 0) == (step == 0)), xh, y, core),
         )
 
-    def swap(value):
-        return send(value, lambda xl, z, xh, y, core: (xl, z, xh, y, 1 - core))
-
-    column_a, row_a = around(column, 0), along(row, 0)
-    column_b, row_b = around(column, 1), along(row, 1)
+    row_a, column_a = along(row, 0), around(column, 0)
+    row_b, column_b = along(row, 1), around(column, 1)
+    pivot = spread(pivot, 4)
     other = swap(column)
-    column_a, row_a = lax.optimization_barrier((column_a, row_a))
-    column_c, row_c = around(column_a, 1), along(row_a, 1)
+    pivot = spread(pivot, 5)
+    column_a, row_a, pivot = lax.optimization_barrier((column_a, row_a, pivot))
+    row_c, column_c = along(row_a, 1), around(column_a, 1)
+    pivots = (pivot, swap(pivot))
     other_a, other_b = swap(column_a), swap(column_b)
     other_c = swap(column_c)
 
@@ -121,18 +180,10 @@
         return [k, one, two, 3 - (k ^ 1)]
 
     pieces = [column, other, column_a, column_b, other_a, other_b, column_c, other_c]
-    mine, theirs = order(y, core), order(y, 1 - core)
-    numbers = [
-        2 * mine[0] + core,
-        2 * theirs[0] + 1 - core,
-        2 * mine[1] + core,
-        2 * mine[2] + core,
-        2 * theirs[1] + 1 - core,
-        2 * theirs[2] + 1 - core,
-        2 * mine[3] + core,
-        2 * theirs[3] + 1 - core,
-    ]
-    return pieces, numbers, [row, row_a, row_b, row_c], order(z, core)
+    mine = [4 * core + k for k in order(y, core)]
+    theirs = [4 * (1 - core) + k for k in order(y, 1 - core)]
+    numbers = [mine[0], theirs[0], mine[1], mine[2], theirs[1], theirs[2], mine[3], theirs[3]]
+    return pieces, numbers, [row, row_a, row_b, row_c], order(z, core), pivots, labels
 
 
 def halves(value):
@@ -151,19 +202,64 @@
     return dot(left_high, right_low) + dot(left_low, right_high) + dot(left_high, right_high)
 
 
+def fold_kernel(table_ref, pivot_ref, other_ref, inverse_ref, *refs):
+    row_refs = refs[:4]
+    high, low, right = refs[4:]
+    depth = inverse_ref.shape[1]
+    lift = row_refs[0].shape[0]
+    for k in range(4):
+        top = pl.multiple_of(table_ref[8 + k] * lift, lift)
+        right[pl.ds(top, lift)] = row_refs[k][...]
+    first = table_ref[14] == 0
+    pivot_one = jnp.where(first, pivot_ref[...], other_ref[...])
+    pivot_two = jnp.where(first, other_ref[...], pivot_ref[...])
+    one = right[:depth]
+    two = right[depth:] - product(pivot_two, one)
+    two = product(inverse_ref[0], two)
+    high[depth:], low[depth:] = halves(two)
+    one = one - product(pivot_one, two)
+    high[:depth], low[:depth] = halves(one)
+
+
+def fold(table, pivots, inverses, layers):
+    depth = inverses.shape[1]
+    columns = layers[0].shape[1]
+    whole = lambda *shape: pl.BlockSpec(shape, lambda i, table: (0,) * len(shape))
+    half = jax.ShapeDtypeStruct((2 * depth, columns), jnp.bfloat16)
+    return pl.pallas_call(
+        fold_kernel,
+        grid_spec=pltpu.PrefetchScalarGridSpec(
+            num_scalar_prefetch=1,
+            grid=(1,),
+            in_specs=[
+                whole(depth, depth),
+                whole(depth, depth),
+                pl.BlockSpec((1, depth, depth), lambda i, table: (1, 0, 0)),
+            ]
+            + [whole(*layers[0].shape)] * 4,
+            out_specs=[whole(2 * depth, columns)] * 2,
+            scratch_shapes=[pltpu.VMEM((2 * depth, columns), jnp.float32)],
+        ),
+        out_shape=[half, half],
+        compiler_params=pltpu.CompilerParams(vmem_limit_bytes=44 * MIB),
+        cost_estimate=pl.CostEstimate(
+            flops=18 * depth * depth * columns, bytes_accessed=12 * MIB, transcendentals=0
+        ),
+        name="fold",
+    )(table, *pivots, inverses, *layers)
+
+
 def update_kernel(
-    table_ref, owner_ref, front_ref, pivot_ref, inverse_ref, *refs
+    table_ref, owner_ref, front_ref, high, low, *refs
 ):
     column_refs = refs[:8]
-    row_refs = refs[8:12]
-    updated_ref, outgoing_ref, mine_ref = refs[12:15]
-    right, high, low, held, result, held_sem, whole_sem, block_sem = refs[15:]
+    updated_ref, outgoing_ref, mine_ref = refs[8:11]
+    held, result, held_sem, whole_sem, block_sem = refs[11:]
     step = pl.program_id(0)
     steps = pl.num_programs(0)
     slot = lax.rem(step, 2)
     tile = result.shape[1]
     edge = outgoing_ref.shape[1]
-    depth = inverse_ref.shape[0]
     down, across = tile // edge, result.shape[2] // edge
 
     def fetch(number, at):
@@ -197,16 +293,6 @@
     @pl.when(step == 0)
     def _():
         fetch(0, 0).start()
-        lift = row_refs[0].shape[0]
-        for k in range(4):
-            top = pl.multiple_of(table_ref[8 + k] * lift, lift)
-            right[pl.ds(top, lift)] = row_refs[k][...]
-        one = right[:depth]
-        two = right[depth:] - product(pivot_ref[depth:], one)
-        two = product(inverse_ref[...], two)
-        high[depth:], low[depth:] = halves(two)
-        one = one - product(pivot_ref[:depth], two)
-        high[:depth], low[:depth] = halves(one)
 
     for number in range(8):
 
@@ -240,8 +326,9 @@
         finish(slot, step)
 
 
-def update(front, block_owner, pivot, inverse, pieces, layers, table, devices, edge):
+def update(front, block_owner, high, low, pieces, table, devices, edge):
     rows, columns = front.shape
+    depth = high.shape[0]
     tile = pieces[0].shape[0]
     whole = lambda *shape: pl.BlockSpec(shape, lambda i, table: (0,) * len(shape))
     return pl.pallas_call(
@@ -252,20 +339,16 @@
             in_specs=[
                 pl.BlockSpec(memory_space=pltpu.SMEM),
                 pl.BlockSpec((tile, columns), lambda i, table: (table[i], 0)),
-                whole(*pivot.shape),
-                whole(*inverse.shape),
+                whole(*high.shape),
+                whole(*low.shape),
             ]
-            + [pl.BlockSpec(memory_space=pl.ANY)] * 8
-            + [whole(*layers[0].shape)] * 4,
+            + [pl.BlockSpec(memory_space=pl.ANY)] * 8,
             out_specs=[
                 pl.BlockSpec(memory_space=pl.ANY),
                 pl.BlockSpec(memory_space=pl.ANY),
                 whole(edge, pieces[0].shape[1]),
             ],
             scratch_shapes=[
-                pltpu.VMEM((2 * inverse.shape[0], columns), jnp.float32),
-                pltpu.VMEM((2 * inverse.shape[0], columns), jnp.bfloat16),
-                pltpu.VMEM((2 * inverse.shape[0], columns), jnp.bfloat16),
                 pltpu.VMEM((2, tile, pieces[0].shape[1]), jnp.float32),
                 pltpu.VMEM((2, tile, columns), jnp.float32),
                 pltpu.SemaphoreType.DMA((2,)),
@@ -280,12 +363,12 @@
         ],
         compiler_params=pltpu.CompilerParams(vmem_limit_bytes=44 * MIB),
         cost_estimate=pl.CostEstimate(
-            flops=16 * rows * columns * inverse.shape[0],
+            flops=6 * rows * columns * depth,
             bytes_accessed=40 * MIB,
             transcendentals=0,
         ),
         name="update",
-    )(table, block_owner, front, pivot, inverse, *pieces, *layers)
+    )(table, block_owner, front, high, low, *pieces)
 
 
 def add_kernel(slot_ref, parent_ref, arrived_ref, out_ref, sem):
@@ -335,8 +418,7 @@
     width = inverses.shape[1]
     edge = parent_in.shape[1]
     devices = lax.axis_size("row") * lax.axis_size("col")
-    row, col = lax.axis_index("row"), lax.axis_index("col")
-    me = row * lax.axis_size("col") + col
+    col = lax.axis_index("col")
 
     columns = front[:, : 2 * width]
     rows_one = product_rows(inverses[0], front[:width])
@@ -344,29 +426,25 @@
 
     owners = block_owner.reshape(-1)
     slots = block_slot.reshape(-1)
-    names = jnp.arange(devices, dtype=jnp.int32)
-    named = owners[None, :] == names[:, None]
+    named = owners[None, :] == jnp.arange(devices, dtype=jnp.int32)[:, None]
     labels = jnp.sum(jnp.where(named, slots[None, :] + 1, 0), axis=1).astype(jnp.float32)
-    labels = jnp.where(names[None, :] == me, labels[:, None], 0.0)
-    pivot = jnp.concatenate(
-        [rows_one[:, width : 2 * width], front[width : 2 * width, :width]], axis=0
-    )
-    pivot = jnp.where(me == 0, pivot, 0.0)
-    fill = devices * devices // width
-    shared = lax.psum(jnp.concatenate([pivot, labels.reshape(fill, width)], axis=0), AXES)
-    pivot = shared[: 2 * width]
-    markers = shared[2 * width :].reshape(devices, devices)
-    markers = lax.dynamic_slice_in_dim(markers, me, 1, 0).reshape(devices).astype(jnp.int32) - 1
-
-    pieces, numbers, layers, heights = exchange(columns, rows)
-    table = jnp.stack(numbers + heights + [col // 2, col % 2]).astype(jnp.int32)
-    updated, outgoing, mine = update(
-        front, block_owner, pivot, inverses[1], pieces, layers, table, devices, edge
-    )
+    pieces, numbers, layers, heights, pivots, labels = exchange(
+        columns,
+        rows,
+        rows_one[:, width : 2 * width],
+        front[width : 2 * width, :width],
+        labels.reshape(devices, 1, 1),
+    )
+    markers = labels.reshape(devices).astype(jnp.int32) - 1
+    core = col % 2
+    table = jnp.stack(numbers + heights + [col // 2, col % 2, core]).astype(jnp.int32)
+    high, low = fold(table, pivots, inverses, layers)
+    updated, outgoing, mine = update(front, block_owner, high, low, pieces, table, devices, edge)
     arrived = lax.all_to_all(outgoing, AXES, 0, 0, tiled=True)
 
     mine_one, mine_two = mine[:, :width], mine[:, width:]
-    mine_two = mine_two - exact(mine_one, pivot[:width])
+    corner = jnp.where(core == 0, pivots[0], pivots[1])
+    mine_two = mine_two - exact(mine_one, corner)
     panels = jnp.concatenate([exact(mine_one, inverses[0]), exact(mine_two, inverses[1])], axis=1)
     parent_out = extend_add(markers, parent_in, arrived)
     return (updated, panels, parent_out)

time: 467 us -> 389 us (0.83)
  waiting for transfers between devices: 306 us -> 183 us
  starting transfers between devices: 74.9 us -> 117 us
  between operations: 14.5 us -> 1.18 us
  other arithmetic: 13.4 us -> 19.7 us
  local copies, waits for them, and re-layouts: 14.4 us -> 20.4 us
    psum x1 -> x0, waiting for transfers between devices: 141 us -> none  [local(): lax.psum(jnp.concatenate([pivot, labels.reshape(fill, width)], axis=0), A...]
    ppermute x0 -> x7, waiting for transfers between devices: none -> 53.4 us  [the longest x6 53.4 us: spread(): return value + lax.ppermute(value, AXES, rounds[number])]
    ppermute x22 -> x20, waiting for transfers between devices: 58.3 us -> 25.5 us  [send(): return lax.ppermute(value, AXES, pairs(move, keep))]
    ppermute x22 -> x20, starting transfers between devices: 67.1 us -> 84.4 us  [send(): return lax.ppermute(value, AXES, pairs(move, keep))]
    ppermute x0 -> x7, starting transfers between devices: none -> 16.6 us  [the longest x6 15.3 us: spread(): return value + lax.ppermute(value, AXES, rounds[number])]
    unnamed x31 -> x29, local copies, waits for them, and re-layouts: 0.14 us -> 11.2 us
    pallas_call x0 -> x1, Pallas kernels: none -> 8.9 us  [fold(): pl.pallas_call(fold_kernel, grid_spec=pltpu.PrefetchScalarGridSpec(num_sc...]
    select_n x4 -> x5, other arithmetic: 7.1 us -> 13.6 us  [the longest x1 5.91 us: exchange(): jnp.where(z == 0, jnp.where(first, layer(3), layer(1)), jnp.where(first,...]
  transfers between devices with their start and end apart: 24 -> 29, of which waited for: 9 -> 7; matrix products, arithmetic and copies ran while one was open for 6% -> 8% of each run, Pallas kernels for 0% -> 8%
where the time goes in v4:
time: 389 us; the launch traced here: 388 us
  waiting for transfers between devices  183 us (47%)
  starting transfers between devices  117 us (30%)
  Pallas kernels  37.5 us (10%)
  local copies, waits for them, and re-layouts  20.4 us (5%)
  other arithmetic  19.7 us (5%)
  matrix products  8.69 us (2%)
    all_to_all x1, waiting for transfers between devices, local(): arrived = lax.all_to_all(outgoing, AXES, 0, 0, tiled=True)  104 us
    ppermute x20, starting transfers between devices, send(): return lax.ppermute(value, AXES, pairs(move, keep))  84.4 us
    ppermute x6, waiting for transfers between devices, spread(): return value + lax.ppermute(value, AXES, rounds[number])  53.4 us
    ppermute x20, waiting for transfers between devices, send(): return lax.ppermute(value, AXES, pairs(move, keep))  25.5 us
    pallas_call x1, Pallas kernels, update(): pl.pallas_call(update_kernel, grid_spec=pltpu.PrefetchScalarGridSpec(num_...  20.4 us
    ppermute x6, starting transfers between devices, spread(): return value + lax.ppermute(value, AXES, rounds[number])  15.3 us
    unnamed x29, local copies, waits for them, and re-layouts  11.2 us
    all_to_all x1, starting transfers between devices, local(): arrived = lax.all_to_all(outgoing, AXES, 0, 0, tiled=True)  10.8 us
  transfers between devices with their start and end apart: 29, of which 7 were waited for; matrix products, arithmetic and copies ran while one was open for 8% of the time, Pallas kernels for 8%

profile of v4, /device:TPU:1, one launch (start us, length us, event | category | flops | bytes accessed | tf_op | source)
XLA Modules:
  0.0 388.2 jit_solution(17239870324749573928)
XLA Ops:
  0.6 2.3 slice.82
  2.9 1.3 collective-permute-start.3
  4.2 5.9 %fusion.19 = (f32[512,1024]{1,0:T(8,128)}, f32[512,1024]{1,0:T(8,128)}, f32[512,1024]{1,0:T(8,128)}) fusion(f32[2048,1024]{1,0:T(8,128)} %front_ref.1), kind=kLoop, calls=%fused_computation.34 | loop fusion | bytes 12582912 | tf_op jit(solution)/shard_map/slice | solution.py:425
  10.1 3.9 %fusion.1 = f32[512,1024]{1,0:T(8,128)S(1)} fusion(f32[2048,1024]{1,0:T(8,128)} %front_ref.1, f32[2,512,512]{2,1,0:T(8,128)} %inverse_ref.1), kind=kOutput, calls=%fused_computation.2 | convolution fusion | flops 1610612736 | bytes 5242880 | tf_op jit(solution)/shard_map/dot_general | solution.py:454
  14.0 1.7 fusion
  15.7 7.3 %collective-permute-start.2 = (f32[512,1024]{1,0:T(8,128)}, f32[512,1024]{1,0:T(8,128)}, u32[]{:S(2)}, u32[]{:S(2)}) collective-permute-start(f32[512,1024]{1,0:T(8,128)} %fusion), channel_id=1, source_target_pairs={{0,16},{1,49},{2,18},{3,51},{4,20},{5,53},{6,22},{7,55},{8,24},{9,... | collective-permute-start | bytes 6291464 | tf_op jit(solution)/shard_map/ppermute | solution.py:30
  23.0 2.0 collective-permute-start.1
  25.0 2.0 collective-permute-start
  27.0 0.2 slice_select_fusion.2
  27.2 3.3 collective-permute-start.4
  30.5 22.3 %collective-permute-done.4 = f32[512,512]{1,0:T(8,128)S(1)} collective-permute-done((f32[512,512]{1,0:T(8,128)S(1)}, f32[512,512]{1,0:T(8,128)S(1)}, u32[]{:S(2)}, u32[]{:S(2)}) %collective-permute-start.4) | collective-permute-done | bytes 1048608 | tf_op jit(solution)/shard_map/ppermute | solution.py:84
  52.8 0.2 add.84
  53.1 4.4 %collective-permute-start.9 = (f32[512,512]{1,0:T(8,128)S(1)}, f32[512,512]{1,0:T(8,128)}, u32[]{:S(2)}, u32[]{:S(2)}) collective-permute-start(f32[512,512]{1,0:T(8,128)S(1)} %add.84), channel_id=1, source_target_pairs={{0,48},{16,32},{1,7},{3,5}} | collective-permute-start | bytes 3145736 | tf_op jit(solution)/shard_map/ppermute | solution.py:84
  57.5 5.9 %fusion.3 = (f32[256,1024]{1,0:T(8,128)}, f32[256,1024]{1,0:T(8,128)}, f32[256,1024]{1,0:T(8,128)}, f32[256,1024]{1,0:T(8,128)}) fusion(f32[512,1024]{1,0:T(8,128)S(1)} %fusion.1, f32[512,1024]{1,0:T(8,128)} %collective-permute-done.2, f32[2048,1024]{1,0:T(8,128)} %front_ref.1, pred[]{:T(512)S(6)} %eq.74, pred[]{:T(512)S(6)} %eq.68, ...), kind=kLoop, calls=%fused_computation.5 | loop fusion | flops 1310720 | bytes 12582915 | tf_op jit(solution)/shard_map/jit(_where)/select_n | solution.py:111
  63.4 2.3 collective-permute-start.8
  65.7 1.3 collective-permute-start.6
  67.0 1.6 collective-permute-start.5
  68.6 1.7 collective-permute-start.7
  70.8 1.4 add.85
  72.2 4.5 %collective-permute-done.8 = f32[256,1024]{1,0:T(8,128)} collective-permute-done((f32[256,1024]{1,0:T(8,128)}, f32[256,1024]{1,0:T(8,128)}, u32[]{:S(2)}, u32[]{:S(2)}) %collective-permute-start.8) | collective-permute-done | bytes 1048608 | tf_op jit(solution)/shard_map/ppermute | solution.py:30
  76.7 2.3 slice_select_fusion.1
  79.0 0.3 collective-permute-done.6
  79.3 3.5 select_select_fusion
  82.8 3.6 collective-permute-start.12
  86.4 1.4 collective-permute-start.10
  87.8 1.4 collective-permute-start.11
  89.2 8.9 %collective-permute-done.12 = f32[512,512]{1,0:T(8,128)S(1)} collective-permute-done((f32[512,512]{1,0:T(8,128)S(1)}, f32[512,512]{1,0:T(8,128)S(1)}, u32[]{:S(2)}, u32[]{:S(2)}) %collective-permute-start.12) | collective-permute-done | bytes 1048608 | tf_op jit(solution)/shard_map/ppermute | solution.py:84
  98.1 0.2 add.89
  98.3 1.4 collective-permute-start.13
  99.9 20.6 %collective-permute-done.11 = f32[256,1024]{1,0:T(8,128)S(1)} collective-permute-done((f32[256,1024]{1,0:T(8,128)S(1)}, f32[256,1024]{1,0:T(8,128)S(1)}, u32[]{:S(2)}, u32[]{:S(2)}) %collective-permute-start.11) | collective-permute-done | bytes 1048608 | tf_op jit(solution)/shard_map/ppermute | solution.py:30
  120.7 0.2 add.90
  120.9 1.4 collective-permute-start.16
  122.3 22.1 %collective-permute-done.16 = f32[512,512]{1,0:T(8,128)S(1)} collective-permute-done((f32[512,512]{1,0:T(8,128)S(1)}, f32[512,512]{1,0:T(8,128)S(1)}, u32[]{:S(2)}, u32[]{:S(2)}) %collective-permute-start.16) | collective-permute-done | bytes 1048608 | tf_op jit(solution)/shard_map/ppermute | solution.py:84
  144.4 0.2 add.91
  144.6 1.4 collective-permute-start.17
  146.1 6.9 %collective-permute-start.14 = (f32[256,1024]{1,0:T(8,128)S(1)}, f32[256,1024]{1,0:T(8,128)}, u32[]{:S(2)}, u32[]{:S(2)}) collective-permute-start(f32[256,1024]{1,0:T(8,128)S(1)} %broadcast_select_fusion.1.refs_0_), channel_id=1, source_target_pairs={{0,2},{1,7},{2,0},{3,5},{4,6},{5,3},{6,4},{7,1},{8,10},{9,15},{10,... | collective-permute-start | bytes 3145736 | tf_op jit(solution)/shard_map/ppermute | solution.py:30
  152.9 16.6 %collective-permute-start.22 = (f32[256,1024]{1,0:T(8,128)S(1)}, f32[256,1024]{1,0:T(8,128)}, u32[]{:S(2)}, u32[]{:S(2)}) collective-permute-start(f32[256,1024]{1,0:T(8,128)S(1)} %broadcast_select_fusion.1.refs_0_), channel_id=1, source_target_pairs={{0,6},{1,3},{2,4},{3,1},{4,2},{5,7},{6,0},{7,5},{8,14},{9,11},{10,... | collective-permute-start | bytes 3145736 | tf_op jit(solution)/shard_map/ppermute | solution.py:30
  169.7 1.5 collective-permute-start.20
  171.2 1.0 copy-done.3
  172.2 20.3 %collective-permute-start.25 = (f32[256,1024]{1,0:T(8,128)}, f32[256,1024]{1,0:T(8,128)}, u32[]{:S(2)}, u32[]{:S(2)}) collective-permute-start(f32[256,1024]{1,0:T(8,128)} %collective-permute-done.14.refs_2_), channel_id=1, source_target_pairs={{0,6},{1,3},{2,4},{3,1},{4,2},{5,7},{6,0},{7,5},{8,14},{9,11},{10,... | collective-permute-start | bytes 3145736 | tf_op jit(solution)/shard_map/ppermute | solution.py:30
  192.5 4.8 %collective-permute-start.18 = (f32[512,512]{1,0:T(8,128)S(1)}, f32[512,512]{1,0:T(8,128)}, u32[]{:S(2)}, u32[]{:S(2)}) collective-permute-start(f32[512,512]{1,0:T(8,128)S(1)} %add.92.pivot_ref), channel_id=1, source_target_pairs={{0,1},{1,0},{2,3},{3,2},{4,5},{5,4},{6,7},{7,6},{8,9},{9,8},{10,11... | collective-permute-start | bytes 3145736 | tf_op jit(solution)/shard_map/ppermute | solution.py:30
  197.3 1.0 copy-done.5
  198.3 0.5 collective-permute-start.24
  198.8 1.0 copy-done.7
  199.8 12.6 %collective-permute-start.23 = (f32[256,1024]{1,0:T(8,128)}, f32[256,1024]{1,0:T(8,128)}, u32[]{:S(2)}, u32[]{:S(2)}) collective-permute-start(f32[256,1024]{1,0:T(8,128)} %collective-permute-done.14.refs_2_), channel_id=1, source_target_pairs={{0,1},{1,0},{2,3},{3,2},{4,5},{5,4},{6,7},{7,6},{8,9},{9,8},{10,11... | collective-permute-start | bytes 3145736 | tf_op jit(solution)/shard_map/ppermute | solution.py:30
  212.4 0.3 collective-permute-start.26
  212.8 0.7 copy.25
  213.5 5.6 %all-to-all-start = ((f32[128,1,1]{2,1,0:T(1,128)}), f32[128,1,1]{2,1,0:T(1,128)S(1)}, u32[]{:S(2)}, u32[]{:S(2)}) async-start(f32[128,1,1]{2,1,0:T(1,128)} %copy.25), calls=%async_computation | async-start | bytes 131072 | tf_op jit(solution)/shard_map/all_to_all | solution.py:148
  219.2 1.2 copy-done.2
  220.4 1.2 copy-done.4
  221.6 1.2 copy-done.6
  222.8 1.2 copy-done.8
  224.1 8.9 %fold.1 = (bf16[1024,1024]{1,0:T(8,128)(2,1)S(1)}, bf16[1024,1024]{1,0:T(8,128)(2,1)}) custom-call(s32[15]{0:T(128)S(1)} %stack.60.table_ref, f32[512,512]{1,0:T(8,128)S(1)} %add.92.pivot_ref, f32[512,512]{1,0:T(8,128)} %collective-permute-done.18.other_ref, f32[2,512,512]{2,1,0:T(8,128)} %inverse_ref.1, f32[256,1024]{1,0:T(8,128)S(1)} %copy-done.2, ...), custom_call_target="tpu_custom_call" | custom-call | flops 4831838208 | bytes 12582912 | tf_op jit(solution)/shard_map/fold/pallas_call | solution.py:229
  233.0 1.4 copy-done.9
  234.3 20.4 %update.1 = (f32[2048,1024]{1,0:T(8,128)}, f32[128,128,128]{2,1,0:T(8,128)}, f32[128,1024]{1,0:T(8,128)S(1)}) custom-call(s32[15]{0:T(128)S(1)} %stack.60.table_ref, s32[16,8]{1,0:T(8,128)S(1)} %copy.24.owner_ref, f32[2048,1024]{1,0:T(8,128)} %front_ref.1, bf16[1024,1024]{1,0:T(8,128)(2,1)} %copy-done.9, bf16[1024,1024]{1,0:T(8,128)(2,1)} %get-tuple-element.35.low, ...), custom_call_target="tpu_custom_call" | custom-call | flops 12884901888 | bytes 41943040 | tf_op jit(solution)/shard_map/update/pallas_call | solution.py:334
  254.7 10.8 %all-to-all-start.1 = ((f32[128,128,128]{2,1,0:T(8,128)}), f32[128,128,128]{2,1,0:T(8,128)}, u32[]{:S(2)}, u32[]{:S(2)}) async-start(f32[128,128,128]{2,1,0:T(8,128)} %get-tuple-element.40), calls=%async_computation.1 | async-start | bytes 16777216 | tf_op jit(solution)/shard_map/all_to_all | solution.py:443
  265.5 2.4 add_reduce_fusion.slot_ref
  267.9 2.1 fusion.6
  270.0 2.0 fusion.10
  272.0 0.7 fusion.4
  272.7 0.8 pad_maximum_fusion.1
  273.5 104.4 %all-to-all-done.1.arrived_ref = f32[128,128,128]{2,1,0:T(8,128)} async-done(((f32[128,128,128]{2,1,0:T(8,128)}), f32[128,128,128]{2,1,0:T(8,128)}, u32[]{:S(2)}, u32[]{:S(2)}) %all-to-all-start.1) | async-done | bytes 8388640 | tf_op jit(solution)/shard_map/all_to_all | solution.py:443
  377.9 1.9 copy-done
  379.8 8.2 %extend_add.1 = f32[48,128,128]{2,1,0:T(8,128)} custom-call(s32[128]{0:T(128)S(1)} %add_reduce_fusion.slot_ref, f32[48,128,128]{2,1,0:T(8,128)S(1)} %copy-done, f32[128,128,128]{2,1,0:T(8,128)} %all-to-all-done.1.arrived_ref), custom_call_target="tpu_custom_call" | custom-call | flops 2097152 | bytes 14680064 | tf_op jit(solution)/shard_map/extend_add/pallas_call | solution.py:396
  (55 shorter events, 1.2 us)
Async XLA Ops:
  2.9 24.1 %collective-permute-start.3 = (f32[512,512]{1,0:T(8,128)}, f32[512,512]{1,0:T(8,128)S(1)}, u32[]{:S(2)}, u32[]{:S(2)}) collective-permute-start(f32[512,512]{1,0:T(8,128)} %slice.82), channel_id=1, source_target_pairs={{0,1}} | collective-permute-start | bytes 3145736 | tf_op jit(solution)/shard_map/ppermute | solution.py:95
  10.1 3.9 %copy-start.10 = (f32[512,1024]{1,0:T(8,128)S(1)}, f32[512,1024]{1,0:T(8,128)}, u32[]{:S(2)}) copy-start(f32[512,1024]{1,0:T(8,128)} %get-tuple-element.45) | copy-start | bytes 6291460
  15.7 37.4 %collective-permute-start.2 = (f32[512,1024]{1,0:T(8,128)}, f32[512,1024]{1,0:T(8,128)}, u32[]{:S(2)}, u32[]{:S(2)}) collective-permute-start(f32[512,1024]{1,0:T(8,128)} %fusion), channel_id=1, source_target_pairs={{0,16},{1,49},{2,18},{3,51},{4,20},{5,53},{6,22},{7,55},{8,24},{9,... | collective-permute-start | bytes 6291464 | tf_op jit(solution)/shard_map/ppermute | solution.py:30
  23.0 30.1 %collective-permute-start.1 = (f32[512,1024]{1,0:T(8,128)}, f32[512,1024]{1,0:T(8,128)}, u32[]{:S(2)}, u32[]{:S(2)}) collective-permute-start(f32[512,1024]{1,0:T(8,128)} %get-tuple-element.46), channel_id=1, source_target_pairs={{0,7},{16,23},{32,39},{48,55},{64,71},{80,87},{96,103},{112,119}} | collective-permute-start | bytes 6291464 | tf_op jit(solution)/shard_map/ppermute | solution.py:30
  25.0 28.1 %collective-permute-start = (f32[512,1024]{1,0:T(8,128)}, f32[512,1024]{1,0:T(8,128)}, u32[]{:S(2)}, u32[]{:S(2)}) collective-permute-start(f32[512,1024]{1,0:T(8,128)} %get-tuple-element.47), channel_id=1, source_target_pairs={{0,2},{16,18},{32,34},{48,50},{64,66},{80,82},{96,98},{112,114}} | collective-permute-start | bytes 6291464 | tf_op jit(solution)/shard_map/ppermute | solution.py:30
  27.2 25.6 %collective-permute-start.4 = (f32[512,512]{1,0:T(8,128)S(1)}, f32[512,512]{1,0:T(8,128)S(1)}, u32[]{:S(2)}, u32[]{:S(2)}) collective-permute-start(f32[512,512]{1,0:T(8,128)S(1)} %slice_select_fusion.2), channel_id=1, source_target_pairs={{0,16},{1,3}} | collective-permute-start | bytes 3145736 | tf_op jit(solution)/shard_map/ppermute | solution.py:84
  53.0 17.3 %copy-start.13 = (s32[16,8]{0,1:T(8,128)S(1)}, s32[16,8]{0,1:T(8,128)}, u32[]{:S(2)}) copy-start(s32[16,8]{0,1:T(8,128)} %param.8) | copy-start | bytes 1540
  53.0 17.5 %copy-start.12 = (s32[16,8]{0,1:T(8,128)S(1)}, s32[16,8]{0,1:T(8,128)}, u32[]{:S(2)}) copy-start(s32[16,8]{0,1:T(8,128)} %param.7) | copy-start | bytes 1540
  53.1 17.7 %collective-permute-start.9 = (f32[512,512]{1,0:T(8,128)S(1)}, f32[512,512]{1,0:T(8,128)}, u32[]{:S(2)}, u32[]{:S(2)}) collective-permute-start(f32[512,512]{1,0:T(8,128)S(1)} %add.84), channel_id=1, source_target_pairs={{0,48},{16,32},{1,7},{3,5}} | collective-permute-start | bytes 3145736 | tf_op jit(solution)/shard_map/ppermute | solution.py:84
  63.4 13.3 %collective-permute-start.8 = (f32[256,1024]{1,0:T(8,128)}, f32[256,1024]{1,0:T(8,128)}, u32[]{:S(2)}, u32[]{:S(2)}) collective-permute-start(f32[256,1024]{1,0:T(8,128)} %get-tuple-element.41), channel_id=1, source_target_pairs={{0,48},{1,17},{2,50},{3,19},{4,52},{5,21},{6,54},{7,23},{8,56},{9,... | collective-permute-start | bytes 3145736 | tf_op jit(solution)/shard_map/ppermute | solution.py:30
  65.7 13.7 %collective-permute-start.6 = (f32[256,1024]{1,0:T(8,128)}, f32[256,1024]{1,0:T(8,128)}, u32[]{:S(2)}, u32[]{:S(2)}) collective-permute-start(f32[256,1024]{1,0:T(8,128)} %get-tuple-element.42), channel_id=1, source_target_pairs={{0,1},{16,17},{32,33},{48,49},{64,65},{80,81},{96,97},{112,113}} | collective-permute-start | bytes 3145736 | tf_op jit(solution)/shard_map/ppermute | solution.py:30
  67.0 12.4 %collective-permute-start.5 = (f32[256,1024]{1,0:T(8,128)}, f32[256,1024]{1,0:T(8,128)}, u32[]{:S(2)}, u32[]{:S(2)}) collective-permute-start(f32[256,1024]{1,0:T(8,128)} %get-tuple-element.43), channel_id=1, source_target_pairs={{0,6},{2,4},{16,22},{18,20},{32,38},{34,36},{48,54},{50,52},{64,70... | collective-permute-start | bytes 3145736 | tf_op jit(solution)/shard_map/ppermute | solution.py:30
  68.6 10.7 %collective-permute-start.7 = (f32[256,1024]{1,0:T(8,128)}, f32[256,1024]{1,0:T(8,128)}, u32[]{:S(2)}, u32[]{:S(2)}) collective-permute-start(f32[256,1024]{1,0:T(8,128)} %get-tuple-element.44), channel_id=1, source_target_pairs={{0,3},{7,5},{16,19},{23,21},{32,35},{39,37},{48,51},{55,53},{64,67... | collective-permute-start | bytes 3145736 | tf_op jit(solution)/shard_map/ppermute | solution.py:30
  82.8 15.3 %collective-permute-start.12 = (f32[512,512]{1,0:T(8,128)S(1)}, f32[512,512]{1,0:T(8,128)S(1)}, u32[]{:S(2)}, u32[]{:S(2)}) collective-permute-start(f32[512,512]{1,0:T(8,128)S(1)} %add.85), channel_id=1, source_target_pairs={{0,2},{16,18},{32,34},{48,50},{1,17},{3,19},{5,21},{7,23}} | collective-permute-start | bytes 3145736 | tf_op jit(solution)/shard_map/ppermute | solution.py:84
  86.4 13.2 %collective-permute-start.10 = (f32[256,1024]{1,0:T(8,128)S(1)}, f32[256,1024]{1,0:T(8,128)S(1)}, u32[]{:S(2)}, u32[]{:S(2)}) collective-permute-start(f32[256,1024]{1,0:T(8,128)S(1)} %select_select_fusion), channel_id=1, source_target_pairs={{0,8},{1,9},{2,10},{3,11},{4,12},{5,13},{6,14},{7,15},{16,24},{17,... | collective-permute-start | bytes 3145736 | tf_op jit(solution)/shard_map/ppermute | solution.py:30
  87.8 32.7 %collective-permute-start.11 = (f32[256,1024]{1,0:T(8,128)S(1)}, f32[256,1024]{1,0:T(8,128)S(1)}, u32[]{:S(2)}, u32[]{:S(2)}) collective-permute-start(f32[256,1024]{1,0:T(8,128)S(1)} %slice_select_fusion.1), channel_id=1, source_target_pairs={{0,64},{1,65},{2,66},{3,67},{4,68},{5,69},{6,70},{7,71},{8,72},{9,... | collective-permute-start | bytes 3145736 | tf_op jit(solution)/shard_map/ppermute | solution.py:30
  98.3 22.4 %collective-permute-start.13 = (f32[512,512]{1,0:T(8,128)S(1)}, f32[512,512]{1,0:T(8,128)S(1)}, u32[]{:S(2)}, u32[]{:S(2)}) collective-permute-start(f32[512,512]{1,0:T(8,128)S(1)} %add.89), channel_id=1, source_target_pairs={{0,6},{2,4},{16,22},{18,20},{32,38},{34,36},{48,54},{50,52},{1,49}... | collective-permute-start | bytes 3145736 | tf_op jit(solution)/shard_map/ppermute | solution.py:84
  120.7 32.3 %copy-start.1 = (f32[256,1024]{1,0:T(8,128)}, f32[256,1024]{1,0:T(8,128)S(1)}, u32[]{:S(2)}) copy-start(f32[256,1024]{1,0:T(8,128)S(1)} %broadcast_select_fusion.refs_0_) | copy-start | bytes 3145732
  120.9 23.5 %collective-permute-start.16 = (f32[512,512]{1,0:T(8,128)S(1)}, f32[512,512]{1,0:T(8,128)S(1)}, u32[]{:S(2)}, u32[]{:S(2)}) collective-permute-start(f32[512,512]{1,0:T(8,128)S(1)} %add.90), channel_id=1, source_target_pairs={{0,64},{2,66},{4,68},{6,70},{16,80},{18,82},{20,84},{22,86},{32,96... | collective-permute-start | bytes 3145736 | tf_op jit(solution)/shard_map/ppermute | solution.py:84
  144.6 24.9 %collective-permute-start.17 = (f32[512,512]{1,0:T(8,128)S(1)}, f32[512,512]{1,0:T(8,128)S(1)}, u32[]{:S(2)}, u32[]{:S(2)}) collective-permute-start(f32[512,512]{1,0:T(8,128)S(1)} %add.91), channel_id=1, source_target_pairs={{0,8},{2,10},{4,12},{6,14},{16,24},{18,26},{20,28},{22,30},{32,40}... | collective-permute-start | bytes 3145736 | tf_op jit(solution)/shard_map/ppermute | solution.py:84
  146.0 23.7 %collective-permute-start.15 = (f32[256,1024]{1,0:T(8,128)S(1)}, f32[256,1024]{1,0:T(8,128)S(1)}, u32[]{:S(2)}, u32[]{:S(2)}) collective-permute-start(f32[256,1024]{1,0:T(8,128)S(1)} %broadcast_select_fusion.refs_0_), channel_id=1, source_target_pairs={{0,16},{1,49},{2,18},{3,51},{4,20},{5,53},{6,22},{7,55},{8,24},{9,... | collective-permute-start | bytes 3145736 | tf_op jit(solution)/shard_map/ppermute | solution.py:30
  146.1 23.7 %collective-permute-start.14 = (f32[256,1024]{1,0:T(8,128)S(1)}, f32[256,1024]{1,0:T(8,128)}, u32[]{:S(2)}, u32[]{:S(2)}) collective-permute-start(f32[256,1024]{1,0:T(8,128)S(1)} %broadcast_select_fusion.1.refs_0_), channel_id=1, source_target_pairs={{0,2},{1,7},{2,0},{3,5},{4,6},{5,3},{6,4},{7,1},{8,10},{9,15},{10,... | collective-permute-start | bytes 3145736 | tf_op jit(solution)/shard_map/ppermute | solution.py:30
  152.9 44.3 %collective-permute-start.19 = (f32[256,1024]{1,0:T(8,128)S(1)}, f32[256,1024]{1,0:T(8,128)S(1)}, u32[]{:S(2)}, u32[]{:S(2)}) collective-permute-start(f32[256,1024]{1,0:T(8,128)S(1)} %broadcast_select_fusion.refs_0_), channel_id=1, source_target_pairs={{0,48},{1,17},{2,50},{3,19},{4,52},{5,21},{6,54},{7,23},{8,56},{9,... | collective-permute-start | bytes 3145736 | tf_op jit(solution)/shard_map/ppermute | solution.py:30
  152.9 45.3 %collective-permute-start.22 = (f32[256,1024]{1,0:T(8,128)S(1)}, f32[256,1024]{1,0:T(8,128)}, u32[]{:S(2)}, u32[]{:S(2)}) collective-permute-start(f32[256,1024]{1,0:T(8,128)S(1)} %broadcast_select_fusion.1.refs_0_), channel_id=1, source_target_pairs={{0,6},{1,3},{2,4},{3,1},{4,2},{5,7},{6,0},{7,5},{8,14},{9,11},{10,... | collective-permute-start | bytes 3145736 | tf_op jit(solution)/shard_map/ppermute | solution.py:30
  169.7 29.0 %collective-permute-start.20 = (f32[256,1024]{1,0:T(8,128)S(1)}, f32[256,1024]{1,0:T(8,128)S(1)}, u32[]{:S(2)}, u32[]{:S(2)}) collective-permute-start(f32[256,1024]{1,0:T(8,128)S(1)} %collective-permute-done.15.refs_1_), channel_id=1, source_target_pairs={{0,48},{1,17},{2,50},{3,19},{4,52},{5,21},{6,54},{7,23},{8,56},{9,... | collective-permute-start | bytes 3145736 | tf_op jit(solution)/shard_map/ppermute | solution.py:30
  171.2 1.0 copy-start.3
  172.2 40.2 %collective-permute-start.25 = (f32[256,1024]{1,0:T(8,128)}, f32[256,1024]{1,0:T(8,128)}, u32[]{:S(2)}, u32[]{:S(2)}) collective-permute-start(f32[256,1024]{1,0:T(8,128)} %collective-permute-done.14.refs_2_), channel_id=1, source_target_pairs={{0,6},{1,3},{2,4},{3,1},{4,2},{5,7},{6,0},{7,5},{8,14},{9,11},{10,... | collective-permute-start | bytes 3145736 | tf_op jit(solution)/shard_map/ppermute | solution.py:30
  192.5 26.7 %collective-permute-start.18 = (f32[512,512]{1,0:T(8,128)S(1)}, f32[512,512]{1,0:T(8,128)}, u32[]{:S(2)}, u32[]{:S(2)}) collective-permute-start(f32[512,512]{1,0:T(8,128)S(1)} %add.92.pivot_ref), channel_id=1, source_target_pairs={{0,1},{1,0},{2,3},{3,2},{4,5},{5,4},{6,7},{7,6},{8,9},{9,8},{10,11... | collective-permute-start | bytes 3145736 | tf_op jit(solution)/shard_map/ppermute | solution.py:30
  197.3 1.0 copy-start.5
  198.3 36.1 %collective-permute-start.21 = (f32[256,1024]{1,0:T(8,128)S(1)}, f32[256,1024]{1,0:T(8,128)}, u32[]{:S(2)}, u32[]{:S(2)}) collective-permute-start(f32[256,1024]{1,0:T(8,128)S(1)} %broadcast_select_fusion.1.refs_0_), channel_id=1, source_target_pairs={{0,1},{1,0},{2,3},{3,2},{4,5},{5,4},{6,7},{7,6},{8,9},{9,8},{10,11... | collective-permute-start | bytes 3145736 | tf_op jit(solution)/shard_map/ppermute | solution.py:30
  198.3 36.1 %collective-permute-start.24 = (f32[256,1024]{1,0:T(8,128)}, f32[256,1024]{1,0:T(8,128)}, u32[]{:S(2)}, u32[]{:S(2)}) collective-permute-start(f32[256,1024]{1,0:T(8,128)} %collective-permute-done.22.refs_3_), channel_id=1, source_target_pairs={{0,1},{1,0},{2,3},{3,2},{4,5},{5,4},{6,7},{7,6},{8,9},{9,8},{10,11... | collective-permute-start | bytes 3145736 | tf_op jit(solution)/shard_map/ppermute | solution.py:30
  198.8 1.0 copy-start.7
  199.8 34.6 %collective-permute-start.23 = (f32[256,1024]{1,0:T(8,128)}, f32[256,1024]{1,0:T(8,128)}, u32[]{:S(2)}, u32[]{:S(2)}) collective-permute-start(f32[256,1024]{1,0:T(8,128)} %collective-permute-done.14.refs_2_), channel_id=1, source_target_pairs={{0,1},{1,0},{2,3},{3,2},{4,5},{5,4},{6,7},{7,6},{8,9},{9,8},{10,11... | collective-permute-start | bytes 3145736 | tf_op jit(solution)/shard_map/ppermute | solution.py:30
  212.4 22.0 %collective-permute-start.26 = (f32[256,1024]{1,0:T(8,128)}, f32[256,1024]{1,0:T(8,128)}, u32[]{:S(2)}, u32[]{:S(2)}) collective-permute-start(f32[256,1024]{1,0:T(8,128)} %collective-permute-done.25.refs_6_), channel_id=1, source_target_pairs={{0,1},{1,0},{2,3},{3,2},{4,5},{5,4},{6,7},{7,6},{8,9},{9,8},{10,11... | collective-permute-start | bytes 3145736 | tf_op jit(solution)/shard_map/ppermute | solution.py:30
  213.5 41.2 %all-to-all-start = ((f32[128,1,1]{2,1,0:T(1,128)}), f32[128,1,1]{2,1,0:T(1,128)S(1)}, u32[]{:S(2)}, u32[]{:S(2)}) async-start(f32[128,1,1]{2,1,0:T(1,128)} %copy.25), calls=%async_computation | async-start | bytes 131072 | tf_op jit(solution)/shard_map/all_to_all | solution.py:148
  219.2 1.2 copy-start.2
  220.4 1.2 copy-start.4
  221.6 1.2 copy-start.6
  222.8 1.2 copy-start.8
  233.0 1.4 copy-start.9
  254.7 123.2 %all-to-all-start.1 = ((f32[128,128,128]{2,1,0:T(8,128)}), f32[128,128,128]{2,1,0:T(8,128)}, u32[]{:S(2)}, u32[]{:S(2)}) async-start(f32[128,128,128]{2,1,0:T(8,128)} %get-tuple-element.40), calls=%async_computation.1 | async-start | bytes 16777216 | tf_op jit(solution)/shard_map/all_to_all | solution.py:443
  267.9 4.1 %copy-start.11 = (f32[2,512,512]{2,1,0:T(8,128)S(1)}, f32[2,512,512]{2,1,0:T(8,128)}, u32[]{:S(2)}) copy-start(f32[2,512,512]{2,1,0:T(8,128)} %inverse_ref.1) | copy-start | bytes 6291460
  377.9 1.9 copy-start

commit v5 on v4

--- a/solution.py
+++ b/solution.py
@@ -40,9 +40,6 @@
     return k ^ 1 if first else 3 - k
 
 
-STEPS = ("z0", "z1", "y0", "y1", "xl", "xh")
-
-
 def moved(spot, step):
     xl, z, xh, y = spot
     if step[0] == "z":
@@ -53,7 +50,7 @@
 
 
 def doubling():
-    orders = (STEPS, STEPS[2:4] + STEPS[:2] + ("xh", "xl"))
+    orders = (("xl", "xh", "z0", "z1", "y0", "y1"), ("xh", "xl", "y0", "y1", "z0", "z1"))
     having = [{(0, 0, 0, 0)}, {(0, 0, 0, 0)}]
     rounds = []
     for number in range(6):
@@ -67,11 +64,11 @@
     return rounds
 
 
-def exchange(columns, rows, pivot_one, pivot_two, labels):
+def exchange(columns, make_rows, labels):
     xl, z, xh, y, core = place()
     first = core == 0
     edge = columns.shape[0] // 8
-    lift = rows.shape[0] // 4
+    lift = columns.shape[1] // 4
     part = lambda k, count=1: columns[k * edge : (k + count) * edge]
     layer = lambda k, count=1: rows[k * lift : (k + count) * lift]
     rounds = doubling()
@@ -85,17 +82,22 @@
 
     source = lambda xl, z, xh, y, core: xh == 0 and y == 0 and core == 0
 
+    half = columns.shape[1] // 2
+    beside = lax.ppermute(columns[half : 2 * half, :half], AXES, [(0, 1)])
+
     one = send(part(1, 2), lambda xl, z, xh, y, core: (xl, z, xh, 1, 0), source)
     two = send(part(6, 2), lambda xl, z, xh, y, core: (xl, z, xh, 3, 1), source)
+    rows = make_rows()
     low = send(
         jnp.where(first, layer(1, 2), layer(2, 2)),
         lambda xl, z, xh, y, core: (xl, partner(z, core == 0), xh, y, core),
         lambda xl, z, xh, y, core: xl == 0 and z == 0,
     )
-    beside = lax.ppermute(pivot_two, AXES, [(0, 1)])
-    pivot = jnp.where(corner & first, pivot_one, beside)
+    pivot = jnp.where(corner & first, rows[:half, half:], beside)
     pivot = spread(pivot, 0)
-    one, two, low, pivot = lax.optimization_barrier((one, two, low, pivot))
+    one, two, low, pivot, columns, rows = lax.optimization_barrier(
+        (one, two, low, pivot, columns, rows)
+    )
 
     three = send(
         jnp.where(y == 0, part(3), one[edge:]),
@@ -147,9 +149,10 @@
     pivot = spread(pivot, 2)
     labels = lax.all_to_all(labels, AXES, 0, 0, tiled=True)
     pivot = spread(pivot, 3)
+    pivot = spread(pivot, 4)
     column = jnp.where(xh == 0, column, column_across)
     row = jnp.where(xl == 0, row, row_across)
-    column, row, pivot = lax.optimization_barrier((column, row, pivot))
+    column, row, pivot, labels = lax.optimization_barrier((column, row, pivot, labels))
 
     def around(value, step):
         return send(
@@ -165,7 +168,6 @@
 
     row_a, column_a = along(row, 0), around(column, 0)
     row_b, column_b = along(row, 1), around(column, 1)
-    pivot = spread(pivot, 4)
     other = swap(column)
     pivot = spread(pivot, 5)
     column_a, row_a, pivot = lax.optimization_barrier((column_a, row_a, pivot))
@@ -241,7 +243,7 @@
             scratch_shapes=[pltpu.VMEM((2 * depth, columns), jnp.float32)],
         ),
         out_shape=[half, half],
-        compiler_params=pltpu.CompilerParams(vmem_limit_bytes=44 * MIB),
+        compiler_params=pltpu.CompilerParams(vmem_limit_bytes=36 * MIB),
         cost_estimate=pl.CostEstimate(
             flops=18 * depth * depth * columns, bytes_accessed=12 * MIB, transcendentals=0
         ),
@@ -361,7 +363,7 @@
             jax.ShapeDtypeStruct((devices, edge, edge), jnp.float32),
             jax.ShapeDtypeStruct((edge, pieces[0].shape[1]), jnp.float32),
         ],
-        compiler_params=pltpu.CompilerParams(vmem_limit_bytes=44 * MIB),
+        compiler_params=pltpu.CompilerParams(vmem_limit_bytes=28 * MIB),
         cost_estimate=pl.CostEstimate(
             flops=6 * rows * columns * depth,
             bytes_accessed=40 * MIB,
@@ -421,19 +423,18 @@
     col = lax.axis_index("col")
 
     columns = front[:, : 2 * width]
-    rows_one = product_rows(inverses[0], front[:width])
-    rows = jnp.concatenate([rows_one, front[width : 2 * width]], axis=0)
+
+    def make_rows():
+        return jnp.concatenate(
+            [product_rows(inverses[0], front[:width]), front[width : 2 * width]], axis=0
+        )
 
     owners = block_owner.reshape(-1)
     slots = block_slot.reshape(-1)
     named = owners[None, :] == jnp.arange(devices, dtype=jnp.int32)[:, None]
     labels = jnp.sum(jnp.where(named, slots[None, :] + 1, 0), axis=1).astype(jnp.float32)
     pieces, numbers, layers, heights, pivots, labels = exchange(
-        columns,
-        rows,
-        rows_one[:, width : 2 * width],
-        front[width : 2 * width, :width],
-        labels.reshape(devices, 1, 1),
+        columns, make_rows, labels.reshape(devices, 1, 1)
     )
     markers = labels.reshape(devices).astype(jnp.int32) - 1
     core = col % 2

time: 389 us -> 387 us (level)
  starting transfers between devices: 117 us -> 78.5 us
  waiting for transfers between devices: 183 us -> 203 us
  other arithmetic: 19.7 us -> 35.5 us
    ppermute x20, starting transfers between devices: 84.4 us -> 26.5 us  [send(): return lax.ppermute(value, AXES, pairs(move, keep))]
    ppermute x20, waiting for transfers between devices: 25.5 us -> 40.3 us  [send(): return lax.ppermute(value, AXES, pairs(move, keep))]
    all_to_all x1, starting transfers between devices: 10.8 us -> 24 us  [local(): arrived = lax.all_to_all(outgoing, AXES, 0, 0, tiled=True)]
    all_to_all x1, starting transfers between devices: 5.62 us -> 13.5 us  [exchange(): labels = lax.all_to_all(labels, AXES, 0, 0, tiled=True)]
    select_n x1 -> x2, other arithmetic: 0.21 us -> 5.99 us  [the longest x1 4.4 us: exchange(): jnp.where(y == 0, part(3), one[edge:])]
    ppermute x6, waiting for transfers between devices: 53.4 us -> 57.7 us  [spread(): return value + lax.ppermute(value, AXES, rounds[number])]
    unnamed x29 -> x35, local copies, waits for them, and re-layouts: 11.2 us -> 12.7 us
  transfers between devices with their start and end apart: 29 -> 29, of which waited for: 7 -> 10; matrix products, arithmetic and copies ran while one was open for 8% -> 11% of each run, Pallas kernels for 8% -> 2%
where the time goes in v5:
time: 387 us; the launch traced here: 386 us
  waiting for transfers between devices  203 us (52%)
  starting transfers between devices  78.5 us (20%)
  Pallas kernels  37.5 us (10%)
  other arithmetic  35.5 us (9%)
  local copies, waits for them, and re-layouts  22 us (6%)
  matrix products  8.15 us (2%)
    all_to_all x1, waiting for transfers between devices, local(): arrived = lax.all_to_all(outgoing, AXES, 0, 0, tiled=True)  105 us
    ppermute x6, waiting for transfers between devices, spread(): return value + lax.ppermute(value, AXES, rounds[number])  57.7 us
    ppermute x20, waiting for transfers between devices, send(): return lax.ppermute(value, AXES, pairs(move, keep))  40.3 us
    ppermute x20, starting transfers between devices, send(): return lax.ppermute(value, AXES, pairs(move, keep))  26.5 us
    all_to_all x1, starting transfers between devices, local(): arrived = lax.all_to_all(outgoing, AXES, 0, 0, tiled=True)  24 us
    pallas_call x1, Pallas kernels, update(): pl.pallas_call(update_kernel, grid_spec=pltpu.PrefetchScalarGridSpec(num_...  21.7 us
    all_to_all x1, starting transfers between devices, exchange(): labels = lax.all_to_all(labels, AXES, 0, 0, tiled=True)  13.5 us
    ppermute x6, starting transfers between devices, spread(): return value + lax.ppermute(value, AXES, rounds[number])  13.3 us
  transfers between devices with their start and end apart: 29, of which 10 were waited for; matrix products, arithmetic and copies ran while one was open for 11% of the time, Pallas kernels for 2%

profile of v5, /device:TPU:1, one launch (start us, length us, event | category | flops | bytes accessed | tf_op | source)
XLA Modules:
  0.0 385.5 jit_solution(13549354977010719798)
XLA Ops:
  0.6 2.3 slice.82
  2.9 1.3 collective-permute-start.3
  4.2 6.0 %fusion.19 = (f32[512,1024]{1,0:T(8,128)}, f32[512,1024]{1,0:T(8,128)}, f32[512,1024]{1,0:T(8,128)}) fusion(f32[2048,1024]{1,0:T(8,128)} %front_ref.1), kind=kLoop, calls=%fused_computation.36 | loop fusion | bytes 12582912 | tf_op jit(solution)/shard_map/slice | solution.py:429
  10.2 3.6 fusion.2
  13.8 1.9 fusion.1
  15.8 7.3 %collective-permute-start.2 = (f32[512,1024]{1,0:T(8,128)}, f32[512,1024]{1,0:T(8,128)}, u32[]{:S(2)}, u32[]{:S(2)}) collective-permute-start(f32[512,1024]{1,0:T(8,128)} %fusion.1), channel_id=1, source_target_pairs={{0,16},{1,49},{2,18},{3,51},{4,20},{5,53},{6,22},{7,55},{8,24},{9,... | collective-permute-start | bytes 6291464 | tf_op jit(solution)/shard_map/ppermute | solution.py:30
  23.1 2.0 collective-permute-start.1
  25.1 2.0 collective-permute-start
  27.1 1.6 slice_select_fusion
  28.7 4.7 %collective-permute-start.4 = (f32[512,512]{1,0:T(8,128)S(1)}, f32[512,512]{1,0:T(8,128)S(1)}, u32[]{:S(2)}, u32[]{:S(2)}) collective-permute-start(f32[512,512]{1,0:T(8,128)S(1)} %slice_select_fusion), channel_id=1, source_target_pairs={{0,64},{1,9}} | collective-permute-start | bytes 3145736 | tf_op jit(solution)/shard_map/ppermute | solution.py:81
  33.4 2.4 pad_maximum_fusion
  35.8 18.6 %collective-permute-done.4 = f32[512,512]{1,0:T(8,128)S(1)} collective-permute-done((f32[512,512]{1,0:T(8,128)S(1)}, f32[512,512]{1,0:T(8,128)S(1)}, u32[]{:S(2)}, u32[]{:S(2)}) %collective-permute-start.4) | collective-permute-done | bytes 1048608 | tf_op jit(solution)/shard_map/ppermute | solution.py:81
  54.4 0.2 add.84
  54.6 3.0 select_select_fusion.1
  57.6 2.4 collective-permute-start.8
  60.0 2.2 collective-permute-start.9
  62.2 4.4 %slice_select_fusion.2 = (f32[256,1024]{1,0:T(8,128)}, f32[256,1024]{1,0:T(8,128)}, f32[256,1024]{1,0:T(8,128)}) fusion(f32[512,1024]{1,0:T(8,128)} %collective-permute-done, f32[2048,1024]{1,0:T(8,128)} %front_ref.1, pred[]{:T(512)S(6)} %eq.71, f32[512,1024]{1,0:T(8,128)} %collective-permute-done.1), kind=kLoop, calls=%fused_computation.20 | loop fusion | flops 524288 | bytes 8388609 | tf_op jit(solution)/shard_map/jit(_where)/select_n | solution.py:103
  66.6 1.6 collective-permute-start.5
  68.3 1.7 collective-permute-start.7
  70.0 1.3 collective-permute-start.6
  71.8 9.9 %collective-permute-done.9 = f32[512,512]{1,0:T(8,128)} collective-permute-done((f32[512,512]{1,0:T(8,128)S(1)}, f32[512,512]{1,0:T(8,128)}, u32[]{:S(2)}, u32[]{:S(2)}) %collective-permute-start.9) | collective-permute-done | bytes 1048608 | tf_op jit(solution)/shard_map/ppermute | solution.py:81
  81.7 1.4 add.85
  83.1 3.6 select_select_fusion
  86.8 4.6 %select_select_fusion.2 = f32[256,1024]{1,0:T(8,128)} fusion(f32[256,1024]{1,0:T(8,128)} %collective-permute-done.6, f32[256,1024]{1,0:T(8,128)} %collective-permute-done.7, f32[512,1024]{1,0:T(8,128)} %collective-permute-done.1, f32[256,1024]{1,0:T(8,128)} %collective-permute-done.5, f32[512,1024]{1,0:T(8,128)} %collective-permute-done, ...), kind=kLoop, calls=%fused_computation.18 | loop fusion | flops 1310720 | bytes 7340036 | tf_op jit(solution)/shard_map/jit(_where)/select_n | solution.py:123
  91.4 1.3 collective-permute-start.12
  92.7 11.7 %collective-permute-done.12 = f32[512,512]{1,0:T(8,128)S(1)} collective-permute-done((f32[512,512]{1,0:T(8,128)S(1)}, f32[512,512]{1,0:T(8,128)S(1)}, u32[]{:S(2)}, u32[]{:S(2)}) %collective-permute-start.12) | collective-permute-done | bytes 1048608 | tf_op jit(solution)/shard_map/ppermute | solution.py:81
  104.4 0.2 add.89
  104.6 1.4 collective-permute-start.13
  106.0 2.3 collective-permute-start.10
  108.2 4.9 %collective-permute-start.11 = (f32[256,1024]{1,0:T(8,128)}, f32[256,1024]{1,0:T(8,128)}, u32[]{:S(2)}, u32[]{:S(2)}) collective-permute-start(f32[256,1024]{1,0:T(8,128)} %select_select_fusion), channel_id=1, source_target_pairs={{0,64},{1,65},{2,66},{3,67},{4,68},{5,69},{6,70},{7,71},{8,72},{9,... | collective-permute-start | bytes 3145736 | tf_op jit(solution)/shard_map/ppermute | solution.py:30
  113.1 4.5 %collective-permute-done.13 = f32[512,512]{1,0:T(8,128)S(1)} collective-permute-done((f32[512,512]{1,0:T(8,128)S(1)}, f32[512,512]{1,0:T(8,128)S(1)}, u32[]{:S(2)}, u32[]{:S(2)}) %collective-permute-start.13) | collective-permute-done | bytes 1048608 | tf_op jit(solution)/shard_map/ppermute | solution.py:81
  117.8 2.3 collective-permute-start.14
  120.1 0.7 copy.24
  120.9 13.5 %all-to-all-start = ((f32[128,1,1]{2,1,0:T(1,128)}), f32[128,1,1]{2,1,0:T(1,128)S(1)}, u32[]{:S(2)}, u32[]{:S(2)}) async-start(f32[128,1,1]{2,1,0:T(1,128)} %copy.24), calls=%async_computation | async-start | bytes 131072 | tf_op jit(solution)/shard_map/all_to_all | solution.py:150
  134.3 2.4 broadcast_select_fusion.1.refs_0_
  136.8 7.8 %collective-permute-done.11 = f32[256,1024]{1,0:T(8,128)} collective-permute-done((f32[256,1024]{1,0:T(8,128)}, f32[256,1024]{1,0:T(8,128)}, u32[]{:S(2)}, u32[]{:S(2)}) %collective-permute-start.11) | collective-permute-done | bytes 1048608 | tf_op jit(solution)/shard_map/ppermute | solution.py:30
  144.6 2.4 broadcast_select_fusion.refs_0_
  146.9 2.4 add.91
  149.3 1.3 collective-permute-start.17
  151.1 13.0 %collective-permute-done.17 = f32[512,512]{1,0:T(8,128)S(1)} collective-permute-done((f32[512,512]{1,0:T(8,128)}, f32[512,512]{1,0:T(8,128)S(1)}, u32[]{:S(2)}, u32[]{:S(2)}) %collective-permute-start.17) | collective-permute-done | bytes 1048608 | tf_op jit(solution)/shard_map/ppermute | solution.py:81
  164.1 1.4 add.92.pivot_ref
  165.5 21.0 %collective-permute-done.16.refs_1_ = f32[256,1024]{1,0:T(8,128)S(1)} collective-permute-done((f32[256,1024]{1,0:T(8,128)}, f32[256,1024]{1,0:T(8,128)S(1)}, u32[]{:S(2)}, u32[]{:S(2)}) %collective-permute-start.16) | collective-permute-done | bytes 1048608 | tf_op jit(solution)/shard_map/ppermute | solution.py:30
  186.6 1.0 copy-done.5
  187.6 1.0 copy-done.7
  188.5 0.5 collective-permute-start.21
  189.1 11.2 %collective-permute-done.20.refs_3_ = f32[256,1024]{1,0:T(8,128)S(1)} collective-permute-done((f32[256,1024]{1,0:T(8,128)S(1)}, f32[256,1024]{1,0:T(8,128)S(1)}, u32[]{:S(2)}, u32[]{:S(2)}) %collective-permute-start.20) | collective-permute-done | bytes 1048608 | tf_op jit(solution)/shard_map/ppermute | solution.py:30
  200.2 1.0 copy-done.9
  201.2 0.3 collective-permute-done.25.refs_6_
  201.8 1.2 copy-done.6
  203.0 1.2 copy-done.8
  204.3 1.2 copy-done.10
  205.5 7.6 %fold.1 = (bf16[1024,1024]{1,0:T(8,128)(2,1)S(1)}, bf16[1024,1024]{1,0:T(8,128)(2,1)S(1)}) custom-call(s32[15]{0:T(128)S(1)} %stack.60.table_ref, f32[512,512]{1,0:T(8,128)S(1)} %add.92.pivot_ref, f32[512,512]{1,0:T(8,128)} %collective-permute-done.18.other_ref, f32[2,512,512]{2,1,0:T(8,128)S(1)} %copy-done.1, f32[256,1024]{1,0:T(8,128)} %broadcast_select_fusion.refs_0_, ...), custom_call_target="tpu_custom_call" | custom-call | flops 4831838208 | bytes 12582912 | tf_op jit(solution)/shard_map/fold/pallas_call | solution.py:231
  213.1 21.7 %update.1 = (f32[2048,1024]{1,0:T(8,128)}, f32[128,128,128]{2,1,0:T(8,128)S(1)}, f32[128,1024]{1,0:T(8,128)S(1)}) custom-call(s32[15]{0:T(128)S(1)} %stack.60.table_ref, s32[16,8]{1,0:T(8,128)S(1)} %copy.25.owner_ref, f32[2048,1024]{1,0:T(8,128)} %front_ref.1, bf16[1024,1024]{1,0:T(8,128)(2,1)S(1)} %get-tuple-element.40.high, ...), custom_call_target="tpu_custom_call" | custom-call | flops 12884901888 | bytes 41943040 | tf_op jit(solution)/shard_map/update/pallas_call | solution.py:336
  234.9 3.2 copy-done
  238.1 0.8 copy-done.3
  238.9 24.0 %all-to-all-start.1 = ((f32[128,128,128]{2,1,0:T(8,128)}), f32[128,128,128]{2,1,0:T(8,128)}, u32[]{:S(2)}, u32[]{:S(2)}) async-start(f32[128,128,128]{2,1,0:T(8,128)} %copy-done), calls=%async_computation.1 | async-start | bytes 16777216 | tf_op jit(solution)/shard_map/all_to_all | solution.py:444
  262.8 2.4 add_reduce_fusion.slot_ref
  265.2 1.7 fusion.6
  266.9 2.1 fusion.10
  269.1 0.7 fusion.4
  269.8 0.8 pad_maximum_fusion.1
  270.6 104.7 %all-to-all-done.1.arrived_ref = f32[128,128,128]{2,1,0:T(8,128)} async-done(((f32[128,128,128]{2,1,0:T(8,128)}), f32[128,128,128]{2,1,0:T(8,128)}, u32[]{:S(2)}, u32[]{:S(2)}) %all-to-all-start.1) | async-done | bytes 8388640 | tf_op jit(solution)/shard_map/all_to_all | solution.py:444
  375.3 1.9 copy-done.2
  377.2 8.2 %extend_add.1 = f32[48,128,128]{2,1,0:T(8,128)} custom-call(s32[128]{0:T(128)S(1)} %add_reduce_fusion.slot_ref, f32[48,128,128]{2,1,0:T(8,128)S(1)} %copy-done.2, f32[128,128,128]{2,1,0:T(8,128)} %all-to-all-done.1.arrived_ref), custom_call_target="tpu_custom_call" | custom-call | flops 2097152 | bytes 14680064 | tf_op jit(solution)/shard_map/extend_add/pallas_call | solution.py:398
  (63 shorter events, 1.4 us)
Async XLA Ops:
  2.9 24.2 %collective-permute-start.3 = (f32[512,512]{1,0:T(8,128)}, f32[512,512]{1,0:T(8,128)S(1)}, u32[]{:S(2)}, u32[]{:S(2)}) collective-permute-start(f32[512,512]{1,0:T(8,128)} %slice.82), channel_id=1, source_target_pairs={{0,1}} | collective-permute-start | bytes 3145736 | tf_op jit(solution)/shard_map/ppermute | solution.py:86
  4.2 6.0 %copy-start.1 = (f32[2,512,512]{2,1,0:T(8,128)S(1)}, f32[2,512,512]{2,1,0:T(8,128)}, u32[]{:S(2)}) copy-start(f32[2,512,512]{2,1,0:T(8,128)} %inverse_ref.1) | copy-start | bytes 6291460
  10.2 3.6 copy-start.13
  13.8 2.0 copy-start.11
  15.8 38.8 %collective-permute-start.2 = (f32[512,1024]{1,0:T(8,128)}, f32[512,1024]{1,0:T(8,128)}, u32[]{:S(2)}, u32[]{:S(2)}) collective-permute-start(f32[512,1024]{1,0:T(8,128)} %fusion.1), channel_id=1, source_target_pairs={{0,16},{1,49},{2,18},{3,51},{4,20},{5,53},{6,22},{7,55},{8,24},{9,... | collective-permute-start | bytes 6291464 | tf_op jit(solution)/shard_map/ppermute | solution.py:30
  23.1 31.5 %collective-permute-start.1 = (f32[512,1024]{1,0:T(8,128)}, f32[512,1024]{1,0:T(8,128)}, u32[]{:S(2)}, u32[]{:S(2)}) collective-permute-start(f32[512,1024]{1,0:T(8,128)} %get-tuple-element.51), channel_id=1, source_target_pairs={{0,7},{16,23},{32,39},{48,55},{64,71},{80,87},{96,103},{112,119}} | collective-permute-start | bytes 6291464 | tf_op jit(solution)/shard_map/ppermute | solution.py:30
  25.1 29.5 %collective-permute-start = (f32[512,1024]{1,0:T(8,128)}, f32[512,1024]{1,0:T(8,128)}, u32[]{:S(2)}, u32[]{:S(2)}) collective-permute-start(f32[512,1024]{1,0:T(8,128)} %get-tuple-element.52), channel_id=1, source_target_pairs={{0,2},{16,18},{32,34},{48,50},{64,66},{80,82},{96,98},{112,114}} | collective-permute-start | bytes 6291464 | tf_op jit(solution)/shard_map/ppermute | solution.py:30
  27.1 6.3 %copy-start.12 = (f32[512,1024]{1,0:T(8,128)S(1)}, f32[512,1024]{1,0:T(8,128)}, u32[]{:S(2)}) copy-start(f32[512,1024]{1,0:T(8,128)} %copy-done.11) | copy-start | bytes 6291460
  28.7 25.7 %collective-permute-start.4 = (f32[512,512]{1,0:T(8,128)S(1)}, f32[512,512]{1,0:T(8,128)S(1)}, u32[]{:S(2)}, u32[]{:S(2)}) collective-permute-start(f32[512,512]{1,0:T(8,128)S(1)} %slice_select_fusion), channel_id=1, source_target_pairs={{0,64},{1,9}} | collective-permute-start | bytes 3145736 | tf_op jit(solution)/shard_map/ppermute | solution.py:81
  35.8 21.8 %copy-start.14 = (f32[1024,1024]{1,0:T(8,128)}, f32[1024,1024]{1,0:T(8,128)S(1)}, u32[]{:S(2)}) copy-start(f32[1024,1024]{1,0:T(8,128)S(1)} %pad_maximum_fusion) | copy-start | bytes 12582916
  57.6 13.7 %copy-start.16 = (s32[16,8]{0,1:T(8,128)S(1)}, s32[16,8]{0,1:T(8,128)}, u32[]{:S(2)}) copy-start(s32[16,8]{0,1:T(8,128)} %param.8) | copy-start | bytes 1540
  57.6 13.9 %copy-start.15 = (s32[16,8]{0,1:T(8,128)S(1)}, s32[16,8]{0,1:T(8,128)}, u32[]{:S(2)}) copy-start(s32[16,8]{0,1:T(8,128)} %param.7) | copy-start | bytes 1540
  57.6 25.5 %collective-permute-start.8 = (f32[256,1024]{1,0:T(8,128)}, f32[256,1024]{1,0:T(8,128)}, u32[]{:S(2)}, u32[]{:S(2)}) collective-permute-start(f32[256,1024]{1,0:T(8,128)} %select_select_fusion.1), channel_id=1, source_target_pairs={{0,48},{1,17},{2,50},{3,19},{4,52},{5,21},{6,54},{7,23},{8,56},{9,... | collective-permute-start | bytes 3145736 | tf_op jit(solution)/shard_map/ppermute | solution.py:30
  60.0 21.7 %collective-permute-start.9 = (f32[512,512]{1,0:T(8,128)S(1)}, f32[512,512]{1,0:T(8,128)}, u32[]{:S(2)}, u32[]{:S(2)}) collective-permute-start(f32[512,512]{1,0:T(8,128)S(1)} %add.84), channel_id=1, source_target_pairs={{0,8},{64,72},{1,65},{9,73}} | collective-permute-start | bytes 3145736 | tf_op jit(solution)/shard_map/ppermute | solution.py:81
  66.6 20.2 %collective-permute-start.5 = (f32[256,1024]{1,0:T(8,128)}, f32[256,1024]{1,0:T(8,128)}, u32[]{:S(2)}, u32[]{:S(2)}) collective-permute-start(f32[256,1024]{1,0:T(8,128)} %get-tuple-element.47), channel_id=1, source_target_pairs={{0,6},{2,4},{16,22},{18,20},{32,38},{34,36},{48,54},{50,52},{64,70... | collective-permute-start | bytes 3145736 | tf_op jit(solution)/shard_map/ppermute | solution.py:30
  68.3 18.5 %collective-permute-start.7 = (f32[256,1024]{1,0:T(8,128)}, f32[256,1024]{1,0:T(8,128)}, u32[]{:S(2)}, u32[]{:S(2)}) collective-permute-start(f32[256,1024]{1,0:T(8,128)} %get-tuple-element.48), channel_id=1, source_target_pairs={{0,3},{7,5},{16,19},{23,21},{32,35},{39,37},{48,51},{55,53},{64,67... | collective-permute-start | bytes 3145736 | tf_op jit(solution)/shard_map/ppermute | solution.py:30
  70.0 16.8 %collective-permute-start.6 = (f32[256,1024]{1,0:T(8,128)}, f32[256,1024]{1,0:T(8,128)}, u32[]{:S(2)}, u32[]{:S(2)}) collective-permute-start(f32[256,1024]{1,0:T(8,128)} %get-tuple-element.49), channel_id=1, source_target_pairs={{0,1},{16,17},{32,33},{48,49},{64,65},{80,81},{96,97},{112,113}} | collective-permute-start | bytes 3145736 | tf_op jit(solution)/shard_map/ppermute | solution.py:30
  91.4 13.0 %collective-permute-start.12 = (f32[512,512]{1,0:T(8,128)S(1)}, f32[512,512]{1,0:T(8,128)S(1)}, u32[]{:S(2)}, u32[]{:S(2)}) collective-permute-start(f32[512,512]{1,0:T(8,128)S(1)} %add.85), channel_id=1, source_target_pairs={{0,16},{8,24},{64,80},{72,88},{1,3},{9,11},{65,67},{73,75}} | collective-permute-start | bytes 3145736 | tf_op jit(solution)/shard_map/ppermute | solution.py:81
  104.6 13.0 %collective-permute-start.13 = (f32[512,512]{1,0:T(8,128)S(1)}, f32[512,512]{1,0:T(8,128)S(1)}, u32[]{:S(2)}, u32[]{:S(2)}) collective-permute-start(f32[512,512]{1,0:T(8,128)S(1)} %add.89), channel_id=1, source_target_pairs={{0,48},{8,56},{16,32},{24,40},{64,112},{72,120},{80,96},{88,104},{... | collective-permute-start | bytes 3145736 | tf_op jit(solution)/shard_map/ppermute | solution.py:81
  106.0 28.4 %collective-permute-start.10 = (f32[256,1024]{1,0:T(8,128)}, f32[256,1024]{1,0:T(8,128)}, u32[]{:S(2)}, u32[]{:S(2)}) collective-permute-start(f32[256,1024]{1,0:T(8,128)} %select_select_fusion.2), channel_id=1, source_target_pairs={{0,8},{1,9},{2,10},{3,11},{4,12},{5,13},{6,14},{7,15},{16,24},{17,... | collective-permute-start | bytes 3145736 | tf_op jit(solution)/shard_map/ppermute | solution.py:30
  108.2 36.3 %collective-permute-start.11 = (f32[256,1024]{1,0:T(8,128)}, f32[256,1024]{1,0:T(8,128)}, u32[]{:S(2)}, u32[]{:S(2)}) collective-permute-start(f32[256,1024]{1,0:T(8,128)} %select_select_fusion), channel_id=1, source_target_pairs={{0,64},{1,65},{2,66},{3,67},{4,68},{5,69},{6,70},{7,71},{8,72},{9,... | collective-permute-start | bytes 3145736 | tf_op jit(solution)/shard_map/ppermute | solution.py:30
  117.8 29.1 %collective-permute-start.14 = (f32[512,512]{1,0:T(8,128)S(1)}, f32[512,512]{1,0:T(8,128)}, u32[]{:S(2)}, u32[]{:S(2)}) collective-permute-start(f32[512,512]{1,0:T(8,128)S(1)} %add.90), channel_id=1, source_target_pairs={{0,2},{8,10},{16,18},{24,26},{32,34},{40,42},{48,50},{56,58},{64,6... | collective-permute-start | bytes 3145736 | tf_op jit(solution)/shard_map/ppermute | solution.py:81
  120.9 28.5 %all-to-all-start = ((f32[128,1,1]{2,1,0:T(1,128)}), f32[128,1,1]{2,1,0:T(1,128)S(1)}, u32[]{:S(2)}, u32[]{:S(2)}) async-start(f32[128,1,1]{2,1,0:T(1,128)} %copy.24), calls=%async_computation | async-start | bytes 131072 | tf_op jit(solution)/shard_map/all_to_all | solution.py:150
  149.3 14.8 %collective-permute-start.17 = (f32[512,512]{1,0:T(8,128)}, f32[512,512]{1,0:T(8,128)S(1)}, u32[]{:S(2)}, u32[]{:S(2)}) collective-permute-start(f32[512,512]{1,0:T(8,128)} %add.91), channel_id=1, source_target_pairs={{0,6},{2,4},{8,14},{10,12},{16,22},{18,20},{24,30},{26,28},{32,38}... | collective-permute-start | bytes 3145736 | tf_op jit(solution)/shard_map/ppermute | solution.py:81
  150.7 35.9 %collective-permute-start.16 = (f32[256,1024]{1,0:T(8,128)}, f32[256,1024]{1,0:T(8,128)S(1)}, u32[]{:S(2)}, u32[]{:S(2)}) collective-permute-start(f32[256,1024]{1,0:T(8,128)} %broadcast_select_fusion.refs_0_), channel_id=1, source_target_pairs={{0,16},{1,49},{2,18},{3,51},{4,20},{5,53},{6,22},{7,55},{8,24},{9,... | collective-permute-start | bytes 3145736 | tf_op jit(solution)/shard_map/ppermute | solution.py:30
  150.8 35.8 %collective-permute-start.15 = (f32[256,1024]{1,0:T(8,128)}, f32[256,1024]{1,0:T(8,128)}, u32[]{:S(2)}, u32[]{:S(2)}) collective-permute-start(f32[256,1024]{1,0:T(8,128)} %broadcast_select_fusion.1.refs_0_), channel_id=1, source_target_pairs={{0,2},{1,7},{2,0},{3,5},{4,6},{5,3},{6,4},{7,1},{8,10},{9,15},{10,... | collective-permute-start | bytes 3145736 | tf_op jit(solution)/shard_map/ppermute | solution.py:30
  150.9 36.7 %collective-permute-start.19 = (f32[256,1024]{1,0:T(8,128)}, f32[256,1024]{1,0:T(8,128)S(1)}, u32[]{:S(2)}, u32[]{:S(2)}) collective-permute-start(f32[256,1024]{1,0:T(8,128)} %broadcast_select_fusion.refs_0_), channel_id=1, source_target_pairs={{0,48},{1,17},{2,50},{3,19},{4,52},{5,21},{6,54},{7,23},{8,56},{9,... | collective-permute-start | bytes 3145736 | tf_op jit(solution)/shard_map/ppermute | solution.py:30
  151.0 38.1 %collective-permute-start.22 = (f32[256,1024]{1,0:T(8,128)}, f32[256,1024]{1,0:T(8,128)}, u32[]{:S(2)}, u32[]{:S(2)}) collective-permute-start(f32[256,1024]{1,0:T(8,128)} %broadcast_select_fusion.1.refs_0_), channel_id=1, source_target_pairs={{0,6},{1,3},{2,4},{3,1},{4,2},{5,7},{6,0},{7,5},{8,14},{9,11},{10,... | collective-permute-start | bytes 3145736 | tf_op jit(solution)/shard_map/ppermute | solution.py:30
  186.6 13.7 %collective-permute-start.20 = (f32[256,1024]{1,0:T(8,128)S(1)}, f32[256,1024]{1,0:T(8,128)S(1)}, u32[]{:S(2)}, u32[]{:S(2)}) collective-permute-start(f32[256,1024]{1,0:T(8,128)S(1)} %collective-permute-done.16.refs_1_), channel_id=1, source_target_pairs={{0,48},{1,17},{2,50},{3,19},{4,52},{5,21},{6,54},{7,23},{8,56},{9,... | collective-permute-start | bytes 3145736 | tf_op jit(solution)/shard_map/ppermute | solution.py:30
  186.6 1.0 copy-start.5
  187.6 14.0 %collective-permute-start.25 = (f32[256,1024]{1,0:T(8,128)}, f32[256,1024]{1,0:T(8,128)}, u32[]{:S(2)}, u32[]{:S(2)}) collective-permute-start(f32[256,1024]{1,0:T(8,128)} %collective-permute-done.15.refs_2_), channel_id=1, source_target_pairs={{0,6},{1,3},{2,4},{3,1},{4,2},{5,7},{6,0},{7,5},{8,14},{9,11},{10,... | collective-permute-start | bytes 3145736 | tf_op jit(solution)/shard_map/ppermute | solution.py:30
  187.6 14.2 %collective-permute-start.18 = (f32[512,512]{1,0:T(8,128)S(1)}, f32[512,512]{1,0:T(8,128)}, u32[]{:S(2)}, u32[]{:S(2)}) collective-permute-start(f32[512,512]{1,0:T(8,128)S(1)} %add.92.pivot_ref), channel_id=1, source_target_pairs={{0,1},{1,0},{2,3},{3,2},{4,5},{5,4},{6,7},{7,6},{8,9},{9,8},{10,11... | collective-permute-start | bytes 3145736 | tf_op jit(solution)/shard_map/ppermute | solution.py:30
  187.6 1.0 copy-start.7
  188.5 24.6 %collective-permute-start.21 = (f32[256,1024]{1,0:T(8,128)}, f32[256,1024]{1,0:T(8,128)}, u32[]{:S(2)}, u32[]{:S(2)}) collective-permute-start(f32[256,1024]{1,0:T(8,128)} %broadcast_select_fusion.1.refs_0_), channel_id=1, source_target_pairs={{0,1},{1,0},{2,3},{3,2},{4,5},{5,4},{6,7},{7,6},{8,9},{9,8},{10,11... | collective-permute-start | bytes 3145736 | tf_op jit(solution)/shard_map/ppermute | solution.py:30
  189.0 24.1 %collective-permute-start.23 = (f32[256,1024]{1,0:T(8,128)}, f32[256,1024]{1,0:T(8,128)}, u32[]{:S(2)}, u32[]{:S(2)}) collective-permute-start(f32[256,1024]{1,0:T(8,128)} %collective-permute-done.15.refs_2_), channel_id=1, source_target_pairs={{0,1},{1,0},{2,3},{3,2},{4,5},{5,4},{6,7},{7,6},{8,9},{9,8},{10,11... | collective-permute-start | bytes 3145736 | tf_op jit(solution)/shard_map/ppermute | solution.py:30
  200.2 1.0 copy-start.9
  201.2 11.9 %collective-permute-start.24 = (f32[256,1024]{1,0:T(8,128)}, f32[256,1024]{1,0:T(8,128)}, u32[]{:S(2)}, u32[]{:S(2)}) collective-permute-start(f32[256,1024]{1,0:T(8,128)} %collective-permute-done.22.refs_3_), channel_id=1, source_target_pairs={{0,1},{1,0},{2,3},{3,2},{4,5},{5,4},{6,7},{7,6},{8,9},{9,8},{10,11... | collective-permute-start | bytes 3145736 | tf_op jit(solution)/shard_map/ppermute | solution.py:30
  201.5 11.6 %collective-permute-start.26 = (f32[256,1024]{1,0:T(8,128)}, f32[256,1024]{1,0:T(8,128)}, u32[]{:S(2)}, u32[]{:S(2)}) collective-permute-start(f32[256,1024]{1,0:T(8,128)} %collective-permute-done.25.refs_6_), channel_id=1, source_target_pairs={{0,1},{1,0},{2,3},{3,2},{4,5},{5,4},{6,7},{7,6},{8,9},{9,8},{10,11... | collective-permute-start | bytes 3145736 | tf_op jit(solution)/shard_map/ppermute | solution.py:30
  201.8 1.2 copy-start.6
  203.0 1.2 copy-start.8
  204.3 1.2 copy-start.10
  234.8 3.2 copy-start
  238.1 0.8 copy-start.3
  238.9 136.4 %all-to-all-start.1 = ((f32[128,128,128]{2,1,0:T(8,128)}), f32[128,128,128]{2,1,0:T(8,128)}, u32[]{:S(2)}, u32[]{:S(2)}) async-start(f32[128,128,128]{2,1,0:T(8,128)} %copy-done), calls=%async_computation.1 | async-start | bytes 16777216 | tf_op jit(solution)/shard_map/all_to_all | solution.py:444
  265.2 3.9 %copy-start.4 = (f32[128,1024]{1,0:T(8,128)S(1)}, f32[128,1024]{1,0:T(8,128)}, u32[]{:S(2)}) copy-start(f32[128,1024]{1,0:T(8,128)} %copy-done.3) | copy-start | bytes 1572868
  375.3 1.9 copy-start.2

commit v6 on v5

--- a/solution.py
+++ b/solution.py
@@ -64,7 +64,7 @@
     return rounds
 
 
-def exchange(columns, make_rows, labels):
+def exchange(front, columns, make_rows, labels):
     xl, z, xh, y, core = place()
     first = core == 0
     edge = columns.shape[0] // 8
@@ -87,7 +87,8 @@
 
     one = send(part(1, 2), lambda xl, z, xh, y, core: (xl, z, xh, 1, 0), source)
     two = send(part(6, 2), lambda xl, z, xh, y, core: (xl, z, xh, 3, 1), source)
-    rows = make_rows()
+    beside, front = lax.optimization_barrier((beside, front))
+    rows = make_rows(front)
     low = send(
         jnp.where(first, layer(1, 2), layer(2, 2)),
         lambda xl, z, xh, y, core: (xl, partner(z, core == 0), xh, y, core),
@@ -95,9 +96,7 @@
     )
     pivot = jnp.where(corner & first, rows[:half, half:], beside)
     pivot = spread(pivot, 0)
-    one, two, low, pivot, columns, rows = lax.optimization_barrier(
-        (one, two, low, pivot, columns, rows)
-    )
+    one, two, low, columns, rows = lax.optimization_barrier((one, two, low, columns, rows))
 
     three = send(
         jnp.where(y == 0, part(3), one[edge:]),
@@ -134,7 +133,7 @@
             jnp.where((core == 1) & (z == 3), low[lift:], high),
         ),
     )
-    column, row, pivot, labels = lax.optimization_barrier((column, row, pivot, labels))
+    column, row, labels = lax.optimization_barrier((column, row, labels))
 
     column_across = send(
         column,
@@ -170,7 +169,7 @@
     row_b, column_b = along(row, 1), around(column, 1)
     other = swap(column)
     pivot = spread(pivot, 5)
-    column_a, row_a, pivot = lax.optimization_barrier((column_a, row_a, pivot))
+    column_a, row_a = lax.optimization_barrier((column_a, row_a))
     row_c, column_c = along(row_a, 1), around(column_a, 1)
     pivots = (pivot, swap(pivot))
     other_a, other_b = swap(column_a), swap(column_b)
@@ -204,59 +203,14 @@
     return dot(left_high, right_low) + dot(left_low, right_high) + dot(left_high, right_high)
 
 
-def fold_kernel(table_ref, pivot_ref, other_ref, inverse_ref, *refs):
-    row_refs = refs[:4]
-    high, low, right = refs[4:]
-    depth = inverse_ref.shape[1]
-    lift = row_refs[0].shape[0]
-    for k in range(4):
-        top = pl.multiple_of(table_ref[8 + k] * lift, lift)
-        right[pl.ds(top, lift)] = row_refs[k][...]
-    first = table_ref[14] == 0
-    pivot_one = jnp.where(first, pivot_ref[...], other_ref[...])
-    pivot_two = jnp.where(first, other_ref[...], pivot_ref[...])
-    one = right[:depth]
-    two = right[depth:] - product(pivot_two, one)
-    two = product(inverse_ref[0], two)
-    high[depth:], low[depth:] = halves(two)
-    one = one - product(pivot_one, two)
-    high[:depth], low[:depth] = halves(one)
-
-
-def fold(table, pivots, inverses, layers):
-    depth = inverses.shape[1]
-    columns = layers[0].shape[1]
-    whole = lambda *shape: pl.BlockSpec(shape, lambda i, table: (0,) * len(shape))
-    half = jax.ShapeDtypeStruct((2 * depth, columns), jnp.bfloat16)
-    return pl.pallas_call(
-        fold_kernel,
-        grid_spec=pltpu.PrefetchScalarGridSpec(
-            num_scalar_prefetch=1,
-            grid=(1,),
-            in_specs=[
-                whole(depth, depth),
-                whole(depth, depth),
-                pl.BlockSpec((1, depth, depth), lambda i, table: (1, 0, 0)),
-            ]
-            + [whole(*layers[0].shape)] * 4,
-            out_specs=[whole(2 * depth, columns)] * 2,
-            scratch_shapes=[pltpu.VMEM((2 * depth, columns), jnp.float32)],
-        ),
-        out_shape=[half, half],
-        compiler_params=pltpu.CompilerParams(vmem_limit_bytes=36 * MIB),
-        cost_estimate=pl.CostEstimate(
-            flops=18 * depth * depth * columns, bytes_accessed=12 * MIB, transcendentals=0
-        ),
-        name="fold",
-    )(table, *pivots, inverses, *layers)
-
-
 def update_kernel(
-    table_ref, owner_ref, front_ref, high, low, *refs
+    table_ref, owner_ref, front_ref, pivot_ref, other_ref, inverse_ref, *refs
 ):
     column_refs = refs[:8]
-    updated_ref, outgoing_ref, mine_ref = refs[8:11]
-    held, result, held_sem, whole_sem, block_sem = refs[11:]
+    row_refs = refs[8:12]
+    updated_ref, outgoing_ref, mine_ref = refs[12:15]
+    right, high, low, held, result, held_sem, whole_sem, block_sem = refs[15:]
+    depth = inverse_ref.shape[1]
     step = pl.program_id(0)
     steps = pl.num_programs(0)
     slot = lax.rem(step, 2)
@@ -295,6 +249,19 @@
     @pl.when(step == 0)
     def _():
         fetch(0, 0).start()
+        lift = row_refs[0].shape[0]
+        for k in range(4):
+            top = pl.multiple_of(table_ref[8 + k] * lift, lift)
+            right[pl.ds(top, lift)] = row_refs[k][...]
+        first = table_ref[14] == 0
+        pivot_one = jnp.where(first, pivot_ref[...], other_ref[...])
+        pivot_two = jnp.where(first, other_ref[...], pivot_ref[...])
+        one = right[:depth]
+        two = right[depth:] - product(pivot_two, one)
+        two = product(inverse_ref[0], two)
+        high[depth:], low[depth:] = halves(two)
+        one = one - product(pivot_one, two)
+        high[:depth], low[:depth] = halves(one)
 
     for number in range(8):
 
@@ -328,9 +295,9 @@
         finish(slot, step)
 
 
-def update(front, block_owner, high, low, pieces, table, devices, edge):
+def update(front, block_owner, pivots, inverses, pieces, layers, table, devices, edge):
     rows, columns = front.shape
-    depth = high.shape[0]
+    depth = inverses.shape[1]
     tile = pieces[0].shape[0]
     whole = lambda *shape: pl.BlockSpec(shape, lambda i, table: (0,) * len(shape))
     return pl.pallas_call(
@@ -341,16 +308,21 @@
             in_specs=[
                 pl.BlockSpec(memory_space=pltpu.SMEM),
                 pl.BlockSpec((tile, columns), lambda i, table: (table[i], 0)),
-                whole(*high.shape),
-                whole(*low.shape),
+                whole(depth, depth),
+                whole(depth, depth),
+                pl.BlockSpec((1, depth, depth), lambda i, table: (1, 0, 0)),
             ]
-            + [pl.BlockSpec(memory_space=pl.ANY)] * 8,
+            + [pl.BlockSpec(memory_space=pl.ANY)] * 8
+            + [whole(*layers[0].shape)] * 4,
             out_specs=[
                 pl.BlockSpec(memory_space=pl.ANY),
                 pl.BlockSpec(memory_space=pl.ANY),
                 whole(edge, pieces[0].shape[1]),
             ],
             scratch_shapes=[
+                pltpu.VMEM((2 * depth, columns), jnp.float32),
+                pltpu.VMEM((2 * depth, columns), jnp.bfloat16),
+                pltpu.VMEM((2 * depth, columns), jnp.bfloat16),
                 pltpu.VMEM((2, tile, pieces[0].shape[1]), jnp.float32),
                 pltpu.VMEM((2, tile, columns), jnp.float32),
                 pltpu.SemaphoreType.DMA((2,)),
@@ -363,14 +335,14 @@
             jax.ShapeDtypeStruct((devices, edge, edge), jnp.float32),
             jax.ShapeDtypeStruct((edge, pieces[0].shape[1]), jnp.float32),
         ],
-        compiler_params=pltpu.CompilerParams(vmem_limit_bytes=28 * MIB),
+        compiler_params=pltpu.CompilerParams(vmem_limit_bytes=46 * MIB),
         cost_estimate=pl.CostEstimate(
-            flops=6 * rows * columns * depth,
+            flops=16 * rows * columns * depth,
             bytes_accessed=40 * MIB,
             transcendentals=0,
         ),
         name="update",
-    )(table, block_owner, front, high, low, *pieces)
+    )(table, block_owner, front, *pivots, inverses, *pieces, *layers)
 
 
 def add_kernel(slot_ref, parent_ref, arrived_ref, out_ref, sem):
@@ -424,7 +396,7 @@
 
     columns = front[:, : 2 * width]
 
-    def make_rows():
+    def make_rows(front):
         return jnp.concatenate(
             [product_rows(inverses[0], front[:width]), front[width : 2 * width]], axis=0
         )
@@ -434,13 +406,14 @@
     named = owners[None, :] == jnp.arange(devices, dtype=jnp.int32)[:, None]
     labels = jnp.sum(jnp.where(named, slots[None, :] + 1, 0), axis=1).astype(jnp.float32)
     pieces, numbers, layers, heights, pivots, labels = exchange(
-        columns, make_rows, labels.reshape(devices, 1, 1)
+        front[: 2 * width], columns, make_rows, labels.reshape(devices, 1, 1)
     )
     markers = labels.reshape(devices).astype(jnp.int32) - 1
     core = col % 2
     table = jnp.stack(numbers + heights + [col // 2, col % 2, core]).astype(jnp.int32)
-    high, low = fold(table, pivots, inverses, layers)
-    updated, outgoing, mine = update(front, block_owner, high, low, pieces, table, devices, edge)
+    updated, outgoing, mine = update(
+        front, block_owner, pivots, inverses, pieces, layers, table, devices, edge
+    )
     arrived = lax.all_to_all(outgoing, AXES, 0, 0, tiled=True)
 
     mine_one, mine_two = mine[:, :width], mine[:, width:]

time: 387 us -> 369 us (0.953)
  starting transfers between devices: 78.5 us -> 104 us
  waiting for transfers between devices: 203 us -> 179 us
  other arithmetic: 35.5 us -> 22 us
    ppermute x20, starting transfers between devices: 26.5 us -> 55.7 us  [send(): return lax.ppermute(value, AXES, pairs(move, keep))]
    ppermute x6, waiting for transfers between devices: 57.7 us -> 39 us  [spread(): return value + lax.ppermute(value, AXES, rounds[number])]
    slice x0 -> x2, local copies, waits for them, and re-layouts: none -> 9.83 us  [the longest x1 4.94 us: local(): front[:2 * width]]
    pallas_call x1 -> x0, Pallas kernels: 7.6 us -> none  [fold(): pl.pallas_call(fold_kernel, grid_spec=pltpu.PrefetchScalarGridSpec(num_sc...]
    unnamed x35 -> x23, local copies, waits for them, and re-layouts: 12.7 us -> 5.09 us
    all_to_all x1, starting transfers between devices: 24 us -> 19 us  [local(): arrived = lax.all_to_all(outgoing, AXES, 0, 0, tiled=True)]
    pallas_call x1, Pallas kernels: 21.7 us -> 26.6 us  [update(): pl.pallas_call(update_kernel, grid_spec=pltpu.PrefetchScalarGridSpec(num_...]
    ppermute x20, waiting for transfers between devices: 40.3 us -> 35.8 us  [send(): return lax.ppermute(value, AXES, pairs(move, keep))]
  transfers between devices with their start and end apart: 29 -> 29, of which waited for: 10 -> 9; matrix products, arithmetic and copies ran while one was open for 11% -> 11% of each run, Pallas kernels for 2% -> 0%
where the time goes in v6:
time: 369 us; the launch traced here: 368 us
  waiting for transfers between devices  179 us (49%)
  starting transfers between devices  104 us (28%)
  Pallas kernels  34.8 us (9%)
  other arithmetic  22 us (6%)
  local copies, waits for them, and re-layouts  20.2 us (5%)
  matrix products  6.7 us (2%)
    all_to_all x1, waiting for transfers between devices, local(): arrived = lax.all_to_all(outgoing, AXES, 0, 0, tiled=True)  104 us
    ppermute x20, starting transfers between devices, send(): return lax.ppermute(value, AXES, pairs(move, keep))  55.7 us
    ppermute x6, waiting for transfers between devices, spread(): return value + lax.ppermute(value, AXES, rounds[number])  39 us
    ppermute x20, waiting for transfers between devices, send(): return lax.ppermute(value, AXES, pairs(move, keep))  35.8 us
    pallas_call x1, Pallas kernels, update(): pl.pallas_call(update_kernel, grid_spec=pltpu.PrefetchScalarGridSpec(num_...  26.6 us
    all_to_all x1, starting transfers between devices, local(): arrived = lax.all_to_all(outgoing, AXES, 0, 0, tiled=True)  19 us
    ppermute x6, starting transfers between devices, spread(): return value + lax.ppermute(value, AXES, rounds[number])  17.1 us
    all_to_all x1, starting transfers between devices, exchange(): labels = lax.all_to_all(labels, AXES, 0, 0, tiled=True)  10.5 us
  transfers between devices with their start and end apart: 29, of which 9 were waited for; matrix products, arithmetic and copies ran while one was open for 11% of the time, Pallas kernels for 0%

profile of v6, /device:TPU:1, one launch (start us, length us, event | category | flops | bytes accessed | tf_op | source)
XLA Modules:
  0.0 367.7 jit_solution(13719039466547050778)
XLA Ops:
  0.6 2.3 slice.80
  2.9 1.3 collective-permute-start.2
  4.2 4.9 %fusion.22 = (f32[512,1024]{1,0:T(8,128)}, f32[512,1024]{1,0:T(8,128)}) fusion(f32[2048,1024]{1,0:T(8,128)} %front_ref.1), kind=kLoop, calls=%fused_computation.37 | loop fusion | bytes 8388608 | tf_op jit(solution)/shard_map/slice | solution.py:72
  9.1 2.0 collective-permute-start.1
  11.1 2.0 collective-permute-start
  13.1 4.9 %slice.81 = f32[1024,1024]{1,0:T(8,128)} slice(f32[2048,1024]{1,0:T(8,128)} %front_ref.1), slice={[0:1024], [0:1024]} | slice | bytes 8388608 | tf_op jit(solution)/shard_map/slice | solution.py:409
  18.0 2.0 slice.84
  20.0 0.8 copy-done.3
  20.8 1.8 fusion.4
  22.7 0.2 slice_select_fusion
  22.9 5.0 %collective-permute-start.10 = (f32[512,512]{1,0:T(8,128)S(1)}, f32[512,512]{1,0:T(8,128)S(1)}, u32[]{:S(2)}, u32[]{:S(2)}) collective-permute-start(f32[512,512]{1,0:T(8,128)S(1)} %slice_select_fusion), channel_id=1, source_target_pairs={{0,64},{1,9}} | collective-permute-start | bytes 3145736 | tf_op jit(solution)/shard_map/ppermute | solution.py:81
  27.9 0.5 fusion.1
  28.4 1.8 collective-permute-start.3
  30.2 16.6 %collective-permute-done.10 = f32[512,512]{1,0:T(8,128)S(1)} collective-permute-done((f32[512,512]{1,0:T(8,128)S(1)}, f32[512,512]{1,0:T(8,128)S(1)}, u32[]{:S(2)}, u32[]{:S(2)}) %collective-permute-start.10) | collective-permute-done | bytes 1048608 | tf_op jit(solution)/shard_map/ppermute | solution.py:81
  46.8 0.2 add.87
  47.0 1.4 collective-permute-start.11
  48.4 0.6 pad_maximum_fusion
  49.0 19.7 %collective-permute-done.11 = f32[512,512]{1,0:T(8,128)S(1)} collective-permute-done((f32[512,512]{1,0:T(8,128)S(1)}, f32[512,512]{1,0:T(8,128)S(1)}, u32[]{:S(2)}, u32[]{:S(2)}) %collective-permute-start.11) | collective-permute-done | bytes 1048608 | tf_op jit(solution)/shard_map/ppermute | solution.py:81
  68.7 0.2 add.88
  68.9 2.4 collective-permute-start.12
  71.3 1.4 select_select_fusion.1
  72.7 2.4 collective-permute-start.7
  75.2 4.3 %slice_select_fusion.2 = (f32[256,1024]{1,0:T(8,128)}, f32[256,1024]{1,0:T(8,128)}, f32[256,1024]{1,0:T(8,128)}) fusion(f32[512,1024]{1,0:T(8,128)} %collective-permute-done, f32[2048,1024]{1,0:T(8,128)} %front_ref.1, pred[]{:T(512)S(6)} %eq.71, f32[512,1024]{1,0:T(8,128)} %collective-permute-done.1), kind=kLoop, calls=%fused_computation.21 | loop fusion | flops 524288 | bytes 8388609 | tf_op jit(solution)/shard_map/jit(_where)/select_n | solution.py:102
  79.5 1.6 collective-permute-start.4
  81.1 1.7 collective-permute-start.6
  82.8 1.3 collective-permute-start.5
  84.6 1.4 add.89
  86.0 1.4 collective-permute-start.13
  87.4 9.0 %collective-permute-done.7 = f32[256,1024]{1,0:T(8,128)} collective-permute-done((f32[256,1024]{1,0:T(8,128)}, f32[256,1024]{1,0:T(8,128)}, u32[]{:S(2)}, u32[]{:S(2)}) %collective-permute-start.7) | collective-permute-done | bytes 1048608 | tf_op jit(solution)/shard_map/ppermute | solution.py:30
  96.4 2.0 select_select_fusion
  98.4 3.5 select_select_fusion.2
  102.0 2.3 collective-permute-start.8
  104.2 2.3 collective-permute-start.9
  106.5 2.6 collective-permute-done.13
  109.3 2.5 collective-permute-start.14
  111.8 0.7 copy.24
  112.5 10.5 %all-to-all-start = ((f32[128,1,1]{2,1,0:T(1,128)}), f32[128,1,1]{2,1,0:T(1,128)S(1)}, u32[]{:S(2)}, u32[]{:S(2)}) async-start(f32[128,1,1]{2,1,0:T(1,128)} %copy.24), calls=%async_computation | async-start | bytes 131072 | tf_op jit(solution)/shard_map/all_to_all | solution.py:149
  123.1 1.4 broadcast_select_fusion.1.refs_0_
  124.5 14.0 %collective-permute-done.9 = f32[256,1024]{1,0:T(8,128)} collective-permute-done((f32[256,1024]{1,0:T(8,128)S(1)}, f32[256,1024]{1,0:T(8,128)}, u32[]{:S(2)}, u32[]{:S(2)}) %collective-permute-start.9) | collective-permute-done | bytes 1048608 | tf_op jit(solution)/shard_map/ppermute | solution.py:30
  138.5 1.1 broadcast_select_fusion.refs_8_
  139.6 1.4 add.91
  141.3 4.5 %collective-permute-start.15 = (f32[512,512]{1,0:T(8,128)S(1)}, f32[512,512]{1,0:T(8,128)S(1)}, u32[]{:S(2)}, u32[]{:S(2)}) collective-permute-start(f32[512,512]{1,0:T(8,128)S(1)} %add.91), channel_id=1, source_target_pairs={{0,6},{2,4},{8,14},{10,12},{16,22},{18,20},{24,30},{26,28},{32,38}... | collective-permute-start | bytes 3145736 | tf_op jit(solution)/shard_map/ppermute | solution.py:81
  145.8 6.8 %collective-permute-start.25 = (f32[256,1024]{1,0:T(8,128)}, f32[256,1024]{1,0:T(8,128)S(1)}, u32[]{:S(2)}, u32[]{:S(2)}) collective-permute-start(f32[256,1024]{1,0:T(8,128)} %broadcast_select_fusion.refs_8_), channel_id=1, source_target_pairs={{0,48},{1,17},{2,50},{3,19},{4,52},{5,21},{6,54},{7,23},{8,56},{9,... | collective-permute-start | bytes 3145736 | tf_op jit(solution)/shard_map/ppermute | solution.py:30
  152.6 3.7 %collective-permute-done.19.refs_9_ = f32[256,1024]{1,0:T(8,128)} collective-permute-done((f32[256,1024]{1,0:T(8,128)}, f32[256,1024]{1,0:T(8,128)}, u32[]{:S(2)}, u32[]{:S(2)}) %collective-permute-start.19) | collective-permute-done | bytes 1048608 | tf_op jit(solution)/shard_map/ppermute | solution.py:30
  156.3 20.7 %collective-permute-start.17 = (f32[256,1024]{1,0:T(8,128)S(1)}, f32[256,1024]{1,0:T(8,128)S(1)}, u32[]{:S(2)}, u32[]{:S(2)}) collective-permute-start(f32[256,1024]{1,0:T(8,128)S(1)} %broadcast_select_fusion.1.refs_0_), channel_id=1, source_target_pairs={{0,1},{1,0},{2,3},{3,2},{4,5},{5,4},{6,7},{7,6},{8,9},{9,8},{10,11... | collective-permute-start | bytes 3145736 | tf_op jit(solution)/shard_map/ppermute | solution.py:30
  177.1 1.2 collective-permute-start.21
  178.3 0.2 add.92.pivot_ref
  178.6 0.8 collective-permute-start.22
  179.5 1.0 copy-done.1
  180.5 5.2 %collective-permute-start.26 = (f32[256,1024]{1,0:T(8,128)}, f32[256,1024]{1,0:T(8,128)}, u32[]{:S(2)}, u32[]{:S(2)}) collective-permute-start(f32[256,1024]{1,0:T(8,128)} %collective-permute-done.19.refs_9_), channel_id=1, source_target_pairs={{0,48},{1,17},{2,50},{3,19},{4,52},{5,21},{6,54},{7,23},{8,56},{9,... | collective-permute-start | bytes 3145736 | tf_op jit(solution)/shard_map/ppermute | solution.py:30
  185.7 5.6 %collective-permute-done.23.refs_6_ = f32[256,1024]{1,0:T(8,128)} collective-permute-done((f32[256,1024]{1,0:T(8,128)}, f32[256,1024]{1,0:T(8,128)}, u32[]{:S(2)}, u32[]{:S(2)}) %collective-permute-start.23) | collective-permute-done | bytes 1048608 | tf_op jit(solution)/shard_map/ppermute | solution.py:30
  191.3 3.3 collective-permute-start.24
  194.7 3.5 collective-permute-done.26.refs_11_
  198.2 1.2 copy-done.2
  199.4 26.6 %update.1 = (f32[2048,1024]{1,0:T(8,128)}, f32[128,128,128]{2,1,0:T(8,128)}, f32[128,1024]{1,0:T(8,128)S(1)}) custom-call(s32[15]{0:T(128)S(1)} %stack.60.table_ref, s32[16,8]{1,0:T(8,128)S(1)} %copy.25.owner_ref, f32[2048,1024]{1,0:T(8,128)} %front_ref.1, f32[512,512]{1,0:T(8,128)S(1)} %add.92.pivot_ref, f32[512,512]{1,0:T(8,128)} %collective-permute-done.16.other_ref, ...), custom_call_target="tpu_custom_call" | custom-call | flops 17179869184 | bytes 41943040 | tf_op jit(solution)/shard_map/update/pallas_call | solution.py:303
  226.0 19.0 %all-to-all-start.1 = ((f32[128,128,128]{2,1,0:T(8,128)}), f32[128,128,128]{2,1,0:T(8,128)}, u32[]{:S(2)}, u32[]{:S(2)}) async-start(f32[128,128,128]{2,1,0:T(8,128)} %get-tuple-element.40), calls=%async_computation.1 | async-start | bytes 16777216 | tf_op jit(solution)/shard_map/all_to_all | solution.py:417
  245.0 2.4 add_reduce_fusion.slot_ref
  247.4 2.1 fusion.9
  249.5 2.0 fusion.13
  251.5 0.7 fusion.7
  252.3 0.8 pad_maximum_fusion.1
  253.1 104.4 %all-to-all-done.1.arrived_ref = f32[128,128,128]{2,1,0:T(8,128)} async-done(((f32[128,128,128]{2,1,0:T(8,128)}), f32[128,128,128]{2,1,0:T(8,128)}, u32[]{:S(2)}, u32[]{:S(2)}) %all-to-all-start.1) | async-done | bytes 8388640 | tf_op jit(solution)/shard_map/all_to_all | solution.py:417
  357.5 1.9 copy-done
  359.3 8.2 %extend_add.1 = f32[48,128,128]{2,1,0:T(8,128)} custom-call(s32[128]{0:T(128)S(1)} %add_reduce_fusion.slot_ref, f32[48,128,128]{2,1,0:T(8,128)S(1)} %copy-done, f32[128,128,128]{2,1,0:T(8,128)} %all-to-all-done.1.arrived_ref), custom_call_target="tpu_custom_call" | custom-call | flops 2097152 | bytes 14680064 | tf_op jit(solution)/shard_map/extend_add/pallas_call | solution.py:370
  (52 shorter events, 1.2 us)
Async XLA Ops:
  2.9 15.1 %collective-permute-start.2 = (f32[512,512]{1,0:T(8,128)}, f32[512,512]{1,0:T(8,128)S(1)}, u32[]{:S(2)}, u32[]{:S(2)}) collective-permute-start(f32[512,512]{1,0:T(8,128)} %slice.80), channel_id=1, source_target_pairs={{0,1}} | collective-permute-start | bytes 3145736 | tf_op jit(solution)/shard_map/ppermute | solution.py:86
  9.1 62.2 %collective-permute-start.1 = (f32[512,1024]{1,0:T(8,128)}, f32[512,1024]{1,0:T(8,128)}, u32[]{:S(2)}, u32[]{:S(2)}) collective-permute-start(f32[512,1024]{1,0:T(8,128)} %get-tuple-element.44), channel_id=1, source_target_pairs={{0,7},{16,23},{32,39},{48,55},{64,71},{80,87},{96,103},{112,119}} | collective-permute-start | bytes 6291464 | tf_op jit(solution)/shard_map/ppermute | solution.py:30
  11.1 60.2 %collective-permute-start = (f32[512,1024]{1,0:T(8,128)}, f32[512,1024]{1,0:T(8,128)}, u32[]{:S(2)}, u32[]{:S(2)}) collective-permute-start(f32[512,1024]{1,0:T(8,128)} %get-tuple-element.45), channel_id=1, source_target_pairs={{0,2},{16,18},{32,34},{48,50},{64,66},{80,82},{96,98},{112,114}} | collective-permute-start | bytes 6291464 | tf_op jit(solution)/shard_map/ppermute | solution.py:30
  13.1 6.9 %copy-start.5 = (f32[2,512,512]{2,1,0:T(8,128)S(1)}, f32[2,512,512]{2,1,0:T(8,128)}, u32[]{:S(2)}) copy-start(f32[2,512,512]{2,1,0:T(8,128)} %inverse_ref.1) | copy-start | bytes 6291460
  18.0 2.8 copy-start.3
  22.9 23.9 %collective-permute-start.10 = (f32[512,512]{1,0:T(8,128)S(1)}, f32[512,512]{1,0:T(8,128)S(1)}, u32[]{:S(2)}, u32[]{:S(2)}) collective-permute-start(f32[512,512]{1,0:T(8,128)S(1)} %slice_select_fusion), channel_id=1, source_target_pairs={{0,64},{1,9}} | collective-permute-start | bytes 3145736 | tf_op jit(solution)/shard_map/ppermute | solution.py:81
  28.4 42.9 %collective-permute-start.3 = (f32[512,1024]{1,0:T(8,128)S(1)}, f32[512,1024]{1,0:T(8,128)S(1)}, u32[]{:S(2)}, u32[]{:S(2)}) collective-permute-start(f32[512,1024]{1,0:T(8,128)S(1)} %fusion.1), channel_id=1, source_target_pairs={{0,16},{1,49},{2,18},{3,51},{4,20},{5,53},{6,22},{7,55},{8,24},{9,... | collective-permute-start | bytes 6291464 | tf_op jit(solution)/shard_map/ppermute | solution.py:30
  47.0 21.7 %collective-permute-start.11 = (f32[512,512]{1,0:T(8,128)S(1)}, f32[512,512]{1,0:T(8,128)S(1)}, u32[]{:S(2)}, u32[]{:S(2)}) collective-permute-start(f32[512,512]{1,0:T(8,128)S(1)} %add.87), channel_id=1, source_target_pairs={{0,8},{64,72},{1,65},{9,73}} | collective-permute-start | bytes 3145736 | tf_op jit(solution)/shard_map/ppermute | solution.py:81
  49.0 23.8 %copy-start.4 = (f32[1024,1024]{1,0:T(8,128)}, f32[1024,1024]{1,0:T(8,128)S(1)}, u32[]{:S(2)}) copy-start(f32[1024,1024]{1,0:T(8,128)S(1)} %pad_maximum_fusion) | copy-start | bytes 12582916
  68.9 15.7 %collective-permute-start.12 = (f32[512,512]{1,0:T(8,128)S(1)}, f32[512,512]{1,0:T(8,128)}, u32[]{:S(2)}, u32[]{:S(2)}) collective-permute-start(f32[512,512]{1,0:T(8,128)S(1)} %add.88), channel_id=1, source_target_pairs={{0,16},{8,24},{64,80},{72,88},{1,3},{9,11},{65,67},{73,75}} | collective-permute-start | bytes 3145736 | tf_op jit(solution)/shard_map/ppermute | solution.py:81
  72.7 11.4 %copy-start.9 = (s32[16,8]{0,1:T(8,128)S(1)}, s32[16,8]{0,1:T(8,128)}, u32[]{:S(2)}) copy-start(s32[16,8]{0,1:T(8,128)} %param.8) | copy-start | bytes 1540
  72.7 11.6 %copy-start.8 = (s32[16,8]{0,1:T(8,128)S(1)}, s32[16,8]{0,1:T(8,128)}, u32[]{:S(2)}) copy-start(s32[16,8]{0,1:T(8,128)} %param.7) | copy-start | bytes 1540
  72.7 23.7 %collective-permute-start.7 = (f32[256,1024]{1,0:T(8,128)}, f32[256,1024]{1,0:T(8,128)}, u32[]{:S(2)}, u32[]{:S(2)}) collective-permute-start(f32[256,1024]{1,0:T(8,128)} %select_select_fusion.1), channel_id=1, source_target_pairs={{0,48},{1,17},{2,50},{3,19},{4,52},{5,21},{6,54},{7,23},{8,56},{9,... | collective-permute-start | bytes 3145736 | tf_op jit(solution)/shard_map/ppermute | solution.py:30
  79.5 18.9 %collective-permute-start.4 = (f32[256,1024]{1,0:T(8,128)}, f32[256,1024]{1,0:T(8,128)}, u32[]{:S(2)}, u32[]{:S(2)}) collective-permute-start(f32[256,1024]{1,0:T(8,128)} %get-tuple-element.41), channel_id=1, source_target_pairs={{0,6},{2,4},{16,22},{18,20},{32,38},{34,36},{48,54},{50,52},{64,70... | collective-permute-start | bytes 3145736 | tf_op jit(solution)/shard_map/ppermute | solution.py:30
  81.1 17.3 %collective-permute-start.6 = (f32[256,1024]{1,0:T(8,128)}, f32[256,1024]{1,0:T(8,128)}, u32[]{:S(2)}, u32[]{:S(2)}) collective-permute-start(f32[256,1024]{1,0:T(8,128)} %get-tuple-element.42), channel_id=1, source_target_pairs={{0,3},{7,5},{16,19},{23,21},{32,35},{39,37},{48,51},{55,53},{64,67... | collective-permute-start | bytes 3145736 | tf_op jit(solution)/shard_map/ppermute | solution.py:30
  82.8 15.6 %collective-permute-start.5 = (f32[256,1024]{1,0:T(8,128)}, f32[256,1024]{1,0:T(8,128)}, u32[]{:S(2)}, u32[]{:S(2)}) collective-permute-start(f32[256,1024]{1,0:T(8,128)} %get-tuple-element.43), channel_id=1, source_target_pairs={{0,1},{16,17},{32,33},{48,49},{64,65},{80,81},{96,97},{112,113}} | collective-permute-start | bytes 3145736 | tf_op jit(solution)/shard_map/ppermute | solution.py:30
  86.0 23.1 %collective-permute-start.13 = (f32[512,512]{1,0:T(8,128)S(1)}, f32[512,512]{1,0:T(8,128)S(1)}, u32[]{:S(2)}, u32[]{:S(2)}) collective-permute-start(f32[512,512]{1,0:T(8,128)S(1)} %add.89), channel_id=1, source_target_pairs={{0,48},{8,56},{16,32},{24,40},{64,112},{72,120},{80,96},{88,104},{... | collective-permute-start | bytes 3145736 | tf_op jit(solution)/shard_map/ppermute | solution.py:81
  101.9 21.2 %copy-start.7 = (f32[256,1024]{1,0:T(8,128)}, f32[256,1024]{1,0:T(8,128)S(1)}, u32[]{:S(2)}) copy-start(f32[256,1024]{1,0:T(8,128)S(1)} %select_select_fusion.2) | copy-start | bytes 3145732
  102.0 21.2 %collective-permute-start.8 = (f32[256,1024]{1,0:T(8,128)S(1)}, f32[256,1024]{1,0:T(8,128)}, u32[]{:S(2)}, u32[]{:S(2)}) collective-permute-start(f32[256,1024]{1,0:T(8,128)S(1)} %select_select_fusion.2), channel_id=1, source_target_pairs={{0,8},{1,9},{2,10},{3,11},{4,12},{5,13},{6,14},{7,15},{16,24},{17,... | collective-permute-start | bytes 3145736 | tf_op jit(solution)/shard_map/ppermute | solution.py:30
  104.2 34.2 %collective-permute-start.9 = (f32[256,1024]{1,0:T(8,128)S(1)}, f32[256,1024]{1,0:T(8,128)}, u32[]{:S(2)}, u32[]{:S(2)}) collective-permute-start(f32[256,1024]{1,0:T(8,128)S(1)} %select_select_fusion), channel_id=1, source_target_pairs={{0,64},{1,65},{2,66},{3,67},{4,68},{5,69},{6,70},{7,71},{8,72},{9,... | collective-permute-start | bytes 3145736 | tf_op jit(solution)/shard_map/ppermute | solution.py:30
  109.3 30.3 %collective-permute-start.14 = (f32[512,512]{1,0:T(8,128)S(1)}, f32[512,512]{1,0:T(8,128)}, u32[]{:S(2)}, u32[]{:S(2)}) collective-permute-start(f32[512,512]{1,0:T(8,128)S(1)} %add.90), channel_id=1, source_target_pairs={{0,2},{8,10},{16,18},{24,26},{32,34},{40,42},{48,50},{56,58},{64,6... | collective-permute-start | bytes 3145736 | tf_op jit(solution)/shard_map/ppermute | solution.py:81
  112.5 28.5 %all-to-all-start = ((f32[128,1,1]{2,1,0:T(1,128)}), f32[128,1,1]{2,1,0:T(1,128)S(1)}, u32[]{:S(2)}, u32[]{:S(2)}) async-start(f32[128,1,1]{2,1,0:T(1,128)} %copy.24), calls=%async_computation | async-start | bytes 131072 | tf_op jit(solution)/shard_map/all_to_all | solution.py:149
  141.1 15.3 %collective-permute-start.19 = (f32[256,1024]{1,0:T(8,128)}, f32[256,1024]{1,0:T(8,128)}, u32[]{:S(2)}, u32[]{:S(2)}) collective-permute-start(f32[256,1024]{1,0:T(8,128)} %broadcast_select_fusion.refs_8_), channel_id=1, source_target_pairs={{0,16},{1,49},{2,18},{3,51},{4,20},{5,53},{6,22},{7,55},{8,24},{9,... | collective-permute-start | bytes 3145736 | tf_op jit(solution)/shard_map/ppermute | solution.py:30
  141.2 35.9 %collective-permute-start.18 = (f32[256,1024]{1,0:T(8,128)S(1)}, f32[256,1024]{1,0:T(8,128)}, u32[]{:S(2)}, u32[]{:S(2)}) collective-permute-start(f32[256,1024]{1,0:T(8,128)S(1)} %broadcast_select_fusion.1.refs_0_), channel_id=1, source_target_pairs={{0,2},{1,7},{2,0},{3,5},{4,6},{5,3},{6,4},{7,1},{8,10},{9,15},{10,... | collective-permute-start | bytes 3145736 | tf_op jit(solution)/shard_map/ppermute | solution.py:30
  141.3 35.8 %collective-permute-start.15 = (f32[512,512]{1,0:T(8,128)S(1)}, f32[512,512]{1,0:T(8,128)S(1)}, u32[]{:S(2)}, u32[]{:S(2)}) collective-permute-start(f32[512,512]{1,0:T(8,128)S(1)} %add.91), channel_id=1, source_target_pairs={{0,6},{2,4},{8,14},{10,12},{16,22},{18,20},{24,30},{26,28},{32,38}... | collective-permute-start | bytes 3145736 | tf_op jit(solution)/shard_map/ppermute | solution.py:81
  145.8 32.7 %collective-permute-start.25 = (f32[256,1024]{1,0:T(8,128)}, f32[256,1024]{1,0:T(8,128)S(1)}, u32[]{:S(2)}, u32[]{:S(2)}) collective-permute-start(f32[256,1024]{1,0:T(8,128)} %broadcast_select_fusion.refs_8_), channel_id=1, source_target_pairs={{0,48},{1,17},{2,50},{3,19},{4,52},{5,21},{6,54},{7,23},{8,56},{9,... | collective-permute-start | bytes 3145736 | tf_op jit(solution)/shard_map/ppermute | solution.py:30
  152.6 26.0 %collective-permute-start.20 = (f32[256,1024]{1,0:T(8,128)S(1)}, f32[256,1024]{1,0:T(8,128)}, u32[]{:S(2)}, u32[]{:S(2)}) collective-permute-start(f32[256,1024]{1,0:T(8,128)S(1)} %broadcast_select_fusion.1.refs_0_), channel_id=1, source_target_pairs={{0,6},{1,3},{2,4},{3,1},{4,2},{5,7},{6,0},{7,5},{8,14},{9,11},{10,... | collective-permute-start | bytes 3145736 | tf_op jit(solution)/shard_map/ppermute | solution.py:30
  156.3 23.1 %collective-permute-start.17 = (f32[256,1024]{1,0:T(8,128)S(1)}, f32[256,1024]{1,0:T(8,128)S(1)}, u32[]{:S(2)}, u32[]{:S(2)}) collective-permute-start(f32[256,1024]{1,0:T(8,128)S(1)} %broadcast_select_fusion.1.refs_0_), channel_id=1, source_target_pairs={{0,1},{1,0},{2,3},{3,2},{4,5},{5,4},{6,7},{7,6},{8,9},{9,8},{10,11... | collective-permute-start | bytes 3145736 | tf_op jit(solution)/shard_map/ppermute | solution.py:30
  177.0 14.3 %collective-permute-start.23 = (f32[256,1024]{1,0:T(8,128)}, f32[256,1024]{1,0:T(8,128)}, u32[]{:S(2)}, u32[]{:S(2)}) collective-permute-start(f32[256,1024]{1,0:T(8,128)} %collective-permute-done.18.refs_2_), channel_id=1, source_target_pairs={{0,6},{1,3},{2,4},{3,1},{4,2},{5,7},{6,0},{7,5},{8,14},{9,11},{10,... | collective-permute-start | bytes 3145736 | tf_op jit(solution)/shard_map/ppermute | solution.py:30
  177.1 21.1 %collective-permute-start.21 = (f32[256,1024]{1,0:T(8,128)}, f32[256,1024]{1,0:T(8,128)}, u32[]{:S(2)}, u32[]{:S(2)}) collective-permute-start(f32[256,1024]{1,0:T(8,128)} %collective-permute-done.18.refs_2_), channel_id=1, source_target_pairs={{0,1},{1,0},{2,3},{3,2},{4,5},{5,4},{6,7},{7,6},{8,9},{9,8},{10,11... | collective-permute-start | bytes 3145736 | tf_op jit(solution)/shard_map/ppermute | solution.py:30
  178.5 1.0 copy-start.10
  178.5 16.2 %collective-permute-start.16 = (f32[512,512]{1,0:T(8,128)S(1)}, f32[512,512]{1,0:T(8,128)}, u32[]{:S(2)}, u32[]{:S(2)}) collective-permute-start(f32[512,512]{1,0:T(8,128)S(1)} %add.92.pivot_ref), channel_id=1, source_target_pairs={{0,1},{1,0},{2,3},{3,2},{4,5},{5,4},{6,7},{7,6},{8,9},{9,8},{10,11... | collective-permute-start | bytes 3145736 | tf_op jit(solution)/shard_map/ppermute | solution.py:30
  178.6 16.1 %collective-permute-start.22 = (f32[256,1024]{1,0:T(8,128)}, f32[256,1024]{1,0:T(8,128)}, u32[]{:S(2)}, u32[]{:S(2)}) collective-permute-start(f32[256,1024]{1,0:T(8,128)} %collective-permute-done.20.refs_3_), channel_id=1, source_target_pairs={{0,1},{1,0},{2,3},{3,2},{4,5},{5,4},{6,7},{7,6},{8,9},{9,8},{10,11... | collective-permute-start | bytes 3145736 | tf_op jit(solution)/shard_map/ppermute | solution.py:30
  179.5 1.0 copy-start.1
  180.5 17.7 %collective-permute-start.26 = (f32[256,1024]{1,0:T(8,128)}, f32[256,1024]{1,0:T(8,128)}, u32[]{:S(2)}, u32[]{:S(2)}) collective-permute-start(f32[256,1024]{1,0:T(8,128)} %collective-permute-done.19.refs_9_), channel_id=1, source_target_pairs={{0,48},{1,17},{2,50},{3,19},{4,52},{5,21},{6,54},{7,23},{8,56},{9,... | collective-permute-start | bytes 3145736 | tf_op jit(solution)/shard_map/ppermute | solution.py:30
  191.3 6.9 %collective-permute-start.24 = (f32[256,1024]{1,0:T(8,128)}, f32[256,1024]{1,0:T(8,128)}, u32[]{:S(2)}, u32[]{:S(2)}) collective-permute-start(f32[256,1024]{1,0:T(8,128)} %collective-permute-done.23.refs_6_), channel_id=1, source_target_pairs={{0,1},{1,0},{2,3},{3,2},{4,5},{5,4},{6,7},{7,6},{8,9},{9,8},{10,11... | collective-permute-start | bytes 3145736 | tf_op jit(solution)/shard_map/ppermute | solution.py:30
  198.2 1.2 copy-start.2
  226.0 131.4 %all-to-all-start.1 = ((f32[128,128,128]{2,1,0:T(8,128)}), f32[128,128,128]{2,1,0:T(8,128)}, u32[]{:S(2)}, u32[]{:S(2)}) async-start(f32[128,128,128]{2,1,0:T(8,128)} %get-tuple-element.40), calls=%async_computation.1 | async-start | bytes 16777216 | tf_op jit(solution)/shard_map/all_to_all | solution.py:417
  247.4 4.1 %copy-start.6 = (f32[2,512,512]{2,1,0:T(8,128)S(1)}, f32[2,512,512]{2,1,0:T(8,128)}, u32[]{:S(2)}) copy-start(f32[2,512,512]{2,1,0:T(8,128)} %inverse_ref.1) | copy-start | bytes 6291460
  357.5 1.9 copy-start

commit v7 on v6

--- a/solution.py
+++ b/solution.py
@@ -96,7 +96,9 @@
     )
     pivot = jnp.where(corner & first, rows[:half, half:], beside)
     pivot = spread(pivot, 0)
-    one, two, low, columns, rows = lax.optimization_barrier((one, two, low, columns, rows))
+    one, two, low, pivot, columns, rows = lax.optimization_barrier(
+        (one, two, low, pivot, columns, rows)
+    )
 
     three = send(
         jnp.where(y == 0, part(3), one[edge:]),
@@ -406,7 +408,7 @@
     named = owners[None, :] == jnp.arange(devices, dtype=jnp.int32)[:, None]
     labels = jnp.sum(jnp.where(named, slots[None, :] + 1, 0), axis=1).astype(jnp.float32)
     pieces, numbers, layers, heights, pivots, labels = exchange(
-        front[: 2 * width], columns, make_rows, labels.reshape(devices, 1, 1)
+        front, columns, make_rows, labels.reshape(devices, 1, 1)
     )
     markers = labels.reshape(devices).astype(jnp.int32) - 1
     core = col % 2

time: 369 us -> 368 us (level)
  starting transfers between devices: 104 us -> 92 us
  waiting for transfers between devices: 179 us -> 191 us
  local copies, waits for them, and re-layouts: 20.2 us -> 14 us
    ppermute x6, waiting for transfers between devices: 39 us -> 46.9 us  [spread(): return value + lax.ppermute(value, AXES, rounds[number])]
    ppermute x20, starting transfers between devices: 55.7 us -> 49.7 us  [send(): return lax.ppermute(value, AXES, pairs(move, keep))]
    slice x1 -> x0, local copies, waits for them, and re-layouts: 4.94 us -> none  [local(): front[:2 * width]]
    all_to_all x1, starting transfers between devices: 10.5 us -> 6.23 us  [exchange(): labels = lax.all_to_all(labels, AXES, 0, 0, tiled=True)]
where the time goes in v7:
time: 368 us; the launch traced here: 366 us
  waiting for transfers between devices  191 us (52%)
  starting transfers between devices  92 us (25%)
  Pallas kernels  34.8 us (9%)
  other arithmetic  24.4 us (7%)
  local copies, waits for them, and re-layouts  14 us (4%)
  matrix products  9.07 us (2%)
    all_to_all x1, waiting for transfers between devices, local(): arrived = lax.all_to_all(outgoing, AXES, 0, 0, tiled=True)  104 us
    ppermute x20, starting transfers between devices, send(): return lax.ppermute(value, AXES, pairs(move, keep))  49.7 us
    ppermute x6, waiting for transfers between devices, spread(): return value + lax.ppermute(value, AXES, rounds[number])  46.9 us
    ppermute x20, waiting for transfers between devices, send(): return lax.ppermute(value, AXES, pairs(move, keep))  39.5 us
    pallas_call x1, Pallas kernels, update(): pl.pallas_call(update_kernel, grid_spec=pltpu.PrefetchScalarGridSpec(num_...  26.6 us
    all_to_all x1, starting transfers between devices, local(): arrived = lax.all_to_all(outgoing, AXES, 0, 0, tiled=True)  19.1 us
    ppermute x6, starting transfers between devices, spread(): return value + lax.ppermute(value, AXES, rounds[number])  15.7 us
    pallas_call x1, Pallas kernels, extend_add(): pl.pallas_call(add_kernel, grid=(arrived.shape[0] // count,), in_specs=[p...  8.21 us
  transfers between devices with their start and end apart: 29, of which 9 were waited for; matrix products, arithmetic and copies ran while one was open for 11% of the time, Pallas kernels for 0%

profile of v7, /device:TPU:1, one launch (start us, length us, event | category | flops | bytes accessed | tf_op | source)
XLA Modules:
  0.0 366.3 jit_solution(15357631352963884423)
XLA Ops:
  0.6 1.3 slice.77
  1.9 1.3 collective-permute-start.2
  3.2 4.9 %fusion.22 = (f32[512,1024]{1,0:T(8,128)}, f32[512,1024]{1,0:T(8,128)}) fusion(f32[2048,1024]{1,0:T(8,128)} %front_ref.1), kind=kLoop, calls=%fused_computation.37 | loop fusion | bytes 8388608 | tf_op jit(solution)/shard_map/slice | solution.py:72
  8.1 2.0 collective-permute-start.1
  10.1 2.0 collective-permute-start
  12.2 2.0 slice.80
  14.1 0.2 copy-done.6
  14.4 4.2 %fusion.4 = f32[512,1024]{1,0:T(8,128)S(1)} fusion(f32[2048,1024]{1,0:T(8,128)} %front_ref.1, f32[2,512,512]{2,1,0:T(8,128)S(1)} %copy-done.6), kind=kOutput, calls=%fused_computation.7 | convolution fusion | flops 1610612736 | bytes 5242880 | tf_op jit(solution)/shard_map/dot_general | solution.py:430
  18.6 1.7 fusion.1
  20.3 7.3 %collective-permute-start.3 = (f32[512,1024]{1,0:T(8,128)}, f32[512,1024]{1,0:T(8,128)}, u32[]{:S(2)}, u32[]{:S(2)}) collective-permute-start(f32[512,1024]{1,0:T(8,128)} %fusion.1), channel_id=1, source_target_pairs={{0,16},{1,49},{2,18},{3,51},{4,20},{5,53},{6,22},{7,55},{8,24},{9,... | collective-permute-start | bytes 6291464 | tf_op jit(solution)/shard_map/ppermute | solution.py:30
  27.6 0.2 slice_select_fusion
  27.9 4.8 %collective-permute-start.4 = (f32[512,512]{1,0:T(8,128)S(1)}, f32[512,512]{1,0:T(8,128)S(1)}, u32[]{:S(2)}, u32[]{:S(2)}) collective-permute-start(f32[512,512]{1,0:T(8,128)S(1)} %slice_select_fusion), channel_id=1, source_target_pairs={{0,64},{1,9}} | collective-permute-start | bytes 3145736 | tf_op jit(solution)/shard_map/ppermute | solution.py:81
  32.7 0.5 pad_maximum_fusion
  33.3 22.3 %collective-permute-done.4 = f32[512,512]{1,0:T(8,128)S(1)} collective-permute-done((f32[512,512]{1,0:T(8,128)S(1)}, f32[512,512]{1,0:T(8,128)S(1)}, u32[]{:S(2)}, u32[]{:S(2)}) %collective-permute-start.4) | collective-permute-done | bytes 1048608 | tf_op jit(solution)/shard_map/ppermute | solution.py:81
  55.6 0.2 add.84
  55.8 1.4 collective-permute-start.11
  57.2 3.0 select_select_fusion.1
  60.2 2.3 collective-permute-start.8
  62.5 17.1 %collective-permute-done.11 = f32[512,512]{1,0:T(8,128)S(1)} collective-permute-done((f32[512,512]{1,0:T(8,128)S(1)}, f32[512,512]{1,0:T(8,128)S(1)}, u32[]{:S(2)}, u32[]{:S(2)}) %collective-permute-start.11) | collective-permute-done | bytes 1048608 | tf_op jit(solution)/shard_map/ppermute | solution.py:81
  79.6 0.2 add.88
  79.9 1.4 collective-permute-start.12
  81.2 4.5 %slice_select_fusion.2 = (f32[256,1024]{1,0:T(8,128)}, f32[256,1024]{1,0:T(8,128)}, f32[256,1024]{1,0:T(8,128)S(1)}) fusion(f32[512,1024]{1,0:T(8,128)} %collective-permute-done, f32[2048,1024]{1,0:T(8,128)} %front_ref.1, pred[]{:T(512)S(6)} %eq.71, f32[512,1024]{1,0:T(8,128)} %collective-permute-done.1), kind=kLoop, calls=%fused_computation.21 | loop fusion | flops 524288 | bytes 8388609 | tf_op jit(solution)/shard_map/jit(_where)/select_n | solution.py:104
  85.7 1.6 collective-permute-start.5
  87.4 1.7 collective-permute-start.7
  89.1 1.3 collective-permute-start.6
  90.8 0.1 select_reduce_fusion
  90.9 3.7 %collective-permute-done.12 = f32[512,512]{1,0:T(8,128)S(1)} collective-permute-done((f32[512,512]{1,0:T(8,128)S(1)}, f32[512,512]{1,0:T(8,128)S(1)}, u32[]{:S(2)}, u32[]{:S(2)}) %collective-permute-start.12) | collective-permute-done | bytes 1048608 | tf_op jit(solution)/shard_map/ppermute | solution.py:81
  94.6 0.2 add.89
  94.8 1.4 collective-permute-start.13
  96.2 2.6 select_select_fusion
  98.8 3.5 select_select_fusion.2
  102.4 2.3 collective-permute-start.9
  104.7 13.3 %collective-permute-start.10 = (f32[256,1024]{1,0:T(8,128)S(1)}, f32[256,1024]{1,0:T(8,128)}, u32[]{:S(2)}, u32[]{:S(2)}) collective-permute-start(f32[256,1024]{1,0:T(8,128)S(1)} %select_select_fusion), channel_id=1, source_target_pairs={{0,64},{1,65},{2,66},{3,67},{4,68},{5,69},{6,70},{7,71},{8,72},{9,... | collective-permute-start | bytes 3145736 | tf_op jit(solution)/shard_map/ppermute | solution.py:30
  118.0 0.2 add.90
  118.2 2.3 collective-permute-start.14
  120.5 0.7 copy.24
  121.2 6.2 %all-to-all-start = ((f32[128,1,1]{2,1,0:T(1,128)}), f32[128,1,1]{2,1,0:T(1,128)S(1)}, u32[]{:S(2)}, u32[]{:S(2)}) async-start(f32[128,1,1]{2,1,0:T(1,128)} %copy.24), calls=%async_computation | async-start | bytes 131072 | tf_op jit(solution)/shard_map/all_to_all | solution.py:151
  127.4 1.4 broadcast_select_fusion.1.refs_0_
  128.8 14.3 %collective-permute-done.10 = f32[256,1024]{1,0:T(8,128)} collective-permute-done((f32[256,1024]{1,0:T(8,128)S(1)}, f32[256,1024]{1,0:T(8,128)}, u32[]{:S(2)}, u32[]{:S(2)}) %collective-permute-start.10) | collective-permute-done | bytes 1048608 | tf_op jit(solution)/shard_map/ppermute | solution.py:30
  143.1 1.1 broadcast_select_fusion.refs_8_
  144.3 1.4 add.91
  145.9 4.5 %collective-permute-start.15 = (f32[512,512]{1,0:T(8,128)S(1)}, f32[512,512]{1,0:T(8,128)S(1)}, u32[]{:S(2)}, u32[]{:S(2)}) collective-permute-start(f32[512,512]{1,0:T(8,128)S(1)} %add.91), channel_id=1, source_target_pairs={{0,6},{2,4},{8,14},{10,12},{16,22},{18,20},{24,30},{26,28},{32,38}... | collective-permute-start | bytes 3145736 | tf_op jit(solution)/shard_map/ppermute | solution.py:81
  150.6 13.1 %collective-permute-done.19.refs_9_ = f32[256,1024]{1,0:T(8,128)} collective-permute-done((f32[256,1024]{1,0:T(8,128)}, f32[256,1024]{1,0:T(8,128)}, u32[]{:S(2)}, u32[]{:S(2)}) %collective-permute-start.19) | collective-permute-done | bytes 1048608 | tf_op jit(solution)/shard_map/ppermute | solution.py:30
  163.7 12.7 %collective-permute-start.17 = (f32[256,1024]{1,0:T(8,128)S(1)}, f32[256,1024]{1,0:T(8,128)S(1)}, u32[]{:S(2)}, u32[]{:S(2)}) collective-permute-start(f32[256,1024]{1,0:T(8,128)S(1)} %broadcast_select_fusion.1.refs_0_), channel_id=1, source_target_pairs={{0,1},{1,0},{2,3},{3,2},{4,5},{5,4},{6,7},{7,6},{8,9},{9,8},{10,11... | collective-permute-start | bytes 3145736 | tf_op jit(solution)/shard_map/ppermute | solution.py:30
  176.4 3.8 %collective-permute-done.15 = f32[512,512]{1,0:T(8,128)S(1)} collective-permute-done((f32[512,512]{1,0:T(8,128)S(1)}, f32[512,512]{1,0:T(8,128)S(1)}, u32[]{:S(2)}, u32[]{:S(2)}) %collective-permute-start.15) | collective-permute-done | bytes 1048608 | tf_op jit(solution)/shard_map/ppermute | solution.py:81
  180.2 0.2 add.92.pivot_ref
  180.5 0.6 collective-permute-start.16
  181.0 0.1 collective-permute-start.22
  181.2 0.3 copy-done.11
  181.4 1.0 copy-done.1
  182.4 8.3 %collective-permute-done.23.refs_6_ = f32[256,1024]{1,0:T(8,128)} collective-permute-done((f32[256,1024]{1,0:T(8,128)}, f32[256,1024]{1,0:T(8,128)}, u32[]{:S(2)}, u32[]{:S(2)}) %collective-permute-start.23) | collective-permute-done | bytes 1048608 | tf_op jit(solution)/shard_map/ppermute | solution.py:30
  190.7 2.1 collective-permute-start.24
  192.9 3.8 %collective-permute-done.26.refs_11_ = f32[256,1024]{1,0:T(8,128)} collective-permute-done((f32[256,1024]{1,0:T(8,128)}, f32[256,1024]{1,0:T(8,128)}, u32[]{:S(2)}, u32[]{:S(2)}) %collective-permute-start.26) | collective-permute-done | bytes 1048608 | tf_op jit(solution)/shard_map/ppermute | solution.py:30
  196.7 1.2 copy-done.2
  197.9 26.6 %update.1 = (f32[2048,1024]{1,0:T(8,128)}, f32[128,128,128]{2,1,0:T(8,128)}, f32[128,1024]{1,0:T(8,128)S(1)}) custom-call(s32[15]{0:T(128)S(1)} %stack.60.table_ref, s32[16,8]{1,0:T(8,128)S(1)} %copy.25.owner_ref, f32[2048,1024]{1,0:T(8,128)} %front_ref.1, f32[512,512]{1,0:T(8,128)S(1)} %add.92.pivot_ref, f32[512,512]{1,0:T(8,128)} %collective-permute-done.16.other_ref, ...), custom_call_target="tpu_custom_call" | custom-call | flops 17179869184 | bytes 41943040 | tf_op jit(solution)/shard_map/update/pallas_call | solution.py:305
  224.5 19.1 %all-to-all-start.1 = ((f32[128,128,128]{2,1,0:T(8,128)}), f32[128,128,128]{2,1,0:T(8,128)}, u32[]{:S(2)}, u32[]{:S(2)}) async-start(f32[128,128,128]{2,1,0:T(8,128)} %get-tuple-element.42), calls=%async_computation.1 | async-start | bytes 16777216 | tf_op jit(solution)/shard_map/all_to_all | solution.py:419
  243.6 2.4 add_reduce_fusion.slot_ref
  246.0 2.1 fusion.9
  248.1 2.0 fusion.13
  250.1 0.7 fusion.7
  250.9 0.8 pad_maximum_fusion.1
  251.7 104.4 %all-to-all-done.1.arrived_ref = f32[128,128,128]{2,1,0:T(8,128)} async-done(((f32[128,128,128]{2,1,0:T(8,128)}), f32[128,128,128]{2,1,0:T(8,128)}, u32[]{:S(2)}, u32[]{:S(2)}) %all-to-all-start.1) | async-done | bytes 8388640 | tf_op jit(solution)/shard_map/all_to_all | solution.py:419
  356.1 1.9 copy-done
  357.9 8.2 %extend_add.1 = f32[48,128,128]{2,1,0:T(8,128)} custom-call(s32[128]{0:T(128)S(1)} %add_reduce_fusion.slot_ref, f32[48,128,128]{2,1,0:T(8,128)S(1)} %copy-done, f32[128,128,128]{2,1,0:T(8,128)} %all-to-all-done.1.arrived_ref), custom_call_target="tpu_custom_call" | custom-call | flops 2097152 | bytes 14680064 | tf_op jit(solution)/shard_map/extend_add/pallas_call | solution.py:372
  (53 shorter events, 0.9 us)
Async XLA Ops:
  1.9 10.2 %collective-permute-start.2 = (f32[512,512]{1,0:T(8,128)S(1)}, f32[512,512]{1,0:T(8,128)S(1)}, u32[]{:S(2)}, u32[]{:S(2)}) collective-permute-start(f32[512,512]{1,0:T(8,128)S(1)} %slice.77), channel_id=1, source_target_pairs={{0,1}} | collective-permute-start | bytes 3145736 | tf_op jit(solution)/shard_map/ppermute | solution.py:86
  8.1 47.7 %collective-permute-start.1 = (f32[512,1024]{1,0:T(8,128)}, f32[512,1024]{1,0:T(8,128)}, u32[]{:S(2)}, u32[]{:S(2)}) collective-permute-start(f32[512,1024]{1,0:T(8,128)} %get-tuple-element.46), channel_id=1, source_target_pairs={{0,7},{16,23},{32,39},{48,55},{64,71},{80,87},{96,103},{112,119}} | collective-permute-start | bytes 6291464 | tf_op jit(solution)/shard_map/ppermute | solution.py:30
  10.1 45.7 %collective-permute-start = (f32[512,1024]{1,0:T(8,128)}, f32[512,1024]{1,0:T(8,128)}, u32[]{:S(2)}, u32[]{:S(2)}) collective-permute-start(f32[512,1024]{1,0:T(8,128)} %get-tuple-element.47), channel_id=1, source_target_pairs={{0,2},{16,18},{32,34},{48,50},{64,66},{80,82},{96,98},{112,114}} | collective-permute-start | bytes 6291464 | tf_op jit(solution)/shard_map/ppermute | solution.py:30
  12.1 2.2 copy-start.6
  14.4 4.2 %copy-start.3 = (f32[512,1024]{1,0:T(8,128)}, f32[512,1024]{1,0:T(8,128)S(1)}, u32[]{:S(2)}) copy-start(f32[512,1024]{1,0:T(8,128)S(1)} %slice.80) | copy-start | bytes 6291460
  20.3 35.5 %collective-permute-start.3 = (f32[512,1024]{1,0:T(8,128)}, f32[512,1024]{1,0:T(8,128)}, u32[]{:S(2)}, u32[]{:S(2)}) collective-permute-start(f32[512,1024]{1,0:T(8,128)} %fusion.1), channel_id=1, source_target_pairs={{0,16},{1,49},{2,18},{3,51},{4,20},{5,53},{6,22},{7,55},{8,24},{9,... | collective-permute-start | bytes 6291464 | tf_op jit(solution)/shard_map/ppermute | solution.py:30
  27.6 5.1 %copy-start.4 = (f32[512,1024]{1,0:T(8,128)S(1)}, f32[512,1024]{1,0:T(8,128)}, u32[]{:S(2)}) copy-start(f32[512,1024]{1,0:T(8,128)} %copy-done.3) | copy-start | bytes 6291460
  27.9 27.7 %collective-permute-start.4 = (f32[512,512]{1,0:T(8,128)S(1)}, f32[512,512]{1,0:T(8,128)S(1)}, u32[]{:S(2)}, u32[]{:S(2)}) collective-permute-start(f32[512,512]{1,0:T(8,128)S(1)} %slice_select_fusion), channel_id=1, source_target_pairs={{0,64},{1,9}} | collective-permute-start | bytes 3145736 | tf_op jit(solution)/shard_map/ppermute | solution.py:81
  33.3 27.0 %copy-start.5 = (f32[1024,1024]{1,0:T(8,128)}, f32[1024,1024]{1,0:T(8,128)S(1)}, u32[]{:S(2)}) copy-start(f32[1024,1024]{1,0:T(8,128)S(1)} %pad_maximum_fusion) | copy-start | bytes 12582916
  55.8 23.8 %collective-permute-start.11 = (f32[512,512]{1,0:T(8,128)S(1)}, f32[512,512]{1,0:T(8,128)S(1)}, u32[]{:S(2)}, u32[]{:S(2)}) collective-permute-start(f32[512,512]{1,0:T(8,128)S(1)} %add.84), channel_id=1, source_target_pairs={{0,8},{64,72},{1,65},{9,73}} | collective-permute-start | bytes 3145736 | tf_op jit(solution)/shard_map/ppermute | solution.py:81
  60.2 36.0 %collective-permute-start.8 = (f32[256,1024]{1,0:T(8,128)}, f32[256,1024]{1,0:T(8,128)}, u32[]{:S(2)}, u32[]{:S(2)}) collective-permute-start(f32[256,1024]{1,0:T(8,128)} %select_select_fusion.1), channel_id=1, source_target_pairs={{0,48},{1,17},{2,50},{3,19},{4,52},{5,21},{6,54},{7,23},{8,56},{9,... | collective-permute-start | bytes 3145736 | tf_op jit(solution)/shard_map/ppermute | solution.py:30
  79.8 10.6 %copy-start.10 = (s32[16,8]{0,1:T(8,128)S(1)}, s32[16,8]{0,1:T(8,128)}, u32[]{:S(2)}) copy-start(s32[16,8]{0,1:T(8,128)} %param.8) | copy-start | bytes 1540
  79.8 10.8 %copy-start.9 = (s32[16,8]{0,1:T(8,128)S(1)}, s32[16,8]{0,1:T(8,128)}, u32[]{:S(2)}) copy-start(s32[16,8]{0,1:T(8,128)} %param.7) | copy-start | bytes 1540
  79.9 14.8 %collective-permute-start.12 = (f32[512,512]{1,0:T(8,128)S(1)}, f32[512,512]{1,0:T(8,128)S(1)}, u32[]{:S(2)}, u32[]{:S(2)}) collective-permute-start(f32[512,512]{1,0:T(8,128)S(1)} %add.88), channel_id=1, source_target_pairs={{0,16},{8,24},{64,80},{72,88},{1,3},{9,11},{65,67},{73,75}} | collective-permute-start | bytes 3145736 | tf_op jit(solution)/shard_map/ppermute | solution.py:81
  85.7 13.1 %collective-permute-start.5 = (f32[256,1024]{1,0:T(8,128)}, f32[256,1024]{1,0:T(8,128)}, u32[]{:S(2)}, u32[]{:S(2)}) collective-permute-start(f32[256,1024]{1,0:T(8,128)} %get-tuple-element.43), channel_id=1, source_target_pairs={{0,6},{2,4},{16,22},{18,20},{32,38},{34,36},{48,54},{50,52},{64,70... | collective-permute-start | bytes 3145736 | tf_op jit(solution)/shard_map/ppermute | solution.py:30
  87.4 11.4 %collective-permute-start.7 = (f32[256,1024]{1,0:T(8,128)}, f32[256,1024]{1,0:T(8,128)}, u32[]{:S(2)}, u32[]{:S(2)}) collective-permute-start(f32[256,1024]{1,0:T(8,128)} %get-tuple-element.44), channel_id=1, source_target_pairs={{0,3},{7,5},{16,19},{23,21},{32,35},{39,37},{48,51},{55,53},{64,67... | collective-permute-start | bytes 3145736 | tf_op jit(solution)/shard_map/ppermute | solution.py:30
  89.1 9.7 %collective-permute-start.6 = (f32[256,1024]{1,0:T(8,128)S(1)}, f32[256,1024]{1,0:T(8,128)}, u32[]{:S(2)}, u32[]{:S(2)}) collective-permute-start(f32[256,1024]{1,0:T(8,128)S(1)} %get-tuple-element.45), channel_id=1, source_target_pairs={{0,1},{16,17},{32,33},{48,49},{64,65},{80,81},{96,97},{112,113}} | collective-permute-start | bytes 3145736 | tf_op jit(solution)/shard_map/ppermute | solution.py:30
  94.8 23.1 %collective-permute-start.13 = (f32[512,512]{1,0:T(8,128)S(1)}, f32[512,512]{1,0:T(8,128)S(1)}, u32[]{:S(2)}, u32[]{:S(2)}) collective-permute-start(f32[512,512]{1,0:T(8,128)S(1)} %add.89), channel_id=1, source_target_pairs={{0,48},{8,56},{16,32},{24,40},{64,112},{72,120},{80,96},{88,104},{... | collective-permute-start | bytes 3145736 | tf_op jit(solution)/shard_map/ppermute | solution.py:81
  102.4 25.1 %copy-start.8 = (f32[256,1024]{1,0:T(8,128)}, f32[256,1024]{1,0:T(8,128)S(1)}, u32[]{:S(2)}) copy-start(f32[256,1024]{1,0:T(8,128)S(1)} %select_select_fusion.2) | copy-start | bytes 3145732
  102.4 25.1 %collective-permute-start.9 = (f32[256,1024]{1,0:T(8,128)S(1)}, f32[256,1024]{1,0:T(8,128)}, u32[]{:S(2)}, u32[]{:S(2)}) collective-permute-start(f32[256,1024]{1,0:T(8,128)S(1)} %select_select_fusion.2), channel_id=1, source_target_pairs={{0,8},{1,9},{2,10},{3,11},{4,12},{5,13},{6,14},{7,15},{16,24},{17,... | collective-permute-start | bytes 3145736 | tf_op jit(solution)/shard_map/ppermute | solution.py:30
  104.7 38.5 %collective-permute-start.10 = (f32[256,1024]{1,0:T(8,128)S(1)}, f32[256,1024]{1,0:T(8,128)}, u32[]{:S(2)}, u32[]{:S(2)}) collective-permute-start(f32[256,1024]{1,0:T(8,128)S(1)} %select_select_fusion), channel_id=1, source_target_pairs={{0,64},{1,65},{2,66},{3,67},{4,68},{5,69},{6,70},{7,71},{8,72},{9,... | collective-permute-start | bytes 3145736 | tf_op jit(solution)/shard_map/ppermute | solution.py:30
  118.2 26.1 %collective-permute-start.14 = (f32[512,512]{1,0:T(8,128)S(1)}, f32[512,512]{1,0:T(8,128)}, u32[]{:S(2)}, u32[]{:S(2)}) collective-permute-start(f32[512,512]{1,0:T(8,128)S(1)} %add.90), channel_id=1, source_target_pairs={{0,2},{8,10},{16,18},{24,26},{32,34},{40,42},{48,50},{56,58},{64,6... | collective-permute-start | bytes 3145736 | tf_op jit(solution)/shard_map/ppermute | solution.py:81
  121.2 24.5 %all-to-all-start = ((f32[128,1,1]{2,1,0:T(1,128)}), f32[128,1,1]{2,1,0:T(1,128)S(1)}, u32[]{:S(2)}, u32[]{:S(2)}) async-start(f32[128,1,1]{2,1,0:T(1,128)} %copy.24), calls=%async_computation | async-start | bytes 131072 | tf_op jit(solution)/shard_map/all_to_all | solution.py:151
  145.7 18.0 %collective-permute-start.19 = (f32[256,1024]{1,0:T(8,128)}, f32[256,1024]{1,0:T(8,128)}, u32[]{:S(2)}, u32[]{:S(2)}) collective-permute-start(f32[256,1024]{1,0:T(8,128)} %broadcast_select_fusion.refs_8_), channel_id=1, source_target_pairs={{0,16},{1,49},{2,18},{3,51},{4,20},{5,53},{6,22},{7,55},{8,24},{9,... | collective-permute-start | bytes 3145736 | tf_op jit(solution)/shard_map/ppermute | solution.py:30
  145.8 30.6 %collective-permute-start.18 = (f32[256,1024]{1,0:T(8,128)S(1)}, f32[256,1024]{1,0:T(8,128)}, u32[]{:S(2)}, u32[]{:S(2)}) collective-permute-start(f32[256,1024]{1,0:T(8,128)S(1)} %broadcast_select_fusion.1.refs_0_), channel_id=1, source_target_pairs={{0,2},{1,7},{2,0},{3,5},{4,6},{5,3},{6,4},{7,1},{8,10},{9,15},{10,... | collective-permute-start | bytes 3145736 | tf_op jit(solution)/shard_map/ppermute | solution.py:30
  145.9 34.3 %collective-permute-start.15 = (f32[512,512]{1,0:T(8,128)S(1)}, f32[512,512]{1,0:T(8,128)S(1)}, u32[]{:S(2)}, u32[]{:S(2)}) collective-permute-start(f32[512,512]{1,0:T(8,128)S(1)} %add.91), channel_id=1, source_target_pairs={{0,6},{2,4},{8,14},{10,12},{16,22},{18,20},{24,30},{26,28},{32,38}... | collective-permute-start | bytes 3145736 | tf_op jit(solution)/shard_map/ppermute | solution.py:81
  150.4 30.0 %collective-permute-start.25 = (f32[256,1024]{1,0:T(8,128)}, f32[256,1024]{1,0:T(8,128)S(1)}, u32[]{:S(2)}, u32[]{:S(2)}) collective-permute-start(f32[256,1024]{1,0:T(8,128)} %broadcast_select_fusion.refs_8_), channel_id=1, source_target_pairs={{0,48},{1,17},{2,50},{3,19},{4,52},{5,21},{6,54},{7,23},{8,56},{9,... | collective-permute-start | bytes 3145736 | tf_op jit(solution)/shard_map/ppermute | solution.py:30
  150.5 30.5 %collective-permute-start.20 = (f32[256,1024]{1,0:T(8,128)S(1)}, f32[256,1024]{1,0:T(8,128)}, u32[]{:S(2)}, u32[]{:S(2)}) collective-permute-start(f32[256,1024]{1,0:T(8,128)S(1)} %broadcast_select_fusion.1.refs_0_), channel_id=1, source_target_pairs={{0,6},{1,3},{2,4},{3,1},{4,2},{5,7},{6,0},{7,5},{8,14},{9,11},{10,... | collective-permute-start | bytes 3145736 | tf_op jit(solution)/shard_map/ppermute | solution.py:30
  163.7 17.5 %collective-permute-start.17 = (f32[256,1024]{1,0:T(8,128)S(1)}, f32[256,1024]{1,0:T(8,128)S(1)}, u32[]{:S(2)}, u32[]{:S(2)}) collective-permute-start(f32[256,1024]{1,0:T(8,128)S(1)} %broadcast_select_fusion.1.refs_0_), channel_id=1, source_target_pairs={{0,1},{1,0},{2,3},{3,2},{4,5},{5,4},{6,7},{7,6},{8,9},{9,8},{10,11... | collective-permute-start | bytes 3145736 | tf_op jit(solution)/shard_map/ppermute | solution.py:30
  176.4 14.3 %collective-permute-start.23 = (f32[256,1024]{1,0:T(8,128)}, f32[256,1024]{1,0:T(8,128)}, u32[]{:S(2)}, u32[]{:S(2)}) collective-permute-start(f32[256,1024]{1,0:T(8,128)} %collective-permute-done.18.refs_2_), channel_id=1, source_target_pairs={{0,6},{1,3},{2,4},{3,1},{4,2},{5,7},{6,0},{7,5},{8,14},{9,11},{10,... | collective-permute-start | bytes 3145736 | tf_op jit(solution)/shard_map/ppermute | solution.py:30
  180.2 16.4 %collective-permute-start.21 = (f32[256,1024]{1,0:T(8,128)}, f32[256,1024]{1,0:T(8,128)}, u32[]{:S(2)}, u32[]{:S(2)}) collective-permute-start(f32[256,1024]{1,0:T(8,128)} %collective-permute-done.18.refs_2_), channel_id=1, source_target_pairs={{0,1},{1,0},{2,3},{3,2},{4,5},{5,4},{6,7},{7,6},{8,9},{9,8},{10,11... | collective-permute-start | bytes 3145736 | tf_op jit(solution)/shard_map/ppermute | solution.py:30
  180.4 1.0 copy-start.11
  180.5 12.4 %collective-permute-start.16 = (f32[512,512]{1,0:T(8,128)S(1)}, f32[512,512]{1,0:T(8,128)}, u32[]{:S(2)}, u32[]{:S(2)}) collective-permute-start(f32[512,512]{1,0:T(8,128)S(1)} %add.92.pivot_ref), channel_id=1, source_target_pairs={{0,1},{1,0},{2,3},{3,2},{4,5},{5,4},{6,7},{7,6},{8,9},{9,8},{10,11... | collective-permute-start | bytes 3145736 | tf_op jit(solution)/shard_map/ppermute | solution.py:30
  181.0 11.8 %collective-permute-start.22 = (f32[256,1024]{1,0:T(8,128)}, f32[256,1024]{1,0:T(8,128)}, u32[]{:S(2)}, u32[]{:S(2)}) collective-permute-start(f32[256,1024]{1,0:T(8,128)} %collective-permute-done.20.refs_3_), channel_id=1, source_target_pairs={{0,1},{1,0},{2,3},{3,2},{4,5},{5,4},{6,7},{7,6},{8,9},{9,8},{10,11... | collective-permute-start | bytes 3145736 | tf_op jit(solution)/shard_map/ppermute | solution.py:30
  181.4 1.0 copy-start.1
  182.4 14.3 %collective-permute-start.26 = (f32[256,1024]{1,0:T(8,128)}, f32[256,1024]{1,0:T(8,128)}, u32[]{:S(2)}, u32[]{:S(2)}) collective-permute-start(f32[256,1024]{1,0:T(8,128)} %collective-permute-done.19.refs_9_), channel_id=1, source_target_pairs={{0,48},{1,17},{2,50},{3,19},{4,52},{5,21},{6,54},{7,23},{8,56},{9,... | collective-permute-start | bytes 3145736 | tf_op jit(solution)/shard_map/ppermute | solution.py:30
  190.7 6.0 %collective-permute-start.24 = (f32[256,1024]{1,0:T(8,128)}, f32[256,1024]{1,0:T(8,128)}, u32[]{:S(2)}, u32[]{:S(2)}) collective-permute-start(f32[256,1024]{1,0:T(8,128)} %collective-permute-done.23.refs_6_), channel_id=1, source_target_pairs={{0,1},{1,0},{2,3},{3,2},{4,5},{5,4},{6,7},{7,6},{8,9},{9,8},{10,11... | collective-permute-start | bytes 3145736 | tf_op jit(solution)/shard_map/ppermute | solution.py:30
  196.7 1.2 copy-start.2
  224.5 131.6 %all-to-all-start.1 = ((f32[128,128,128]{2,1,0:T(8,128)}), f32[128,128,128]{2,1,0:T(8,128)}, u32[]{:S(2)}, u32[]{:S(2)}) async-start(f32[128,128,128]{2,1,0:T(8,128)} %get-tuple-element.42), calls=%async_computation.1 | async-start | bytes 16777216 | tf_op jit(solution)/shard_map/all_to_all | solution.py:419
  246.0 4.1 %copy-start.7 = (f32[2,512,512]{2,1,0:T(8,128)S(1)}, f32[2,512,512]{2,1,0:T(8,128)}, u32[]{:S(2)}) copy-start(f32[2,512,512]{2,1,0:T(8,128)} %inverse_ref.1) | copy-start | bytes 6291460
  356.1 1.9 copy-start

commit v8 on v7

--- a/solution.py
+++ b/solution.py
@@ -135,7 +135,7 @@
             jnp.where((core == 1) & (z == 3), low[lift:], high),
         ),
     )
-    column, row, labels = lax.optimization_barrier((column, row, labels))
+    column, row, pivot, labels = lax.optimization_barrier((column, row, pivot, labels))
 
     column_across = send(
         column,
@@ -153,7 +153,7 @@
     pivot = spread(pivot, 4)
     column = jnp.where(xh == 0, column, column_across)
     row = jnp.where(xl == 0, row, row_across)
-    column, row, pivot, labels = lax.optimization_barrier((column, row, pivot, labels))
+    column, row, labels = lax.optimization_barrier((column, row, labels))
 
     def around(value, step):
         return send(

time: 368 us -> 359 us (0.976)
  starting transfers between devices: 92 us -> 87 us
    ppermute x20, waiting for transfers between devices: 39.5 us -> 28.1 us  [send(): return lax.ppermute(value, AXES, pairs(move, keep))]
    all_to_all x1, starting transfers between devices: 19.1 us -> 10.3 us  [local(): arrived = lax.all_to_all(outgoing, AXES, 0, 0, tiled=True)]
    ppermute x6, waiting for transfers between devices: 46.9 us -> 55.2 us  [spread(): return value + lax.ppermute(value, AXES, rounds[number])]
    ppermute x20, starting transfers between devices: 49.7 us -> 54.7 us  [send(): return lax.ppermute(value, AXES, pairs(move, keep))]
  transfers between devices with their start and end apart: 29 -> 29, of which waited for: 9 -> 10; matrix products, arithmetic and copies ran while one was open for 11% -> 10% of each run, Pallas kernels for 0% -> 0%
where the time goes in v8:
time: 359 us; the launch traced here: 358 us
  waiting for transfers between devices  188 us (52%)
  starting transfers between devices  87 us (24%)
  Pallas kernels  34.8 us (10%)
  other arithmetic  24.4 us (7%)
  local copies, waits for them, and re-layouts  13.7 us (4%)
  matrix products  9.08 us (3%)
    all_to_all x1, waiting for transfers between devices, local(): arrived = lax.all_to_all(outgoing, AXES, 0, 0, tiled=True)  104 us
    ppermute x6, waiting for transfers between devices, spread(): return value + lax.ppermute(value, AXES, rounds[number])  55.2 us
    ppermute x20, starting transfers between devices, send(): return lax.ppermute(value, AXES, pairs(move, keep))  54.7 us
    ppermute x20, waiting for transfers between devices, send(): return lax.ppermute(value, AXES, pairs(move, keep))  28.1 us
    pallas_call x1, Pallas kernels, update(): pl.pallas_call(update_kernel, grid_spec=pltpu.PrefetchScalarGridSpec(num_...  26.6 us
    ppermute x6, starting transfers between devices, spread(): return value + lax.ppermute(value, AXES, rounds[number])  12.5 us
    all_to_all x1, starting transfers between devices, local(): arrived = lax.all_to_all(outgoing, AXES, 0, 0, tiled=True)  10.3 us
    all_to_all x1, starting transfers between devices, exchange(): labels = lax.all_to_all(labels, AXES, 0, 0, tiled=True)  8.22 us
  transfers between devices with their start and end apart: 29, of which 10 were waited for; matrix products, arithmetic and copies ran while one was open for 10% of the time, Pallas kernels for 0%

profile of v8, /device:TPU:1, one launch (start us, length us, event | category | flops | bytes accessed | tf_op | source)
XLA Modules:
  0.0 358.0 jit_solution(5910744641347407308)
XLA Ops:
  0.6 1.3 slice.77
  1.9 1.3 collective-permute-start.2
  3.2 4.9 %fusion.22 = (f32[512,1024]{1,0:T(8,128)}, f32[512,1024]{1,0:T(8,128)}) fusion(f32[2048,1024]{1,0:T(8,128)} %front_ref.1), kind=kLoop, calls=%fused_computation.37 | loop fusion | bytes 8388608 | tf_op jit(solution)/shard_map/slice | solution.py:72
  8.1 2.0 collective-permute-start.1
  10.1 2.0 collective-permute-start
  12.2 2.0 slice.80
  14.1 0.2 copy-done.6
  14.4 4.2 %fusion.4 = f32[512,1024]{1,0:T(8,128)S(1)} fusion(f32[2048,1024]{1,0:T(8,128)} %front_ref.1, f32[2,512,512]{2,1,0:T(8,128)S(1)} %copy-done.6), kind=kOutput, calls=%fused_computation.7 | convolution fusion | flops 1610612736 | bytes 5242880 | tf_op jit(solution)/shard_map/dot_general | solution.py:430
  18.6 1.7 fusion.1
  20.3 7.3 %collective-permute-start.3 = (f32[512,1024]{1,0:T(8,128)}, f32[512,1024]{1,0:T(8,128)}, u32[]{:S(2)}, u32[]{:S(2)}) collective-permute-start(f32[512,1024]{1,0:T(8,128)} %fusion.1), channel_id=1, source_target_pairs={{0,16},{1,49},{2,18},{3,51},{4,20},{5,53},{6,22},{7,55},{8,24},{9,... | collective-permute-start | bytes 6291464 | tf_op jit(solution)/shard_map/ppermute | solution.py:30
  27.6 0.2 slice_select_fusion
  27.9 4.8 %collective-permute-start.4 = (f32[512,512]{1,0:T(8,128)S(1)}, f32[512,512]{1,0:T(8,128)S(1)}, u32[]{:S(2)}, u32[]{:S(2)}) collective-permute-start(f32[512,512]{1,0:T(8,128)S(1)} %slice_select_fusion), channel_id=1, source_target_pairs={{0,64},{1,9}} | collective-permute-start | bytes 3145736 | tf_op jit(solution)/shard_map/ppermute | solution.py:81
  32.7 0.5 pad_maximum_fusion
  33.3 22.3 %collective-permute-done.4 = f32[512,512]{1,0:T(8,128)S(1)} collective-permute-done((f32[512,512]{1,0:T(8,128)S(1)}, f32[512,512]{1,0:T(8,128)S(1)}, u32[]{:S(2)}, u32[]{:S(2)}) %collective-permute-start.4) | collective-permute-done | bytes 1048608 | tf_op jit(solution)/shard_map/ppermute | solution.py:81
  55.6 0.2 add.84
  55.8 3.0 select_select_fusion.1
  58.9 2.4 collective-permute-start.8
  61.3 1.3 collective-permute-start.9
  62.6 4.5 %slice_select_fusion.2 = (f32[256,1024]{1,0:T(8,128)}, f32[256,1024]{1,0:T(8,128)}, f32[256,1024]{1,0:T(8,128)S(1)}) fusion(f32[512,1024]{1,0:T(8,128)} %collective-permute-done, f32[2048,1024]{1,0:T(8,128)} %front_ref.1, pred[]{:T(512)S(6)} %eq.70, f32[512,1024]{1,0:T(8,128)} %collective-permute-done.1), kind=kLoop, calls=%fused_computation.21 | loop fusion | flops 524288 | bytes 8388609 | tf_op jit(solution)/shard_map/jit(_where)/select_n | solution.py:104
  67.1 1.6 collective-permute-start.5
  68.8 1.7 collective-permute-start.7
  70.5 1.3 collective-permute-start.6
  72.3 12.7 %collective-permute-done.9 = f32[512,512]{1,0:T(8,128)S(1)} collective-permute-done((f32[512,512]{1,0:T(8,128)S(1)}, f32[512,512]{1,0:T(8,128)S(1)}, u32[]{:S(2)}, u32[]{:S(2)}) %collective-permute-start.9) | collective-permute-done | bytes 1048608 | tf_op jit(solution)/shard_map/ppermute | solution.py:81
  85.0 0.2 add.85
  85.2 2.6 select_select_fusion
  87.9 3.5 select_select_fusion.2
  91.4 1.4 collective-permute-start.10
  92.8 2.3 collective-permute-start.15
  95.1 4.8 %collective-permute-start.16 = (f32[256,1024]{1,0:T(8,128)S(1)}, f32[256,1024]{1,0:T(8,128)}, u32[]{:S(2)}, u32[]{:S(2)}) collective-permute-start(f32[256,1024]{1,0:T(8,128)S(1)} %select_select_fusion), channel_id=1, source_target_pairs={{0,64},{1,65},{2,66},{3,67},{4,68},{5,69},{6,70},{7,71},{8,72},{9,... | collective-permute-start | bytes 3145736 | tf_op jit(solution)/shard_map/ppermute | solution.py:30
  99.8 4.6 %collective-permute-done.10 = f32[512,512]{1,0:T(8,128)S(1)} collective-permute-done((f32[512,512]{1,0:T(8,128)S(1)}, f32[512,512]{1,0:T(8,128)S(1)}, u32[]{:S(2)}, u32[]{:S(2)}) %collective-permute-start.10) | collective-permute-done | bytes 1048608 | tf_op jit(solution)/shard_map/ppermute | solution.py:81
  104.4 0.2 add.89
  104.6 2.3 collective-permute-start.11
  106.9 0.7 copy.24
  107.7 8.2 %all-to-all-start = ((f32[128,1,1]{2,1,0:T(1,128)}), f32[128,1,1]{2,1,0:T(1,128)S(1)}, u32[]{:S(2)}, u32[]{:S(2)}) async-start(f32[128,1,1]{2,1,0:T(1,128)} %copy.24), calls=%async_computation | async-start | bytes 131072 | tf_op jit(solution)/shard_map/all_to_all | solution.py:151
  115.9 1.4 broadcast_select_fusion.1.refs_0_
  117.3 16.5 %collective-permute-done.16 = f32[256,1024]{1,0:T(8,128)} collective-permute-done((f32[256,1024]{1,0:T(8,128)S(1)}, f32[256,1024]{1,0:T(8,128)}, u32[]{:S(2)}, u32[]{:S(2)}) %collective-permute-start.16) | collective-permute-done | bytes 1048608 | tf_op jit(solution)/shard_map/ppermute | solution.py:30
  133.8 1.1 broadcast_select_fusion.refs_8_
  134.9 1.4 add.90
  136.3 1.4 collective-permute-start.12
  137.9 15.6 %collective-permute-done.12 = f32[512,512]{1,0:T(8,128)S(1)} collective-permute-done((f32[512,512]{1,0:T(8,128)S(1)}, f32[512,512]{1,0:T(8,128)S(1)}, u32[]{:S(2)}, u32[]{:S(2)}) %collective-permute-start.12) | collective-permute-done | bytes 1048608 | tf_op jit(solution)/shard_map/ppermute | solution.py:81
  153.7 1.4 collective-permute-start.13
  155.1 2.4 collective-permute-start.25
  157.5 1.5 collective-permute-start.23
  158.9 18.0 %collective-permute-start.17 = (f32[256,1024]{1,0:T(8,128)S(1)}, f32[256,1024]{1,0:T(8,128)S(1)}, u32[]{:S(2)}, u32[]{:S(2)}) collective-permute-start(f32[256,1024]{1,0:T(8,128)S(1)} %broadcast_select_fusion.1.refs_0_), channel_id=1, source_target_pairs={{0,1},{1,0},{2,3},{3,2},{4,5},{5,4},{6,7},{7,6},{8,9},{9,8},{10,11... | collective-permute-start | bytes 3145736 | tf_op jit(solution)/shard_map/ppermute | solution.py:30
  176.9 0.3 collective-permute-start.21
  177.1 0.2 add.92.pivot_ref
  177.5 1.0 collective-permute-done.20.refs_3_
  178.5 3.5 collective-permute-start.22
  182.0 7.8 %collective-permute-done.23.refs_6_ = f32[256,1024]{1,0:T(8,128)} collective-permute-done((f32[256,1024]{1,0:T(8,128)}, f32[256,1024]{1,0:T(8,128)}, u32[]{:S(2)}, u32[]{:S(2)}) %collective-permute-start.23) | collective-permute-done | bytes 1048608 | tf_op jit(solution)/shard_map/ppermute | solution.py:30
  189.8 3.4 collective-permute-start.24
  193.2 1.0 copy-done.1
  194.3 1.5 collective-permute-done.24.refs_7_
  195.8 1.3 collective-permute-done.14.other_ref
  197.1 1.2 copy-done.2
  198.3 26.6 %update.1 = (f32[2048,1024]{1,0:T(8,128)}, f32[128,128,128]{2,1,0:T(8,128)}, f32[128,1024]{1,0:T(8,128)S(1)}) custom-call(s32[15]{0:T(128)S(1)} %stack.60.table_ref, s32[16,8]{1,0:T(8,128)S(1)} %copy.25.owner_ref, f32[2048,1024]{1,0:T(8,128)} %front_ref.1, f32[512,512]{1,0:T(8,128)S(1)} %add.92.pivot_ref, f32[512,512]{1,0:T(8,128)} %collective-permute-done.14.other_ref, ...), custom_call_target="tpu_custom_call" | custom-call | flops 17179869184 | bytes 41943040 | tf_op jit(solution)/shard_map/update/pallas_call | solution.py:305
  225.0 10.3 %all-to-all-start.1 = ((f32[128,128,128]{2,1,0:T(8,128)}), f32[128,128,128]{2,1,0:T(8,128)}, u32[]{:S(2)}, u32[]{:S(2)}) async-start(f32[128,128,128]{2,1,0:T(8,128)} %get-tuple-element.42), calls=%async_computation.1 | async-start | bytes 16777216 | tf_op jit(solution)/shard_map/all_to_all | solution.py:419
  235.3 2.4 add_reduce_fusion.slot_ref
  237.6 2.1 fusion.9
  239.7 2.0 fusion.13
  241.8 0.7 fusion.7
  242.5 0.8 pad_maximum_fusion.1
  243.4 104.4 %all-to-all-done.1.arrived_ref = f32[128,128,128]{2,1,0:T(8,128)} async-done(((f32[128,128,128]{2,1,0:T(8,128)}), f32[128,128,128]{2,1,0:T(8,128)}, u32[]{:S(2)}, u32[]{:S(2)}) %all-to-all-start.1) | async-done | bytes 8388640 | tf_op jit(solution)/shard_map/all_to_all | solution.py:419
  347.7 1.9 copy-done
  349.6 8.2 %extend_add.1 = f32[48,128,128]{2,1,0:T(8,128)} custom-call(s32[128]{0:T(128)S(1)} %add_reduce_fusion.slot_ref, f32[48,128,128]{2,1,0:T(8,128)S(1)} %copy-done, f32[128,128,128]{2,1,0:T(8,128)} %all-to-all-done.1.arrived_ref), custom_call_target="tpu_custom_call" | custom-call | flops 2097152 | bytes 14680064 | tf_op jit(solution)/shard_map/extend_add/pallas_call | solution.py:372
  (55 shorter events, 1.1 us)
Async XLA Ops:
  1.9 10.2 %collective-permute-start.2 = (f32[512,512]{1,0:T(8,128)S(1)}, f32[512,512]{1,0:T(8,128)S(1)}, u32[]{:S(2)}, u32[]{:S(2)}) collective-permute-start(f32[512,512]{1,0:T(8,128)S(1)} %slice.77), channel_id=1, source_target_pairs={{0,1}} | collective-permute-start | bytes 3145736 | tf_op jit(solution)/shard_map/ppermute | solution.py:86
  8.1 47.7 %collective-permute-start.1 = (f32[512,1024]{1,0:T(8,128)}, f32[512,1024]{1,0:T(8,128)}, u32[]{:S(2)}, u32[]{:S(2)}) collective-permute-start(f32[512,1024]{1,0:T(8,128)} %get-tuple-element.46), channel_id=1, source_target_pairs={{0,7},{16,23},{32,39},{48,55},{64,71},{80,87},{96,103},{112,119}} | collective-permute-start | bytes 6291464 | tf_op jit(solution)/shard_map/ppermute | solution.py:30
  10.1 45.7 %collective-permute-start = (f32[512,1024]{1,0:T(8,128)}, f32[512,1024]{1,0:T(8,128)}, u32[]{:S(2)}, u32[]{:S(2)}) collective-permute-start(f32[512,1024]{1,0:T(8,128)} %get-tuple-element.47), channel_id=1, source_target_pairs={{0,2},{16,18},{32,34},{48,50},{64,66},{80,82},{96,98},{112,114}} | collective-permute-start | bytes 6291464 | tf_op jit(solution)/shard_map/ppermute | solution.py:30
  12.2 2.2 copy-start.6
  14.4 4.2 %copy-start.3 = (f32[512,1024]{1,0:T(8,128)}, f32[512,1024]{1,0:T(8,128)S(1)}, u32[]{:S(2)}) copy-start(f32[512,1024]{1,0:T(8,128)S(1)} %slice.80) | copy-start | bytes 6291460
  20.3 35.5 %collective-permute-start.3 = (f32[512,1024]{1,0:T(8,128)}, f32[512,1024]{1,0:T(8,128)}, u32[]{:S(2)}, u32[]{:S(2)}) collective-permute-start(f32[512,1024]{1,0:T(8,128)} %fusion.1), channel_id=1, source_target_pairs={{0,16},{1,49},{2,18},{3,51},{4,20},{5,53},{6,22},{7,55},{8,24},{9,... | collective-permute-start | bytes 6291464 | tf_op jit(solution)/shard_map/ppermute | solution.py:30
  27.6 5.1 %copy-start.4 = (f32[512,1024]{1,0:T(8,128)S(1)}, f32[512,1024]{1,0:T(8,128)}, u32[]{:S(2)}) copy-start(f32[512,1024]{1,0:T(8,128)} %copy-done.3) | copy-start | bytes 6291460
  27.9 27.7 %collective-permute-start.4 = (f32[512,512]{1,0:T(8,128)S(1)}, f32[512,512]{1,0:T(8,128)S(1)}, u32[]{:S(2)}, u32[]{:S(2)}) collective-permute-start(f32[512,512]{1,0:T(8,128)S(1)} %slice_select_fusion), channel_id=1, source_target_pairs={{0,64},{1,9}} | collective-permute-start | bytes 3145736 | tf_op jit(solution)/shard_map/ppermute | solution.py:81
  33.3 25.6 %copy-start.5 = (f32[1024,1024]{1,0:T(8,128)}, f32[1024,1024]{1,0:T(8,128)S(1)}, u32[]{:S(2)}) copy-start(f32[1024,1024]{1,0:T(8,128)S(1)} %pad_maximum_fusion) | copy-start | bytes 12582916
  58.9 13.0 %copy-start.11 = (s32[16,8]{0,1:T(8,128)S(1)}, s32[16,8]{0,1:T(8,128)}, u32[]{:S(2)}) copy-start(s32[16,8]{0,1:T(8,128)} %param.8) | copy-start | bytes 1540
  58.9 13.1 %copy-start.10 = (s32[16,8]{0,1:T(8,128)S(1)}, s32[16,8]{0,1:T(8,128)}, u32[]{:S(2)}) copy-start(s32[16,8]{0,1:T(8,128)} %param.7) | copy-start | bytes 1540
  58.9 26.4 %collective-permute-start.8 = (f32[256,1024]{1,0:T(8,128)}, f32[256,1024]{1,0:T(8,128)}, u32[]{:S(2)}, u32[]{:S(2)}) collective-permute-start(f32[256,1024]{1,0:T(8,128)} %select_select_fusion.1), channel_id=1, source_target_pairs={{0,48},{1,17},{2,50},{3,19},{4,52},{5,21},{6,54},{7,23},{8,56},{9,... | collective-permute-start | bytes 3145736 | tf_op jit(solution)/shard_map/ppermute | solution.py:30
  61.3 23.8 %collective-permute-start.9 = (f32[512,512]{1,0:T(8,128)S(1)}, f32[512,512]{1,0:T(8,128)S(1)}, u32[]{:S(2)}, u32[]{:S(2)}) collective-permute-start(f32[512,512]{1,0:T(8,128)S(1)} %add.84), channel_id=1, source_target_pairs={{0,8},{64,72},{1,65},{9,73}} | collective-permute-start | bytes 3145736 | tf_op jit(solution)/shard_map/ppermute | solution.py:81
  67.1 20.7 %collective-permute-start.5 = (f32[256,1024]{1,0:T(8,128)}, f32[256,1024]{1,0:T(8,128)}, u32[]{:S(2)}, u32[]{:S(2)}) collective-permute-start(f32[256,1024]{1,0:T(8,128)} %get-tuple-element.43), channel_id=1, source_target_pairs={{0,6},{2,4},{16,22},{18,20},{32,38},{34,36},{48,54},{50,52},{64,70... | collective-permute-start | bytes 3145736 | tf_op jit(solution)/shard_map/ppermute | solution.py:30
  68.8 19.1 %collective-permute-start.7 = (f32[256,1024]{1,0:T(8,128)}, f32[256,1024]{1,0:T(8,128)}, u32[]{:S(2)}, u32[]{:S(2)}) collective-permute-start(f32[256,1024]{1,0:T(8,128)} %get-tuple-element.44), channel_id=1, source_target_pairs={{0,3},{7,5},{16,19},{23,21},{32,35},{39,37},{48,51},{55,53},{64,67... | collective-permute-start | bytes 3145736 | tf_op jit(solution)/shard_map/ppermute | solution.py:30
  70.5 17.4 %collective-permute-start.6 = (f32[256,1024]{1,0:T(8,128)S(1)}, f32[256,1024]{1,0:T(8,128)}, u32[]{:S(2)}, u32[]{:S(2)}) collective-permute-start(f32[256,1024]{1,0:T(8,128)S(1)} %get-tuple-element.45), channel_id=1, source_target_pairs={{0,1},{16,17},{32,33},{48,49},{64,65},{80,81},{96,97},{112,113}} | collective-permute-start | bytes 3145736 | tf_op jit(solution)/shard_map/ppermute | solution.py:30
  91.4 24.5 %copy-start.8 = (f32[256,1024]{1,0:T(8,128)}, f32[256,1024]{1,0:T(8,128)S(1)}, u32[]{:S(2)}) copy-start(f32[256,1024]{1,0:T(8,128)S(1)} %select_select_fusion.2) | copy-start | bytes 3145732
  91.4 13.0 %collective-permute-start.10 = (f32[512,512]{1,0:T(8,128)S(1)}, f32[512,512]{1,0:T(8,128)S(1)}, u32[]{:S(2)}, u32[]{:S(2)}) collective-permute-start(f32[512,512]{1,0:T(8,128)S(1)} %add.85), channel_id=1, source_target_pairs={{0,16},{8,24},{64,80},{72,88},{1,3},{9,11},{65,67},{73,75}} | collective-permute-start | bytes 3145736 | tf_op jit(solution)/shard_map/ppermute | solution.py:81
  92.8 23.1 %collective-permute-start.15 = (f32[256,1024]{1,0:T(8,128)S(1)}, f32[256,1024]{1,0:T(8,128)}, u32[]{:S(2)}, u32[]{:S(2)}) collective-permute-start(f32[256,1024]{1,0:T(8,128)S(1)} %select_select_fusion.2), channel_id=1, source_target_pairs={{0,8},{1,9},{2,10},{3,11},{4,12},{5,13},{6,14},{7,15},{16,24},{17,... | collective-permute-start | bytes 3145736 | tf_op jit(solution)/shard_map/ppermute | solution.py:30
  95.1 38.7 %collective-permute-start.16 = (f32[256,1024]{1,0:T(8,128)S(1)}, f32[256,1024]{1,0:T(8,128)}, u32[]{:S(2)}, u32[]{:S(2)}) collective-permute-start(f32[256,1024]{1,0:T(8,128)S(1)} %select_select_fusion), channel_id=1, source_target_pairs={{0,64},{1,65},{2,66},{3,67},{4,68},{5,69},{6,70},{7,71},{8,72},{9,... | collective-permute-start | bytes 3145736 | tf_op jit(solution)/shard_map/ppermute | solution.py:30
  104.6 30.3 %collective-permute-start.11 = (f32[512,512]{1,0:T(8,128)S(1)}, f32[512,512]{1,0:T(8,128)}, u32[]{:S(2)}, u32[]{:S(2)}) collective-permute-start(f32[512,512]{1,0:T(8,128)S(1)} %add.89), channel_id=1, source_target_pairs={{0,48},{8,56},{16,32},{24,40},{64,112},{72,120},{80,96},{88,104},{... | collective-permute-start | bytes 3145736 | tf_op jit(solution)/shard_map/ppermute | solution.py:81
  107.7 30.0 %all-to-all-start = ((f32[128,1,1]{2,1,0:T(1,128)}), f32[128,1,1]{2,1,0:T(1,128)S(1)}, u32[]{:S(2)}, u32[]{:S(2)}) async-start(f32[128,1,1]{2,1,0:T(1,128)} %copy.24), calls=%async_computation | async-start | bytes 131072 | tf_op jit(solution)/shard_map/all_to_all | solution.py:151
  136.3 17.1 %collective-permute-start.12 = (f32[512,512]{1,0:T(8,128)S(1)}, f32[512,512]{1,0:T(8,128)S(1)}, u32[]{:S(2)}, u32[]{:S(2)}) collective-permute-start(f32[512,512]{1,0:T(8,128)S(1)} %add.90), channel_id=1, source_target_pairs={{0,2},{8,10},{16,18},{24,26},{32,34},{40,42},{48,50},{56,58},{64,6... | collective-permute-start | bytes 3145736 | tf_op jit(solution)/shard_map/ppermute | solution.py:81
  137.7 17.3 %copy-start.9 = (f32[256,1024]{1,0:T(8,128)S(1)}, f32[256,1024]{1,0:T(8,128)}, u32[]{:S(2)}) copy-start(f32[256,1024]{1,0:T(8,128)} %broadcast_select_fusion.refs_8_) | copy-start | bytes 3145732
  137.7 19.7 %collective-permute-start.19 = (f32[256,1024]{1,0:T(8,128)}, f32[256,1024]{1,0:T(8,128)}, u32[]{:S(2)}, u32[]{:S(2)}) collective-permute-start(f32[256,1024]{1,0:T(8,128)} %broadcast_select_fusion.refs_8_), channel_id=1, source_target_pairs={{0,16},{1,49},{2,18},{3,51},{4,20},{5,53},{6,22},{7,55},{8,24},{9,... | collective-permute-start | bytes 3145736 | tf_op jit(solution)/shard_map/ppermute | solution.py:30
  137.8 19.6 %collective-permute-start.18 = (f32[256,1024]{1,0:T(8,128)S(1)}, f32[256,1024]{1,0:T(8,128)}, u32[]{:S(2)}, u32[]{:S(2)}) collective-permute-start(f32[256,1024]{1,0:T(8,128)S(1)} %broadcast_select_fusion.1.refs_0_), channel_id=1, source_target_pairs={{0,2},{1,7},{2,0},{3,5},{4,6},{5,3},{6,4},{7,1},{8,10},{9,15},{10,... | collective-permute-start | bytes 3145736 | tf_op jit(solution)/shard_map/ppermute | solution.py:30
  153.7 23.2 %collective-permute-start.13 = (f32[512,512]{1,0:T(8,128)S(1)}, f32[512,512]{1,0:T(8,128)S(1)}, u32[]{:S(2)}, u32[]{:S(2)}) collective-permute-start(f32[512,512]{1,0:T(8,128)S(1)} %add.91), channel_id=1, source_target_pairs={{0,6},{2,4},{8,14},{10,12},{16,22},{18,20},{24,30},{26,28},{32,38}... | collective-permute-start | bytes 3145736 | tf_op jit(solution)/shard_map/ppermute | solution.py:81
  155.1 22.3 %collective-permute-start.25 = (f32[256,1024]{1,0:T(8,128)S(1)}, f32[256,1024]{1,0:T(8,128)S(1)}, u32[]{:S(2)}, u32[]{:S(2)}) collective-permute-start(f32[256,1024]{1,0:T(8,128)S(1)} %copy-done.9), channel_id=1, source_target_pairs={{0,48},{1,17},{2,50},{3,19},{4,52},{5,21},{6,54},{7,23},{8,56},{9,... | collective-permute-start | bytes 3145736 | tf_op jit(solution)/shard_map/ppermute | solution.py:30
  157.4 21.0 %collective-permute-start.20 = (f32[256,1024]{1,0:T(8,128)S(1)}, f32[256,1024]{1,0:T(8,128)}, u32[]{:S(2)}, u32[]{:S(2)}) collective-permute-start(f32[256,1024]{1,0:T(8,128)S(1)} %broadcast_select_fusion.1.refs_0_), channel_id=1, source_target_pairs={{0,6},{1,3},{2,4},{3,1},{4,2},{5,7},{6,0},{7,5},{8,14},{9,11},{10,... | collective-permute-start | bytes 3145736 | tf_op jit(solution)/shard_map/ppermute | solution.py:30
  157.5 32.4 %collective-permute-start.23 = (f32[256,1024]{1,0:T(8,128)}, f32[256,1024]{1,0:T(8,128)}, u32[]{:S(2)}, u32[]{:S(2)}) collective-permute-start(f32[256,1024]{1,0:T(8,128)} %collective-permute-done.18.refs_2_), channel_id=1, source_target_pairs={{0,6},{1,3},{2,4},{3,1},{4,2},{5,7},{6,0},{7,5},{8,14},{9,11},{10,... | collective-permute-start | bytes 3145736 | tf_op jit(solution)/shard_map/ppermute | solution.py:30
  158.9 34.3 %collective-permute-start.17 = (f32[256,1024]{1,0:T(8,128)S(1)}, f32[256,1024]{1,0:T(8,128)S(1)}, u32[]{:S(2)}, u32[]{:S(2)}) collective-permute-start(f32[256,1024]{1,0:T(8,128)S(1)} %broadcast_select_fusion.1.refs_0_), channel_id=1, source_target_pairs={{0,1},{1,0},{2,3},{3,2},{4,5},{5,4},{6,7},{7,6},{8,9},{9,8},{10,11... | collective-permute-start | bytes 3145736 | tf_op jit(solution)/shard_map/ppermute | solution.py:30
  176.9 17.4 %collective-permute-start.21 = (f32[256,1024]{1,0:T(8,128)}, f32[256,1024]{1,0:T(8,128)}, u32[]{:S(2)}, u32[]{:S(2)}) collective-permute-start(f32[256,1024]{1,0:T(8,128)} %collective-permute-done.18.refs_2_), channel_id=1, source_target_pairs={{0,1},{1,0},{2,3},{3,2},{4,5},{5,4},{6,7},{7,6},{8,9},{9,8},{10,11... | collective-permute-start | bytes 3145736 | tf_op jit(solution)/shard_map/ppermute | solution.py:30
  177.4 16.8 %copy-start.12 = (f32[256,1024]{1,0:T(8,128)}, f32[256,1024]{1,0:T(8,128)S(1)}, u32[]{:S(2)}) copy-start(f32[256,1024]{1,0:T(8,128)S(1)} %collective-permute-done.25.refs_10_) | copy-start | bytes 3145732
  177.4 16.9 %collective-permute-start.26 = (f32[256,1024]{1,0:T(8,128)}, f32[256,1024]{1,0:T(8,128)}, u32[]{:S(2)}, u32[]{:S(2)}) collective-permute-start(f32[256,1024]{1,0:T(8,128)} %collective-permute-done.19.refs_9_), channel_id=1, source_target_pairs={{0,48},{1,17},{2,50},{3,19},{4,52},{5,21},{6,54},{7,23},{8,56},{9,... | collective-permute-start | bytes 3145736 | tf_op jit(solution)/shard_map/ppermute | solution.py:30
  178.5 15.8 %collective-permute-start.22 = (f32[256,1024]{1,0:T(8,128)}, f32[256,1024]{1,0:T(8,128)}, u32[]{:S(2)}, u32[]{:S(2)}) collective-permute-start(f32[256,1024]{1,0:T(8,128)} %collective-permute-done.20.refs_3_), channel_id=1, source_target_pairs={{0,1},{1,0},{2,3},{3,2},{4,5},{5,4},{6,7},{7,6},{8,9},{9,8},{10,11... | collective-permute-start | bytes 3145736 | tf_op jit(solution)/shard_map/ppermute | solution.py:30
  189.8 6.0 %collective-permute-start.24 = (f32[256,1024]{1,0:T(8,128)}, f32[256,1024]{1,0:T(8,128)}, u32[]{:S(2)}, u32[]{:S(2)}) collective-permute-start(f32[256,1024]{1,0:T(8,128)} %collective-permute-done.23.refs_6_), channel_id=1, source_target_pairs={{0,1},{1,0},{2,3},{3,2},{4,5},{5,4},{6,7},{7,6},{8,9},{9,8},{10,11... | collective-permute-start | bytes 3145736 | tf_op jit(solution)/shard_map/ppermute | solution.py:30
  193.2 1.0 copy-start.1
  194.2 2.9 collective-permute-start.14
  197.1 1.2 copy-start.2
  225.0 122.8 %all-to-all-start.1 = ((f32[128,128,128]{2,1,0:T(8,128)}), f32[128,128,128]{2,1,0:T(8,128)}, u32[]{:S(2)}, u32[]{:S(2)}) async-start(f32[128,128,128]{2,1,0:T(8,128)} %get-tuple-element.42), calls=%async_computation.1 | async-start | bytes 16777216 | tf_op jit(solution)/shard_map/all_to_all | solution.py:419
  237.6 4.1 %copy-start.7 = (f32[2,512,512]{2,1,0:T(8,128)S(1)}, f32[2,512,512]{2,1,0:T(8,128)}, u32[]{:S(2)}) copy-start(f32[2,512,512]{2,1,0:T(8,128)} %inverse_ref.1) | copy-start | bytes 6291460
  347.7 1.9 copy-start
